TPU v7x, 128 devices: a whole 4x4x4 slice. The times are simulated.
128 devices in a mesh: type: 4 (over z), rows: 32 (over y, x, core).
Axes of the slice: x: 4, y: 4, z: 4, core: 2. Of those that a mesh axis runs over, the one named last changes fastest.
Arguments:
- features: bfloat16 [524288, 256], P(('type', 'rows')), may hold values from -6 to 6
- out_grad: bfloat16 [524288, 256], P(('type', 'rows')), may hold values from -6 to 6
- rel_weight: bfloat16 [5, 256, 256], replicated, may hold values from -0.375 to 0.375
- root_weight: bfloat16 [256, 256], replicated, may hold values from -0.375 to 0.375
- tiles: bfloat16 [16384, 128, 128], P(('type', 'rows')), may hold values from 0 to 0.25
- tile_dest: int32 [16384], P(('type', 'rows')), may hold values from 0 to 31
- tile_peer: int32 [16384, 1], P(('type', 'rows')), may hold values from 0 to 127; in each aligned block of 128 rows (0 to 127, 128 to 255, ...) at most 2 rows name the same one
- tile_source: int32 [16384], P(('type', 'rows')), may hold values from 0 to 31
- tile_rel: int32 [16384], P(('type', 'rows')), may hold values from 0 to 4
Outputs:
- grad_feat: bfloat16 [524288, 256], P(('type', 'rows'))
- grad_weights: float32 [6, 256, 256], replicated
Inputs may be any that keep to these rules, and one draw needn't show every extreme that they name: `tile_peer`: among the tiles of one device, no owner is named more than 2 times, a bound that some block reaches.
All inputs are finite; a program needn't handle non-finite values.
Results may differ from a plain program's by a relative error of at most 0.0085.
Values may be sent and summed in bfloat16 or wider, within the bound.
No kernel may reach another device: no remote copies, remote signals or barrier semaphores. Data moves between devices by JAX's collectives and lax.ppermute only.
A program may use at most 128 MiB of HBM per device.

v0:
```python
import math

import jax
import jax.numpy as jnp
from jax import lax
from jax.sharding import PartitionSpec as P


def shards(
    features, out_grad, rel_weight, root_weight, tiles, tile_dest, tile_peer, tile_source, tile_rel
):
    dev_count = lax.axis_size(("type", "rows"))
    tile_count = tiles.shape[0]
    block_rows = tiles.shape[1]
    feat_width = features.shape[1]
    rel_count = rel_weight.shape[0]
    local_blocks = features.shape[0] // block_rows
    capacity = max(2, 3 * tile_count // (2 * dev_count))
    slot_total = dev_count * capacity
    grad_scale = 1.0 / math.sqrt(features.shape[0] * dev_count)
    grad_blocks = out_grad.reshape(local_blocks, block_rows, feat_width)
    dest_rows = grad_blocks[tile_dest]
    messages = jnp.einsum(
        "tij,tic->tjc", tiles, dest_rows, preferred_element_type=jnp.float32
    ).astype(jnp.bfloat16)
    peer_list = tile_peer[:, 0]
    tile_order = jnp.arange(tile_count, dtype=jnp.int32)
    before = (peer_list[:, None] == peer_list[None, :]) & (
        tile_order[None, :] < tile_order[:, None]
    )
    tile_ranks = jnp.sum(before.astype(jnp.int32), axis=1)
    slot_index = peer_list * capacity + tile_ranks
    outgoing = (
        jnp.zeros((slot_total, block_rows, feat_width), jnp.bfloat16).at[slot_index].set(messages)
    )
    labels = jnp.stack([tile_rel, tile_source], axis=1).astype(jnp.bfloat16)
    slot_tags = jnp.full((slot_total, 2), -1.0, jnp.bfloat16).at[slot_index].set(labels)
    root_grad = jnp.einsum("nd,nc->dc", features, out_grad, preferred_element_type=jnp.float32)
    incoming, in_tags = (
        lax.all_to_all(
            outgoing.reshape(dev_count, capacity, block_rows, feat_width),
            ("type", "rows"),
            split_axis=0,
            concat_axis=0,
            tiled=True,
        ),
        lax.all_to_all(
            slot_tags.reshape(dev_count, capacity, 2),
            ("type", "rows"),
            split_axis=0,
            concat_axis=0,
            tiled=True,
        ),
    )
    incoming = incoming.reshape(slot_total, block_rows * feat_width)
    in_tags = in_tags.reshape(slot_total, 2).astype(jnp.int32)
    target = jnp.where(in_tags[:, 0] >= 0, in_tags[:, 0] * local_blocks + in_tags[:, 1], -1)
    onehot = (
        jnp.arange(rel_count * local_blocks, dtype=jnp.int32)[:, None] == target[None, :]
    ).astype(jnp.bfloat16)
    gathered = jnp.dot(onehot, incoming, preferred_element_type=jnp.float32)
    gathered = gathered.reshape(rel_count, local_blocks * block_rows, feat_width)
    upper_part = gathered.astype(jnp.bfloat16)
    lower_part = (gathered - upper_part.astype(jnp.float32)).astype(jnp.bfloat16)
    grad_feat = jnp.einsum("nc,dc->nd", out_grad, root_weight, preferred_element_type=jnp.float32)
    grad_feat = grad_feat + jnp.einsum(
        "rnc,rdc->nd", upper_part, rel_weight, preferred_element_type=jnp.float32
    )
    grad_feat = grad_feat + jnp.einsum(
        "rnc,rdc->nd", lower_part, rel_weight, preferred_element_type=jnp.float32
    )
    rel_grad = jnp.einsum("nd,rnc->rdc", features, upper_part, preferred_element_type=jnp.float32)
    rel_grad = rel_grad + jnp.einsum(
        "nd,rnc->rdc", features, lower_part, preferred_element_type=jnp.float32
    )
    root_total, rel_total = lax.psum((root_grad, rel_grad), ("type", "rows"))
    grad_weights = jnp.concatenate([root_total[None], rel_total], axis=0) * grad_scale
    return (grad_feat.astype(jnp.bfloat16), grad_weights)


def solution(mesh):
    return jax.shard_map(
        shards,
        mesh=mesh,
        in_specs=(
            P(("type", "rows"), None),
            P(("type", "rows"), None),
            P(),
            P(),
            P(("type", "rows"), None, None),
            P(("type", "rows")),
            P(("type", "rows"), None),
            P(("type", "rows")),
            P(("type", "rows")),
        ),
        out_specs=(P(("type", "rows"), None), P()),
        check_vma=False,
    )
```

profile of v0, /device:TPU:1, one launch (start us, length us, event | category | flops | bytes accessed | tf_op | source)
XLA Modules:
  0.0 618.4 jit_solution(11600020434645122468)
XLA Ops:
  7.2 0.0 copy-start
  7.2 1.0 convert_reduce_fusion
  8.2 0.7 fusion.17
  8.8 0.7 convert_bitcast_fusion.1
  9.5 0.1 copy.60
  9.7 0.9 scatter_custom_fusion
  10.6 1.5 copy.61
  12.1 11.5 %all-to-all-start = ((bf16[128,2,2]{1,2,0:T(2,128)(2,1)}), bf16[128,2,2]{1,2,0:T(2,128)(2,1)S(1)}, u32[]{:S(2)}, u32[]{:S(2)}) async-start(bf16[128,2,2]{1,2,0:T(2,128)(2,1)} %copy.61), calls=%async_computation | async-start | bytes 131072 | tf_op jit(solution)/shard_map/all_to_all | solution.py:47
  23.6 0.7 compare_select_fusion.1
  24.2 0.0 copy-done
  24.2 6.6 %gather_fusion = bf16[128,128,256]{2,1,0:T(8,128)(2,1)} fusion(bf16[32,128,256]{2,1,0:T(8,128)(2,1)S(1)} %bitcast.48, s32[1024]{0:T(1024)S(1)} %pad_clamp_fusion), kind=kCustom, calls=%fused_computation | custom fusion | bytes 16777728 | tf_op jit(solution)/shard_map/gather | solution.py:22
  30.8 8.5 %convert_bitcast_fusion = bf16[128,128,256]{1,2,0:T(8,128)(2,1)} fusion(bf16[128,128,256]{2,1,0:T(8,128)(2,1)} %gather_fusion, bf16[128,128,128]{2,1,0:T(8,128)(2,1)} %param.13), kind=kOutput, calls=%fused_computation.4 | convolution fusion | flops 1077936128 | bytes 20971520 | tf_op jit(solution)/shard_map/tij,tic->tjc/dot_general | solution.py:23
  39.3 12.0 %copy.65 = bf16[128,128,256]{2,1,0:T(8,128)(2,1)} copy(bf16[128,128,256]{1,2,0:T(8,128)(2,1)} %convert_bitcast_fusion) | data formatting | bytes 16777216 | tf_op jit(solution)/shard_map/convert_element_type | solution.py:25
  51.3 6.0 broadcast_in_dim.24
  57.2 23.3 %scatter_fusion = bf16[256,128,256]{2,1,0:T(8,128)(2,1)} fusion(bf16[256,128,256]{2,1,0:T(8,128)(2,1)} %broadcast_in_dim.24, s32[128]{0:T(128)S(1)} %fusion.17, bf16[128,128,256]{2,1,0:T(8,128)(2,1)} %copy.65), kind=kCustom, calls=%fused_computation.2 | custom fusion | bytes 25166336 | tf_op jit(solution)/shard_map/scatter | solution.py:34
  80.6 0.0 all-to-all-done
  80.6 10.5 %all-to-all-start.1 = ((bf16[128,2,128,256]{3,2,1,0:T(8,128)(2,1)}), bf16[128,2,128,256]{3,2,1,0:T(8,128)(2,1)}, u32[]{:S(2)}, u32[]{:S(2)}) async-start(bf16[128,2,128,256]{3,2,1,0:T(8,128)(2,1)} %bitcast.49), calls=%async_computation.1 | async-start | bytes 33554432 | tf_op jit(solution)/shard_map/all_to_all | solution.py:40
  91.0 0.2 all-reduce.3.cloned.1.call-start
  91.3 3.1 convolution_bitcast_fusion.2
  94.3 0.1 copy.62
  94.4 0.2 copy.63
  94.6 0.1 reshape.51
  94.7 208.1 %all-to-all-done.1 = bf16[128,2,128,256]{3,2,1,0:T(8,128)(2,1)} async-done(((bf16[128,2,128,256]{3,2,1,0:T(8,128)(2,1)}), bf16[128,2,128,256]{3,2,1,0:T(8,128)(2,1)}, u32[]{:S(2)}, u32[]{:S(2)}) %all-to-all-start.1) | async-done | bytes 16777248 | tf_op jit(solution)/shard_map/all_to_all | solution.py:40
  302.8 17.9 %copy.75 = bf16[32,8,128,256]{3,1,2,0:T(8,128)(2,1)} copy(bf16[32,8,128,256]{3,2,1,0:T(8,128)(2,1)} %bitcast.17) | data formatting | bytes 33554432
  320.7 15.6 %fusion.12 = f32[160,32768]{1,0:T(8,128)} fusion(bf16[256,32768]{1,0:T(8,128)(2,1)} %bitcast.50, s32[256]{0:T(256)S(1)} %bitcast.52), kind=kOutput, calls=%fused_computation.19 | convolution fusion | flops 2684395520 | bytes 37749760 | tf_op jit(solution)/shard_map/dot_general | solution.py:61
  336.4 22.4 %reshape.50 = f32[5,4096,256]{2,1,0:T(8,128)} reshape(f32[160,32768]{1,0:T(8,128)} %fusion.12) | data formatting | bytes 41943040 | tf_op jit(solution)/shard_map/reshape | solution.py:62
  358.7 22.4 %copy.66 = f32[5,4096,256]{1,2,0:T(8,128)} copy(f32[5,4096,256]{2,1,0:T(8,128)} %reshape.50) | data formatting | bytes 41943040 | tf_op jit(solution)/shard_map/reshape | solution.py:62
  381.1 0.0 copy-start.3
  381.1 15.3 %fusion.2 = f32[5,256,256]{2,1,0:T(8,128)S(1)} fusion(bf16[4096,256]{1,0:T(8,128)(2,1)} %param.9, f32[5,4096,256]{1,2,0:T(8,128)} %copy.66), kind=kOutput, calls=%fused_computation.10 | convolution fusion | flops 2705326080 | bytes 24379392 | tf_op jit(solution)/shard_map/nd,rnc->rdc/dot_general | solution.py:73
  396.4 0.0 copy-done.3
  396.4 0.0 copy-start.2
  396.4 17.9 %convolution_bitcast_fusion = f32[4096,256]{1,0:T(8,128)} fusion(bf16[5,256,256]{2,1,0:T(8,128)(2,1)S(1)} %copy-done.3, f32[5,4096,256]{1,2,0:T(8,128)} %copy.66), kind=kOutput, calls=%fused_computation.5 | convolution fusion | flops 2705326080 | bytes 25821184 | tf_op jit(solution)/shard_map/rnc,rdc->nd/dot_general | solution.py:69
  414.3 0.0 copy-done.2
  414.3 11.0 %fusion.9 = f32[5,256,256]{1,2,0:T(8,128)} fusion(f32[5,256,256]{2,1,0:T(8,128)S(1)} %fusion.2, bf16[4096,256]{1,0:T(8,128)(2,1)S(1)} %copy-done.2, f32[5,4096,256]{1,2,0:T(8,128)} %copy.66), kind=kOutput, calls=%fused_computation.16 | convolution fusion | flops 2689925120 | bytes 25690112 | tf_op jit(solution)/shard_map/nd,rnc->rdc/dot_general | solution.py:72
  425.4 0.0 all-reduce.3.cloned.1.call-update
  425.4 0.0 copy-start.1
  425.4 0.0 copy-start.4
  425.4 8.8 %convolution_bitcast_fusion.1 = f32[4096,256]{1,0:T(8,128)S(1)} fusion(bf16[5,256,256]{2,1,0:T(8,128)(2,1)S(1)} %copy-done.3, f32[5,4096,256]{1,2,0:T(8,128)} %copy.66), kind=kOutput, calls=%fused_computation.6 | convolution fusion | flops 2689597440 | bytes 25821184 | tf_op jit(solution)/shard_map/rnc,rdc->nd/dot_general | solution.py:66
  434.2 0.0 copy-done.1
  434.2 0.0 copy-done.4
  434.2 2.2 fusion.1
  436.4 168.3 %all-reduce.3.cloned.1.call-done = (f32[5,256,256]{1,2,0:T(8,128)}, f32[1,256,256]{2,1,0:T(8,128)}) async-done(((f32[5,256,256]{1,2,0:T(8,128)}, f32[1,256,256]{2,1,0:T(8,128)}), (f32[5,256,256]{1,2,0:T(8,128)}, f32[1,256,256]{2,1,0:T(8,128)})) %all-reduce.3.cloned.1.call-update) | async-done | bytes 1572880 | tf_op jit(solution)/shard_map/psum | solution.py:76
  604.8 1.1 copy.70
  605.8 2.7 maximum_multiply_fusion
  608.5 3.0 copy.71
  (4 shorter events, 0.0 us)
Async XLA Ops:
  7.2 17.1 %copy-start = (bf16[4096,256]{1,0:T(8,128)(2,1)S(1)}, bf16[4096,256]{1,0:T(8,128)(2,1)}, u32[]{:S(2)}) copy-start(bf16[4096,256]{1,0:T(8,128)(2,1)} %param.10) | copy-start | bytes 6291460
  12.1 68.5 %all-to-all-start = ((bf16[128,2,2]{1,2,0:T(2,128)(2,1)}), bf16[128,2,2]{1,2,0:T(2,128)(2,1)S(1)}, u32[]{:S(2)}, u32[]{:S(2)}) async-start(bf16[128,2,2]{1,2,0:T(2,128)(2,1)} %copy.61), calls=%async_computation | async-start | bytes 131072 | tf_op jit(solution)/shard_map/all_to_all | solution.py:47
  80.6 222.3 %all-to-all-start.1 = ((bf16[128,2,128,256]{3,2,1,0:T(8,128)(2,1)}), bf16[128,2,128,256]{3,2,1,0:T(8,128)(2,1)}, u32[]{:S(2)}, u32[]{:S(2)}) async-start(bf16[128,2,128,256]{3,2,1,0:T(8,128)(2,1)} %bitcast.49), calls=%async_computation.1 | async-start | bytes 33554432 | tf_op jit(solution)/shard_map/all_to_all | solution.py:40
  91.0 513.7 %all-reduce.3.cloned.1.call-start = ((), (), s32[]{:S(2)}) async-start(), calls=%async_computation.2 | async-start | bytes 3145728 | tf_op jit(solution)/shard_map/psum | solution.py:76
  381.1 15.3 %copy-start.3 = (bf16[5,256,256]{2,1,0:T(8,128)(2,1)S(1)}, bf16[5,256,256]{2,1,0:T(8,128)(2,1)}, u32[]{:S(2)}) copy-start(bf16[5,256,256]{2,1,0:T(8,128)(2,1)} %param.11) | copy-start | bytes 1966084
  396.4 17.9 %copy-start.2 = (bf16[4096,256]{1,0:T(8,128)(2,1)S(1)}, bf16[4096,256]{1,0:T(8,128)(2,1)}, u32[]{:S(2)}) copy-start(bf16[4096,256]{1,0:T(8,128)(2,1)} %param.9) | copy-start | bytes 6291460
  425.4 8.8 %copy-start.1 = (f32[4096,256]{1,0:T(8,128)S(1)}, f32[4096,256]{1,0:T(8,128)}, u32[]{:S(2)}) copy-start(f32[4096,256]{1,0:T(8,128)} %convolution_bitcast_fusion) | copy-start | bytes 12582916
  425.4 8.8 %copy-start.4 = (bf16[256,256]{1,0:T(8,128)(2,1)S(1)}, bf16[256,256]{1,0:T(8,128)(2,1)}, u32[]{:S(2)}) copy-start(bf16[256,256]{1,0:T(8,128)(2,1)} %param.12) | copy-start | bytes 393220
Sparse Core Ops, SparseCore 0:
  425.5 179.2 all-reduce.2
where the time goes:
time: 621 us; the launch traced here: 618 us
  waiting for transfers between devices  376 us (61%)
  local copies, waits for them, and re-layouts  118 us (19%)
  matrix products  82.4 us (13%)
  starting transfers between devices  22.2 us (4%)
  between operations  14.2 us (2%)
    all_to_all x1, waiting for transfers between devices, shards(): lax.all_to_all(outgoing.reshape(dev_count, capacity, block_rows, feat_wid...  208 us
    psum x1, waiting for transfers between devices, shards(): root_total, rel_total = lax.psum((root_grad, rel_grad), ('type', 'rows'))  168 us
    reshape x2, local copies, waits for them, and re-layouts, shards(): gathered.reshape(rel_count, local_blocks * block_rows, feat_width)  44.7 us
    scatter x1, local copies, waits for them, and re-layouts, shards(): jnp.zeros((slot_total, block_rows, feat_width), jnp.bfloat16).at[slot_index]  23.3 us
    unnamed x12, local copies, waits for them, and re-layouts  20.9 us
    dot_general x1, matrix products, shards(): jnp.einsum('rnc,rdc->nd', lower_part, rel_weight, preferred_element_type=...  17.9 us
    dot_general x1, matrix products, shards(): gathered = jnp.dot(onehot, incoming, preferred_element_type=jnp.float32)  15.6 us
    dot_general x1, matrix products, shards(): jnp.einsum('nd,rnc->rdc', features, lower_part, preferred_element_type=jn...  15.3 us
  transfers between devices with their start and end apart: 3, of which 2 were waited for; matrix products, arithmetic and copies ran while one was open for 12% of the time, Pallas kernels for 0%

commit v1 on v0

v1 whole, which is shorter than its diff:
```python
import math

import jax
import jax.numpy as jnp
from jax import lax
from jax.experimental import pallas as pl
from jax.experimental.pallas import tpu as pltpu
from jax.sharding import Mesh
from jax.sharding import PartitionSpec as P

AXES = ("z", "y", "x", "c")
CHIPS = ("z", "y", "x")
VMEM = pl.BlockSpec(memory_space=pltpu.VMEM)
ANY = pl.BlockSpec(memory_space=pl.ANY)
SMEM = pl.BlockSpec(memory_space=pltpu.SMEM)
LIMIT = 40 * 1024 * 1024
GROUP = 4
DEPTH = 4


def message_kernel(cap, parts, dest_ref, peer_ref, tiles_ref, grad_ref, out_ref, held, made, count, in_sems, out_sem):
    tile_count = tiles_ref.shape[0]
    part = tile_count // parts

    def fetch(i):
        rows = pl.ds(i * part, part)
        return pltpu.make_async_copy(tiles_ref.at[rows], held.at[rows], in_sems.at[i])

    for i in range(parts):
        fetch(i).start()

    def clear(i, carry):
        count[i] = 0
        return carry

    lax.fori_loop(0, count.shape[0], clear, 0)

    def one(t):
        peer = peer_ref[t]
        rank = count[peer]
        count[peer] = rank + 1
        made[t] = lax.dot_general(
            held[t], grad_ref[dest_ref[t]], (((0,), (0,)), ((), ())), preferred_element_type=jnp.float32
        ).astype(jnp.bfloat16)
        pltpu.make_async_copy(made.at[t], out_ref.at[peer * cap + rank], out_sem).start()

    for i in range(parts):
        fetch(i).wait()

        def step(j, carry):
            for k in range(4):
                one(i * part + j * 4 + k)
            return carry

        lax.fori_loop(0, part // 4, step, 0)
    pltpu.make_async_copy(made, out_ref.at[pl.ds(0, tile_count)], out_sem).wait()


def make_messages(tile_dest, peer_list, tiles, grad_blocks, slots, cap):
    tile_count, block, _ = tiles.shape
    width = grad_blocks.shape[2]
    parts = 8

    def kernel(*refs):
        message_kernel(cap, parts, *refs)

    return pl.pallas_call(
        kernel,
        out_shape=jax.ShapeDtypeStruct((slots, block, width), jnp.bfloat16),
        in_specs=[SMEM, SMEM, ANY, VMEM],
        out_specs=ANY,
        scratch_shapes=[
            pltpu.VMEM(tiles.shape, jnp.bfloat16),
            pltpu.VMEM((tile_count, block, width), jnp.bfloat16),
            pltpu.SMEM((slots // cap,), jnp.int32),
            pltpu.SemaphoreType.DMA((parts,)),
            pltpu.SemaphoreType.DMA,
        ],
        compiler_params=pltpu.CompilerParams(vmem_limit_bytes=LIMIT),
        cost_estimate=pl.CostEstimate(
            flops=2 * tile_count * block * block * width,
            bytes_accessed=tile_count * block * (block + width) * 2,
            transcendentals=0,
        ),
    )(tile_dest, peer_list, tiles, grad_blocks)


def walk_groups(slots_ref, total, arrived_ref, held, sems, use):
    def fetch(g):
        for k in range(GROUP):
            pltpu.make_async_copy(
                arrived_ref.at[slots_ref[g * GROUP + k]], held.at[lax.rem(g, DEPTH), k], sems.at[lax.rem(g, DEPTH)]
            ).start()

    for g in range(DEPTH - 1):
        @pl.when(g < total)
        def _():
            fetch(g)

    def step(g, carry):
        @pl.when(g + DEPTH - 1 < total)
        def _():
            fetch(g + DEPTH - 1)

        now = lax.rem(g, DEPTH)
        pltpu.make_async_copy(arrived_ref.at[pl.ds(0, GROUP)], held.at[now], sems.at[now]).wait()
        block, width = held.shape[2:]
        use(g, held[now].reshape(GROUP * block, width))
        return carry

    lax.fori_loop(0, total, step, 0)


def weight_kernel(slots_ref, blocks_ref, rels_ref, total_ref, arrived_ref, turned_ref, out_ref, held, sems):
    out_ref[...] = jnp.zeros_like(out_ref)

    def use(g, rows):
        left = jnp.concatenate([turned_ref[blocks_ref[g * GROUP + k]] for k in range(GROUP)], axis=1)
        out_ref[rels_ref[g]] += jnp.dot(left, rows, preferred_element_type=jnp.float32)

    walk_groups(slots_ref, total_ref[0], arrived_ref, held, sems, use)


def feat_kernel(
    slots_ref, blocks_ref, rels_ref, total_ref, arrived_ref, base_ref, weight_ref, out_ref, held, acc, sems, base_sem
):
    blocks, block, _ = out_ref.shape
    base = pltpu.make_async_copy(base_ref, acc.at[pl.ds(0, blocks)], base_sem)
    base.start()
    acc[blocks] = jnp.zeros(acc.shape[1:], jnp.float32)
    base.wait()

    def use(g, rows):
        part = jnp.dot(rows, weight_ref[rels_ref[g]], preferred_element_type=jnp.float32)
        for k in range(GROUP):
            acc[blocks_ref[g * GROUP + k]] += part[k * block : (k + 1) * block]

    walk_groups(slots_ref, total_ref[0], arrived_ref, held, sems, use)

    def finish(b, carry):
        out_ref[b] = acc[b].astype(jnp.bfloat16)
        return carry

    lax.fori_loop(0, blocks, finish, 0)


def plan_groups(table, me, blocks, rel_count):
    senders, tile_count = table.shape
    kinds = rel_count * blocks
    mine = (table // kinds) == me
    key = lax.broadcasted_iota(jnp.int32, table.shape, 1) * kinds + table % kinds
    low = jnp.min(jnp.where(mine, key, tile_count * kinds), axis=1)
    high = jnp.max(jnp.where(mine, key, -1), axis=1)
    tags = jnp.stack(
        [jnp.where(high >= 0, low % kinds, -1), jnp.where(high > low, high % kinds, -1)], axis=1
    ).reshape(-1)
    slot_total = tags.shape[0]
    rel = jnp.where(tags >= 0, tags // blocks, rel_count)
    block_of = tags % blocks
    order = jnp.arange(slot_total, dtype=jnp.int32)
    ranks = jnp.sum(((rel[None, :] == rel[:, None]) & (order[None, :] < order[:, None])).astype(jnp.int32), axis=1)
    kinds_of = jnp.arange(rel_count, dtype=jnp.int32)
    counts = jnp.sum((rel[None, :] == kinds_of[:, None]).astype(jnp.int32), axis=1)
    padded = (counts + GROUP - 1) // GROUP * GROUP
    ends = jnp.sum(jnp.where(kinds_of[None, :] <= kinds_of[:, None], padded[None, :], 0), axis=1)
    starts = ends - padded
    start_of = jnp.sum(jnp.where(rel[:, None] == kinds_of[None, :], starts[None, :], 0), axis=1)
    places = slot_total + GROUP * rel_count
    places = places // GROUP * GROUP
    place = jnp.where(tags >= 0, start_of + ranks, places)
    hit = place[None, :] == jnp.arange(places, dtype=jnp.int32)[:, None]
    slot_at = jnp.sum(jnp.where(hit, order[None, :], 0), axis=1)
    block_at = jnp.sum(jnp.where(hit, block_of[None, :] - blocks, 0), axis=1) + blocks
    filled = jnp.any(hit, axis=1)
    by_group = slot_at.reshape(-1, GROUP)
    slot_at = jnp.where(filled.reshape(-1, GROUP), by_group, by_group[:, :1]).reshape(-1)
    group_start = jnp.arange(places // GROUP, dtype=jnp.int32) * GROUP
    rel_at = jnp.sum((group_start[:, None] >= ends[None, :]).astype(jnp.int32), axis=1)
    rel_at = jnp.minimum(rel_at, rel_count - 1)
    return slot_at, block_at, rel_at, ends[-1:] // GROUP


def all_sum(part):
    kinds, rows, width = part.shape
    chips = lax.axis_size(CHIPS)
    swap = [(0, 1), (1, 0)]
    core = lax.axis_index("c")
    halves = part.reshape(2, kinds * rows // 2, width)
    own = lax.dynamic_index_in_dim(halves, core, 0, keepdims=False)
    other = lax.dynamic_index_in_dim(halves, 1 - core, 0, keepdims=False)
    own = own + lax.ppermute(other, "c", swap)
    shape = (chips, own.size // chips // 128, 128)
    spread = lax.all_to_all(own.reshape(shape), CHIPS, 0, 0, tiled=True).sum(axis=0)
    own = lax.all_to_all(jnp.broadcast_to(spread[None], shape), CHIPS, 0, 0, tiled=True)
    own = own.reshape(kinds * rows // 2, width)
    other = lax.ppermute(own, "c", swap)
    first = jnp.where(core == 0, own, other)
    second = jnp.where(core == 0, other, own)
    return jnp.concatenate([first, second], axis=0).reshape(part.shape)


def shards(features, out_grad, rel_weight, root_weight, tiles, tile_dest, tile_peer, tile_source, tile_rel):
    dev_count = lax.axis_size(AXES)
    me = lax.axis_index(AXES)
    tile_count, block, _ = tiles.shape
    width = features.shape[1]
    rel_count = rel_weight.shape[0]
    blocks = features.shape[0] // block
    cap = 2
    slots = dev_count * cap
    scale = 1.0 / math.sqrt(features.shape[0] * dev_count)
    peer_list = tile_peer[:, 0]
    grad_blocks = out_grad.reshape(blocks, block, width)

    outgoing = make_messages(tile_dest, peer_list, tiles, grad_blocks, slots, cap)
    arrived = lax.all_to_all(
        outgoing.reshape(dev_count, cap, block, width), AXES, split_axis=0, concat_axis=0, tiled=True
    ).reshape(slots, block, width)

    codes = (peer_list * rel_count + tile_rel) * blocks + tile_source
    table = lax.all_gather(codes, AXES, axis=0)
    slot_at, block_at, rel_at, total = plan_groups(table, me, blocks, rel_count)

    turned = jnp.swapaxes(features.reshape(blocks, block, width), 1, 2)
    turned = jnp.concatenate([turned, jnp.zeros((1, width, block), jnp.bfloat16)], axis=0)
    root_grad = jnp.einsum("nd,nc->dc", features, out_grad, preferred_element_type=jnp.float32)
    base = jnp.einsum("nc,dc->nd", out_grad, root_weight, preferred_element_type=jnp.float32)
    turned_weight = jnp.swapaxes(rel_weight, 1, 2)

    ring = [pltpu.VMEM((DEPTH, GROUP, block, width), jnp.bfloat16)]
    sems = [pltpu.SemaphoreType.DMA((DEPTH,))]
    params = pltpu.CompilerParams(vmem_limit_bytes=LIMIT)
    cost = pl.CostEstimate(
        flops=slots * block * width * width, bytes_accessed=slots * block * width * 2, transcendentals=0
    )
    rel_grad = pl.pallas_call(
        weight_kernel,
        out_shape=jax.ShapeDtypeStruct((rel_count, width, width), jnp.float32),
        in_specs=[SMEM] * 4 + [ANY, VMEM],
        out_specs=VMEM,
        scratch_shapes=ring + sems,
        compiler_params=params,
        cost_estimate=cost,
    )(slot_at, block_at, rel_at, total, arrived, turned)
    grad_feat = pl.pallas_call(
        feat_kernel,
        out_shape=jax.ShapeDtypeStruct((blocks, block, width), jnp.bfloat16),
        in_specs=[SMEM] * 4 + [ANY, ANY, VMEM],
        out_specs=VMEM,
        scratch_shapes=ring
        + [pltpu.VMEM((blocks + 1, block, width), jnp.float32)]
        + sems
        + [pltpu.SemaphoreType.DMA],
        compiler_params=params,
        cost_estimate=cost,
    )(slot_at, block_at, rel_at, total, arrived, base.reshape(blocks, block, width), turned_weight)

    grad_weights = all_sum(jnp.concatenate([root_grad[None], rel_grad], axis=0) * scale)
    return grad_feat.reshape(features.shape), grad_weights


def solution(mesh):
    sizes = (4, 4, 4, 2)
    fine = Mesh(mesh.devices.reshape(sizes), AXES)
    return jax.shard_map(
        shards,
        mesh=fine,
        in_specs=(
            P(AXES, None),
            P(AXES, None),
            P(),
            P(),
            P(AXES, None, None),
            P(AXES),
            P(AXES, None),
            P(AXES),
            P(AXES),
        ),
        out_specs=(P(AXES, None), P()),
        check_vma=False,
    )
```

time: 621 us -> 411 us (0.66)
  the two profiles are of different devices: /device:TPU:1 before, /device:TPU:102 now
where the time goes in v1:
time: 411 us; the launch traced here: 404 us
  blocking collectives  301 us (73%)
  Pallas kernels  54.9 us (13%)
  local copies, waits for them, and re-layouts  18.8 us (5%)
  starting transfers between devices  10.4 us (3%)
  other arithmetic  10.3 us (3%)
    all_gather x1, blocking collectives, shards(): table = lax.all_gather(codes, AXES, axis=0)  260 us
    pallas_call x1, Pallas kernels, shards(): pl.pallas_call(feat_kernel, out_shape=jax.ShapeDtypeStruct((blocks, block...  23.3 us
    all_to_all x1, blocking collectives, all_sum(): lax.all_to_all(own.reshape(shape), CHIPS, 0, 0, tiled=True).sum(axis=0)  21.2 us
    pallas_call x1, Pallas kernels, shards(): pl.pallas_call(weight_kernel, out_shape=jax.ShapeDtypeStruct((rel_count,...  21 us
    all_to_all x1, blocking collectives, all_sum(): lax.all_to_all(jnp.broadcast_to(spread[None], shape), CHIPS, 0, 0, tiled=...  19.6 us
    pallas_call x1, Pallas kernels, make_messages(): pl.pallas_call(kernel, out_shape=jax.ShapeDtypeStruct((slots, block, widt...  10.7 us
    all_to_all x1, starting transfers between devices, shards(): lax.all_to_all(outgoing.reshape(dev_count, cap, block, width), AXES, spli...  10.3 us
    unnamed x27, local copies, waits for them, and re-layouts  9.23 us
  transfers between devices with their start and end apart: 3, of which 1 were waited for; matrix products, arithmetic and copies ran while one was open for 4% of the time, Pallas kernels for 6%

profile of v1, /device:TPU:102, one launch (start us, length us, event | category | flops | bytes accessed | tf_op | source)
XLA Modules:
  0.0 404.1 jit_solution(10615797335900887605)
XLA Ops:
  0.6 0.0 copy-start
  0.6 0.0 copy-start.1
  0.7 1.6 copy-done.1
  2.3 2.2 copy-done.4
  4.5 0.7 copy-done.5
  5.1 0.7 copy-done.7
  5.8 10.7 %shard_map.104 = bf16[256,128,256]{2,1,0:T(8,128)(2,1)} custom-call(s32[128]{0:T(128)S(1)} %copy-done.7, s32[128]{0:T(128)S(1)} %bitcast.47, bf16[128,128,128]{2,1,0:T(8,128)(2,1)S(1)} %copy-done.4, bf16[32,128,256]{2,1,0:T(8,128)(2,1)S(1)} %bitcast.45), custom_call_target="tpu_custom_call" | custom-call | flops 1073741824 | bytes 12582912 | tf_op jit(solution)/shard_map/pallas_call | solution.py:67
  16.5 0.0 copy-start.11
  16.5 10.3 %all-to-all-start = ((bf16[128,2,128,256]{3,2,1,0:T(8,128)(2,1)}), bf16[128,2,128,256]{3,2,1,0:T(8,128)(2,1)}, u32[]{:S(2)}, u32[]{:S(2)}) async-start(bf16[128,2,128,256]{3,2,1,0:T(8,128)(2,1)} %bitcast.48), calls=%async_computation | async-start | bytes 33554432 | tf_op jit(solution)/shard_map/all_to_all | solution.py:216
  26.8 259.8 %all-gather.1 = s32[128,1,128]{2,1,0:T(1,128)S(1)} all-gather(s32[1,1,128]{2,1,0:T(1,128)S(1)} %add_bitcast_fusion), channel_id=2, replica_groups=mesh['z'=4,'y'=4,'x'=4,'c'=2] {'z','y','x','c'}, dimensions={0}, use_global_device_ids=true | all-gather | bytes 66048 | tf_op jit(solution)/shard_map/all_gather | solution.py:221
  286.7 4.9 %rem.132 = s32[128,1,128]{2,1,0:T(1,128)S(1)} remainder(s32[128,1,128]{2,1,0:T(1,128)S(1)} %all-gather.1, s32[128,1,128]{2,1,0:T(1,128)S(1)} %bitcast.57) | non-fusion elementwise | flops 16384 | bytes 196608 | tf_op jit(solution)/shard_map/jit(floor_divide)/rem | solution.py:150
  291.6 0.2 select_reduce_fusion.2
  291.8 0.1 copy.36
  291.9 0.1 reshape.247
  292.1 0.1 convert_reduce_fusion.1
  292.2 0.1 select_reduce_fusion.5
  292.3 0.6 slice.7
  295.5 0.1 select_reduce_fusion.4
  295.6 0.2 convert_reduce_fusion
  295.8 0.2 select_reduce_fusion
  296.0 0.1 reshape.248
  296.1 0.1 slice_reduce_fusion
  296.2 0.1 broadcast_in_dim.107
  296.3 0.1 broadcast_in_dim.108
  296.4 2.9 copy.38
  299.3 0.1 fusion
  299.5 3.4 concatenate.9.turned_ref
  302.8 0.1 convert_reduce_fusion.2
  302.9 2.3 convolution_bitcast_fusion
  305.3 1.6 copy-done.3
  306.9 21.0 %shard_map.106 = f32[5,256,256]{2,1,0:T(8,128)S(1)} custom-call(s32[276]{0:T(512)S(1)} %select_n.177.slots_ref, s32[276]{0:T(512)S(1)} %broadcast_add_fusion.blocks_ref, s32[69]{0:T(128)S(1)} %broadcast_minimum_fusion.rels_ref, s32[1]{0:T(128)S(6)} %select_n.180.total_ref, bf16[256,128,256]{2,1,0:T(8,128)(2,1)} %bitcast.14.arrived_ref, ...), custom_call_target="tpu_custom_call" | custom-call | flops 2147483648 | bytes 16777216 | tf_op jit(solution)/shard_map/pallas_call | solution.py:236
  327.9 0.2 maximum_multiply_fusion
  328.0 1.1 copy-done.8
  329.2 0.1 dynamic-slice_bitcast_fusion
  329.2 0.1 collective-permute-start
  329.3 2.4 collective-permute-done
  331.7 1.5 bitcast_add_fusion
  333.2 0.9 reshape.255
  334.1 21.2 %all_to_all.15 = f32[64,24,128]{2,1,0:T(8,128)S(1)} all-to-all(f32[64,24,128]{2,1,0:T(8,128)} %reshape.255), channel_id=1, replica_groups=mesh['z'=4,'y'=4,'x'=4,'c'=2] {'z','y','x'}, dimensions={0} | all-to-all | bytes 1572864 | tf_op jit(solution)/shard_map/all_to_all | solution.py:193
  355.3 0.1 reduce_sum.79
  355.4 0.1 broadcast_in_dim.111
  355.5 19.6 %all_to_all.16 = f32[64,24,128]{2,1,0:T(8,128)S(1)} all-to-all(f32[64,24,128]{2,1,0:T(8,128)S(1)} %broadcast_in_dim.111), channel_id=1, replica_groups=mesh['z'=4,'y'=4,'x'=4,'c'=2] {'z','y','x'}, dimensions={0} | all-to-all | bytes 1572864 | tf_op jit(solution)/shard_map/all_to_all | solution.py:194
  375.1 1.1 reshape.256
  376.2 1.3 copy.37
  377.5 0.7 fusion.9
  378.2 23.3 %shard_map.105 = bf16[32,128,256]{2,1,0:T(8,128)(2,1)} custom-call(s32[276]{0:T(512)S(1)} %select_n.177.slots_ref, s32[276]{0:T(512)S(1)} %broadcast_add_fusion.blocks_ref, s32[69]{0:T(128)S(1)} %broadcast_minimum_fusion.rels_ref, s32[1]{0:T(128)S(6)} %select_n.180.total_ref, bf16[256,128,256]{2,1,0:T(8,128)(2,1)} %bitcast.14.arrived_ref, ...), custom_call_target="tpu_custom_call" | custom-call | flops 2147483648 | bytes 16777216 | tf_op jit(solution)/shard_map/pallas_call | solution.py:245
  401.6 1.2 broadcast_select_fusion.1
  402.8 1.2 pad_maximum_fusion
  (33 shorter events, 0.2 us)
Async XLA Ops:
  0.6 376.9 %copy-start = (bf16[256,256]{1,0:T(8,128)(2,1)S(1)}, bf16[256,256]{1,0:T(8,128)(2,1)}, u32[]{:S(2)}) copy-start(bf16[256,256]{1,0:T(8,128)(2,1)} %param.12) | copy-start | bytes 393220
  0.6 1.6 copy-start.1
  2.3 2.2 copy-start.4
  4.5 0.7 copy-start.5
  5.1 0.7 copy-start.7
  16.4 10.4 %copy-start.6 = (s32[128,1]{0,1:T(1,128)S(1)}, s32[128,1]{0,1:T(1,128)}, u32[]{:S(2)}) copy-start(s32[128,1]{0,1:T(1,128)} %param.15) | copy-start | bytes 1540
  16.5 10.4 %copy-start.11 = (s32[128]{0:T(128)S(1)}, s32[128]{0:T(128)}, u32[]{:S(2)}) copy-start(s32[128]{0:T(128)} %param.16) | copy-start | bytes 1540
  16.5 10.4 %copy-start.12 = (s32[128]{0:T(128)S(1)}, s32[128]{0:T(128)}, u32[]{:S(2)}) copy-start(s32[128]{0:T(128)} %param.17) | copy-start | bytes 1540
  16.5 279.9 %copy-start.10 = (bf16[4096,256]{1,0:T(8,128)(2,1)S(1)}, bf16[4096,256]{1,0:T(8,128)(2,1)}, u32[]{:S(2)}) copy-start(bf16[4096,256]{1,0:T(8,128)(2,1)} %param.9) | copy-start | bytes 6291460
  16.5 288.8 %all-to-all-start = ((bf16[128,2,128,256]{3,2,1,0:T(8,128)(2,1)}), bf16[128,2,128,256]{3,2,1,0:T(8,128)(2,1)}, u32[]{:S(2)}, u32[]{:S(2)}) async-start(bf16[128,2,128,256]{3,2,1,0:T(8,128)(2,1)} %bitcast.48), calls=%async_computation | async-start | bytes 33554432 | tf_op jit(solution)/shard_map/all_to_all | solution.py:216
  299.4 3.5 copy-start.2
  305.3 1.6 copy-start.3
  328.0 1.1 copy-start.8
  329.2 2.5 collective-permute-start
  376.2 25.4 %collective-permute-start.1 = (f32[768,256]{1,0:T(8,128)}, f32[768,256]{1,0:T(8,128)}, u32[]{:S(2)}, u32[]{:S(2)}) collective-permute-start(f32[768,256]{1,0:T(8,128)} %reshape.256), channel_id=1, source_target_pairs={{0,1},{1,0},{2,3},{3,2},{4,5},{5,4},{6,7},{7,6},{8,9},{9,8},{10,11... | collective-permute-start | bytes 2359304 | tf_op jit(solution)/shard_map/ppermute | solution.py:196
  378.2 23.4 %copy-start.9 = (f32[768,256]{1,0:T(8,128)S(1)}, f32[768,256]{1,0:T(8,128)}, u32[]{:S(2)}) copy-start(f32[768,256]{1,0:T(8,128)} %reshape.256) | copy-start | bytes 2359300

commit v2 on v1

v2 whole, which is shorter than its diff:
```python
import math

import jax
import jax.numpy as jnp
from jax import lax
from jax.experimental import pallas as pl
from jax.experimental.pallas import tpu as pltpu
from jax.sharding import Mesh
from jax.sharding import PartitionSpec as P

AXES = ("z", "y", "x", "c")
CHIPS = ("z", "y", "x")
VMEM = pl.BlockSpec(memory_space=pltpu.VMEM)
ANY = pl.BlockSpec(memory_space=pl.ANY)
SMEM = pl.BlockSpec(memory_space=pltpu.SMEM)
GROUP = 8
DEPTH = 4
MIB = 1024 * 1024


def message_kernel(
    cap, parts, dest_any, peer_any, tiles_ref, grad_any, out_ref, dest, peers, count, grad, held, made, sems, out_sem
):
    tile_count = tiles_ref.shape[0]
    part = tile_count // parts
    early = [
        pltpu.make_async_copy(src, dst, sems.at[parts + i])
        for i, (src, dst) in enumerate(((dest_any, dest), (peer_any, peers), (grad_any, grad)))
    ]
    for copy in early:
        copy.start()

    def fetch(i):
        rows = pl.ds(i * part, part)
        return pltpu.make_async_copy(tiles_ref.at[rows], held.at[rows], sems.at[i])

    for i in range(parts):
        fetch(i).start()

    def clear(i, carry):
        count[i] = 0
        return carry

    lax.fori_loop(0, count.shape[0], clear, 0)
    for copy in early:
        copy.wait()

    for i in range(parts):
        fetch(i).wait()

        def step(j, carry):
            for k in range(16):
                t = i * part + j * 16 + k
                peer = peers[t]
                rank = count[peer]
                count[peer] = rank + 1
                made[t] = lax.dot_general(
                    held[t], grad[dest[t]], (((0,), (0,)), ((), ())), preferred_element_type=jnp.float32
                ).astype(jnp.bfloat16)
                pltpu.make_async_copy(made.at[t], out_ref.at[peer * cap + rank], out_sem).start()
            return carry

        lax.fori_loop(0, part // 16, step, 0)
    pltpu.make_async_copy(made, out_ref.at[pl.ds(0, tile_count)], out_sem).wait()


def make_messages(tile_dest, peer_list, tiles, grad_blocks, slots, cap):
    tile_count, block, _ = tiles.shape
    width = grad_blocks.shape[2]
    parts = 8

    def kernel(*refs):
        message_kernel(cap, parts, *refs)

    return pl.pallas_call(
        kernel,
        out_shape=jax.ShapeDtypeStruct((slots, block, width), jnp.bfloat16),
        in_specs=[ANY] * 4,
        out_specs=ANY,
        scratch_shapes=[
            pltpu.SMEM((tile_count,), jnp.int32),
            pltpu.SMEM((tile_count,), jnp.int32),
            pltpu.SMEM((slots // cap,), jnp.int32),
            pltpu.VMEM(grad_blocks.shape, jnp.bfloat16),
            pltpu.VMEM(tiles.shape, jnp.bfloat16),
            pltpu.VMEM((tile_count, block, width), jnp.bfloat16),
            pltpu.SemaphoreType.DMA((parts + 3,)),
            pltpu.SemaphoreType.DMA,
        ],
        compiler_params=pltpu.CompilerParams(vmem_limit_bytes=58 * MIB),
        cost_estimate=pl.CostEstimate(
            flops=2 * tile_count * block * block * width,
            bytes_accessed=tile_count * block * (block + width) * 2,
            transcendentals=0,
        ),
    )(tile_dest, peer_list, tiles, grad_blocks)


def walk_groups(slots_ref, total, arrived_ref, held, sems, use):
    block, width = held.shape[2:]

    def fetch(g):
        now = lax.rem(g, DEPTH)
        for k in range(GROUP):
            pltpu.make_async_copy(arrived_ref.at[slots_ref[g * GROUP + k]], held.at[now, k], sems.at[now]).start()

    def settle(g):
        now = lax.rem(g, DEPTH)
        pltpu.make_async_copy(arrived_ref.at[pl.ds(0, GROUP)], held.at[now], sems.at[now]).wait()

    for g in range(DEPTH - 1):
        fetch(g)

    def step(g, carry):
        settle(g)
        fetch(g + DEPTH - 1)
        use(g, held[lax.rem(g, DEPTH)].reshape(GROUP * block, width))
        return carry

    lax.fori_loop(0, total, step, 0)
    for g in range(DEPTH - 1):
        settle(total + g)


def weight_kernel(slots_ref, blocks_ref, rels_ref, total_ref, arrived_ref, turned_ref, root_ref, own_ref, other_ref, held, acc, sems):
    rel_count, width, _ = acc.shape
    half = width // 2
    acc[...] = jnp.zeros_like(acc)

    def use(g, rows):
        left = jnp.concatenate([turned_ref[blocks_ref[g * GROUP + k]] for k in range(GROUP)], axis=1)
        acc[rels_ref[g]] += jnp.dot(left, rows, preferred_element_type=jnp.float32)

    walk_groups(slots_ref, total_ref[0], arrived_ref, held, sems, use)

    def split(first, second):
        for ref, lanes in ((first, pl.ds(0, half)), (second, pl.ds(half, half))):
            ref[pl.ds(0, width)] = root_ref[:, lanes]
            for r in range(rel_count):
                ref[pl.ds((1 + r) * width, width)] = acc[r, :, lanes]

    @pl.when(total_ref[1] == 0)
    def _():
        split(own_ref, other_ref)

    @pl.when(total_ref[1] != 0)
    def _():
        split(other_ref, own_ref)


def feat_kernel(slots_ref, blocks_ref, rels_ref, total_ref, arrived_ref, base_ref, weight_ref, out_ref, held, acc, sems):
    blocks, block, _ = out_ref.shape
    acc[pl.ds(0, blocks)] = base_ref[...]
    acc[blocks] = jnp.zeros(acc.shape[1:], jnp.float32)

    def use(g, rows):
        part = jnp.dot(rows, weight_ref[rels_ref[g]], preferred_element_type=jnp.float32)
        for k in range(GROUP):
            acc[blocks_ref[g * GROUP + k]] += part[k * block : (k + 1) * block]

    walk_groups(slots_ref, total_ref[0], arrived_ref, held, sems, use)
    out_ref[...] = acc[pl.ds(0, blocks)].astype(jnp.bfloat16)


def plan_groups(table, me, blocks, rel_count):
    senders, tile_count = table.shape
    kinds = rel_count * blocks
    mine = (table // kinds) == me
    key = lax.broadcasted_iota(jnp.int32, table.shape, 1) * kinds + table % kinds
    low = jnp.min(jnp.where(mine, key, tile_count * kinds), axis=1)
    high = jnp.max(jnp.where(mine, key, -1), axis=1)
    tags = jnp.stack(
        [jnp.where(high >= 0, low % kinds, -1), jnp.where(high > low, high % kinds, -1)], axis=1
    ).reshape(-1)
    slot_total = tags.shape[0]
    rel = jnp.where(tags >= 0, tags // blocks, rel_count)
    block_of = tags % blocks
    order = jnp.arange(slot_total, dtype=jnp.int32)
    ranks = jnp.sum(((rel[None, :] == rel[:, None]) & (order[None, :] < order[:, None])).astype(jnp.int32), axis=1)
    kinds_of = jnp.arange(rel_count, dtype=jnp.int32)
    counts = jnp.sum((rel[None, :] == kinds_of[:, None]).astype(jnp.int32), axis=1)
    padded = (counts + GROUP - 1) // GROUP * GROUP
    ends = jnp.sum(jnp.where(kinds_of[None, :] <= kinds_of[:, None], padded[None, :], 0), axis=1)
    starts = ends - padded
    start_of = jnp.sum(jnp.where(rel[:, None] == kinds_of[None, :], starts[None, :], 0), axis=1)
    places = (-(-slot_total // GROUP) + rel_count + DEPTH - 1) * GROUP
    place = jnp.where(tags >= 0, start_of + ranks, places)
    hit = place[None, :] == jnp.arange(places, dtype=jnp.int32)[:, None]
    slot_at = jnp.sum(jnp.where(hit, order[None, :], 0), axis=1)
    block_at = jnp.sum(jnp.where(hit, block_of[None, :] - blocks, 0), axis=1) + blocks
    filled = jnp.any(hit, axis=1)
    by_group = slot_at.reshape(-1, GROUP)
    slot_at = jnp.where(filled.reshape(-1, GROUP), by_group, by_group[:, :1]).reshape(-1)
    group_start = jnp.arange(places // GROUP, dtype=jnp.int32) * GROUP
    rel_at = jnp.sum((group_start[:, None] >= ends[None, :]).astype(jnp.int32), axis=1)
    rel_at = jnp.minimum(rel_at, rel_count - 1)
    return slot_at, block_at, rel_at, ends[-1:] // GROUP


def shards(features, out_grad, rel_weight, root_weight, tiles, tile_dest, tile_peer, tile_source, tile_rel):
    dev_count = lax.axis_size(AXES)
    chips = lax.axis_size(CHIPS)
    me = lax.axis_index(AXES)
    core = lax.axis_index("c")
    tile_count, block, _ = tiles.shape
    width = features.shape[1]
    rel_count = rel_weight.shape[0]
    blocks = features.shape[0] // block
    cap = 2
    slots = dev_count * cap
    scale = 1.0 / math.sqrt(features.shape[0] * dev_count)
    peer_list = tile_peer[:, 0]
    grad_blocks = out_grad.reshape(blocks, block, width)

    codes = ((peer_list * rel_count + tile_rel) * blocks + tile_source).astype(jnp.float32)
    rows = lax.broadcasted_iota(jnp.int32, (dev_count, tile_count), 0)
    table = lax.psum(jnp.where(rows == me, codes[None, :], 0.0), AXES).astype(jnp.int32)
    slot_at, block_at, rel_at, total = plan_groups(table, me, blocks, rel_count)
    total = jnp.concatenate([total, core[None].astype(jnp.int32)])

    outgoing = make_messages(tile_dest, peer_list, tiles, grad_blocks, slots, cap)
    arrived = lax.all_to_all(
        outgoing.reshape(dev_count, cap, block, width), AXES, split_axis=0, concat_axis=0, tiled=True
    ).reshape(slots, block, width)

    turned = jnp.swapaxes(features.reshape(blocks, block, width), 1, 2)
    turned = jnp.concatenate([turned, jnp.zeros((1, width, block), jnp.bfloat16)], axis=0)
    root_grad = jnp.einsum("nd,nc->dc", features, out_grad, preferred_element_type=jnp.float32)
    base = jnp.einsum("nc,dc->nd", out_grad, root_weight, preferred_element_type=jnp.float32)
    turned_weight = jnp.swapaxes(rel_weight, 1, 2)

    slot_at, block_at, rel_at, total, turned, root_grad, base, turned_weight = lax.optimization_barrier(
        (slot_at, block_at, rel_at, total, turned, root_grad, base, turned_weight)
    )
    ring = [pltpu.VMEM((DEPTH, GROUP, block, width), jnp.bfloat16)]
    sems = [pltpu.SemaphoreType.DMA((DEPTH,))]
    cost = pl.CostEstimate(
        flops=slots * block * width * width, bytes_accessed=slots * block * width * 2, transcendentals=0
    )
    half_rows = (1 + rel_count) * width
    half = jax.ShapeDtypeStruct((half_rows, width // 2), jnp.float32)
    own, other = pl.pallas_call(
        weight_kernel,
        out_shape=(half, half),
        in_specs=[SMEM] * 4 + [ANY, VMEM, VMEM],
        out_specs=(VMEM, VMEM),
        scratch_shapes=ring + [pltpu.VMEM((rel_count, width, width), jnp.float32)] + sems,
        compiler_params=pltpu.CompilerParams(vmem_limit_bytes=20 * MIB),
        cost_estimate=cost,
    )(slot_at, block_at, rel_at, total, arrived, turned, root_grad)
    swap = [(0, 1), (1, 0)]
    own = own + lax.ppermute(other, "c", swap)
    own, total = lax.optimization_barrier((own, total))
    grad_feat = pl.pallas_call(
        feat_kernel,
        out_shape=jax.ShapeDtypeStruct((blocks, block, width), jnp.bfloat16),
        in_specs=[SMEM] * 4 + [ANY, VMEM, VMEM],
        out_specs=VMEM,
        scratch_shapes=ring + [pltpu.VMEM((blocks + 1, block, width), jnp.float32)] + sems,
        compiler_params=pltpu.CompilerParams(vmem_limit_bytes=28 * MIB),
        cost_estimate=cost,
    )(slot_at, block_at, rel_at, total, arrived, base.reshape(blocks, block, width), turned_weight)

    shape = (chips, half_rows // chips, width // 2)
    spread = lax.all_to_all(own.reshape(shape), CHIPS, 0, 0, tiled=True)
    spread, grad_feat = lax.optimization_barrier((spread, grad_feat))
    share = (spread.sum(axis=0) * scale).astype(jnp.bfloat16)
    own = lax.all_to_all(jnp.broadcast_to(share[None], shape), CHIPS, 0, 0, tiled=True).reshape(half.shape)
    other = lax.ppermute(own, "c", swap)
    left = jnp.where(core == 0, own, other).astype(jnp.float32)
    right = jnp.where(core == 0, other, own).astype(jnp.float32)
    grad_weights = jnp.concatenate([left, right], axis=1).reshape(1 + rel_count, width, width)
    return grad_feat.reshape(features.shape), grad_weights


def solution(mesh):
    sizes = (4, 4, 4, 2)
    fine = Mesh(mesh.devices.reshape(sizes), AXES)
    return jax.shard_map(
        shards,
        mesh=fine,
        in_specs=(
            P(AXES, None),
            P(AXES, None),
            P(),
            P(),
            P(AXES, None, None),
            P(AXES),
            P(AXES, None),
            P(AXES),
            P(AXES),
        ),
        out_specs=(P(AXES, None), P()),
        check_vma=False,
    )
```

time: 411 us -> 414 us (level)
  the two profiles are of different devices: /device:TPU:102 before, /device:TPU:1 now
where the time goes in v2:
time: 414 us; the launch traced here: 412 us
  waiting for transfers between devices  299 us (72%)
  starting transfers between devices  27.7 us (7%)
  Pallas kernels  25.1 us (6%)
  blocking collectives  22.8 us (6%)
  between operations  16.9 us (4%)
  local copies, waits for them, and re-layouts  10.7 us (3%)
  other arithmetic  5.33 us (1%)
  matrix products  5.12 us (1%)
    psum x1, waiting for transfers between devices, shards(): lax.psum(jnp.where(rows == me, codes[None, :], 0.0), AXES).astype(jnp.int32)  292 us
    all_to_all x1, blocking collectives, shards(): lax.all_to_all(jnp.broadcast_to(share[None], shape), CHIPS, 0, 0, tiled=T...  22.8 us
    all_to_all x1, starting transfers between devices, shards(): spread = lax.all_to_all(own.reshape(shape), CHIPS, 0, 0, tiled=True)  12.4 us
    all_to_all x1, starting transfers between devices, shards(): lax.all_to_all(outgoing.reshape(dev_count, cap, block, width), AXES, spli...  12 us
    pallas_call x1, Pallas kernels, shards(): pl.pallas_call(feat_kernel, out_shape=jax.ShapeDtypeStruct((blocks, block...  10.1 us
    pallas_call x1, Pallas kernels, shards(): pl.pallas_call(weight_kernel, out_shape=(half, half), in_specs=[SMEM] * 4...  8.59 us
  transfers between devices with their start and end apart: 5, of which 4 were waited for; matrix products, arithmetic and copies ran while one was open for 4% of the time, Pallas kernels for 2%

profile of v2, /device:TPU:1, one launch (start us, length us, event | category | flops | bytes accessed | tf_op | source)
XLA Modules:
  0.0 412.1 jit_solution(13499697604157336673)
XLA Ops:
  7.2 0.0 copy-start
  7.2 6.4 %shard_map.104 = bf16[256,128,256]{2,1,0:T(8,128)(2,1)} custom-call(s32[128]{0:T(128)} %refs_0_.1, s32[128]{0:T(128)} %bitcast.38, bf16[128,128,128]{2,1,0:T(8,128)(2,1)} %refs_2_.1, bf16[32,128,256]{2,1,0:T(8,128)(2,1)} %bitcast.32), custom_call_target="tpu_custom_call" | custom-call | flops 1073741824 | bytes 12582912 | tf_op jit(solution)/shard_map/pallas_call | solution.py:75
  13.6 0.0 copy-start.3
  13.6 0.0 copy-start.4
  13.6 0.0 copy-start.5
  13.6 0.0 copy-start.2
  13.6 12.0 %all-to-all-start = ((bf16[128,2,128,256]{3,2,1,0:T(8,128)(2,1)}), bf16[128,2,128,256]{3,2,1,0:T(8,128)(2,1)}, u32[]{:S(2)}, u32[]{:S(2)}) async-start(bf16[128,2,128,256]{3,2,1,0:T(8,128)(2,1)} %bitcast.31), calls=%async_computation | async-start | bytes 33554432 | tf_op jit(solution)/shard_map/all_to_all | solution.py:222
  25.6 0.0 all-reduce.3.cloned.1.call-start
  25.7 0.7 broadcast_select_fusion.2
  26.4 0.0 all-reduce.3.cloned.1.call-update
  26.5 2.3 fusion.9.root_ref
  28.8 2.8 fusion.10
  31.6 1.3 copy.20
  33.0 4.1 copy.19
  37.0 1.8 concatenate.11.turned_ref
  38.9 291.7 %all-reduce.3.cloned.1.call-done = f32[128,128]{1,0:T(8,128)} async-done(((f32[128,128]{1,0:T(8,128)}), f32[128,128]{1,0:T(8,128)}) %all-reduce.3.cloned.1.call-update) | async-done | bytes 65552 | tf_op jit(solution)/shard_map/psum | solution.py:217
  330.6 1.0 select_reduce_fusion.2
  331.6 0.1 copy.18
  331.7 0.1 reshape.250
  331.9 0.1 convert_reduce_fusion.1
  332.0 0.1 select_reduce_fusion.5
  332.1 0.6 slice.7
  335.3 0.1 select_reduce_fusion.4
  335.4 0.2 convert_reduce_fusion
  335.6 0.2 select_reduce_fusion
  335.8 0.1 reshape.251
  335.9 0.1 slice_reduce_fusion
  336.0 0.1 broadcast_in_dim.122
  336.1 0.1 broadcast_in_dim.123
  336.2 0.1 fusion
  336.4 0.1 pad_add_fusion.1.total_ref
  336.4 0.1 convert_reduce_fusion.2
  336.6 8.6 %shard_map.105 = (f32[1536,128]{1,0:T(8,128)S(1)}, f32[1536,128]{1,0:T(8,128)S(1)}) custom-call(s32[320]{0:T(512)S(1)} %select_n.175.slots_ref, s32[320]{0:T(512)S(1)} %broadcast_add_fusion.blocks_ref, s32[40]{0:T(128)S(1)} %broadcast_minimum_fusion.rels_ref, s32[2]{0:T(128)S(1)} %pad_add_fusion.1.total_ref, bf16[256,128,256]{2,1,0:T(8,128)(2,1)} %bitcast.11.arrived_ref, ...), custom_call_target="tpu_custom_call" | custom-call | flops 2147483648 | bytes 16777216 | tf_op jit(solution)/shard_map/pallas_call | solution.py:242
  345.1 0.1 collective-permute-start
  345.2 2.3 collective-permute-done
  347.5 1.0 add.129
  348.5 12.4 %all-to-all-start.1 = ((f32[64,24,128]{2,1,0:T(8,128)}), f32[64,24,128]{2,1,0:T(8,128)S(1)}, u32[]{:S(2)}, u32[]{:S(2)}) async-start(f32[64,24,128]{2,1,0:T(8,128)} %bitcast.12), calls=%async_computation.1 | async-start | bytes 1572864 | tf_op jit(solution)/shard_map/all_to_all | solution.py:265
  360.9 2.2 copy-done.1
  363.1 10.1 %shard_map.106 = bf16[32,128,256]{2,1,0:T(8,128)(2,1)} custom-call(s32[320]{0:T(512)S(1)} %select_n.175.slots_ref, s32[320]{0:T(512)S(1)} %broadcast_add_fusion.blocks_ref, s32[40]{0:T(128)S(1)} %broadcast_minimum_fusion.rels_ref, s32[2]{0:T(128)S(1)} %pad_add_fusion.1.total_ref, bf16[256,128,256]{2,1,0:T(8,128)(2,1)} %bitcast.11.arrived_ref, ...), custom_call_target="tpu_custom_call" | custom-call | flops 2147483648 | bytes 16777216 | tf_op jit(solution)/shard_map/pallas_call | solution.py:254
  373.2 3.2 all-to-all-done.1
  376.3 0.1 reduce_sum.79
  376.4 0.1 broadcast_in_dim.126
  376.5 22.8 %all_to_all.15 = bf16[64,24,128]{2,1,0:T(8,128)(2,1)S(1)} all-to-all(bf16[64,24,128]{2,1,0:T(8,128)(2,1)S(1)} %broadcast_in_dim.126), channel_id=1, replica_groups=mesh['z'=4,'y'=4,'x'=4,'c'=2] {'z','y','x'}, dimensions={0} | all-to-all | bytes 786432 | tf_op jit(solution)/shard_map/all_to_all | solution.py:268
  399.3 3.2 collective-permute-start.1
  402.5 1.3 collective-permute-done.1
  403.8 0.1 broadcast_select_fusion.1
  403.9 0.1 pad_maximum_fusion
  404.0 1.3 convert.2
  (21 shorter events, 0.1 us)
Async XLA Ops:
  7.2 21.7 %copy-start = (bf16[256,256]{1,0:T(8,128)(2,1)S(1)}, bf16[256,256]{1,0:T(8,128)(2,1)}, u32[]{:S(2)}) copy-start(bf16[256,256]{1,0:T(8,128)(2,1)} %param.12) | copy-start | bytes 393220
  13.6 12.1 %copy-start.3 = (s32[128,1]{0,1:T(1,128)S(1)}, s32[128,1]{0,1:T(1,128)}, u32[]{:S(2)}) copy-start(s32[128,1]{0,1:T(1,128)} %param.15) | copy-start | bytes 1540
  13.6 12.1 %copy-start.4 = (s32[128]{0:T(128)S(1)}, s32[128]{0:T(128)}, u32[]{:S(2)}) copy-start(s32[128]{0:T(128)} %param.16) | copy-start | bytes 1540
  13.6 12.1 %copy-start.5 = (s32[128]{0:T(128)S(1)}, s32[128]{0:T(128)}, u32[]{:S(2)}) copy-start(s32[128]{0:T(128)} %param.17) | copy-start | bytes 1540
  13.6 12.9 %copy-start.2 = (bf16[4096,256]{1,0:T(8,128)(2,1)S(1)}, bf16[4096,256]{1,0:T(8,128)(2,1)}, u32[]{:S(2)}) copy-start(bf16[4096,256]{1,0:T(8,128)(2,1)} %param.10) | copy-start | bytes 6291460
  13.6 322.9 %all-to-all-start = ((bf16[128,2,128,256]{3,2,1,0:T(8,128)(2,1)}), bf16[128,2,128,256]{3,2,1,0:T(8,128)(2,1)}, u32[]{:S(2)}, u32[]{:S(2)}) async-start(bf16[128,2,128,256]{3,2,1,0:T(8,128)(2,1)} %bitcast.31), calls=%async_computation | async-start | bytes 33554432 | tf_op jit(solution)/shard_map/all_to_all | solution.py:222
  25.6 305.0 %all-reduce.3.cloned.1.call-start = ((), (), s32[]{:S(2)}) async-start(), calls=%async_computation.3 | async-start | bytes 131072 | tf_op jit(solution)/shard_map/psum | solution.py:217
  345.1 2.4 collective-permute-start
  348.5 27.9 %all-to-all-start.1 = ((f32[64,24,128]{2,1,0:T(8,128)}), f32[64,24,128]{2,1,0:T(8,128)S(1)}, u32[]{:S(2)}, u32[]{:S(2)}) async-start(f32[64,24,128]{2,1,0:T(8,128)} %bitcast.12), calls=%async_computation.1 | async-start | bytes 1572864 | tf_op jit(solution)/shard_map/all_to_all | solution.py:265
  360.9 2.2 copy-start.1
  399.3 4.6 %collective-permute-start.1 = (bf16[1536,128]{1,0:T(8,128)(2,1)S(1)}, bf16[1536,128]{1,0:T(8,128)(2,1)S(1)}, u32[]{:S(2)}, u32[]{:S(2)}) collective-permute-start(bf16[1536,128]{1,0:T(8,128)(2,1)S(1)} %bitcast.37), channel_id=1, source_target_pairs={{0,1},{1,0},{2,3},{3,2},{4,5},{5,4},{6,7},{7,6},{8,9},{9,8},{10,11... | collective-permute-start | bytes 1179656 | tf_op jit(solution)/shard_map/ppermute | solution.py:269
Sparse Core Ops, SparseCore 0:
  31.8 298.7 all-reduce.2

commit v3 on v2

--- a/solution.py
+++ b/solution.py
@@ -14,7 +14,7 @@
 ANY = pl.BlockSpec(memory_space=pl.ANY)
 SMEM = pl.BlockSpec(memory_space=pltpu.SMEM)
 GROUP = 8
-DEPTH = 4
+BATCHES = 2
 MIB = 1024 * 1024
 
 
@@ -96,42 +96,58 @@
     )(tile_dest, peer_list, tiles, grad_blocks)
 
 
-def walk_groups(slots_ref, total, arrived_ref, held, sems, use):
-    block, width = held.shape[2:]
-
-    def fetch(g):
-        now = lax.rem(g, DEPTH)
-        for k in range(GROUP):
-            pltpu.make_async_copy(arrived_ref.at[slots_ref[g * GROUP + k]], held.at[now, k], sems.at[now]).start()
-
-    def settle(g):
-        now = lax.rem(g, DEPTH)
-        pltpu.make_async_copy(arrived_ref.at[pl.ds(0, GROUP)], held.at[now], sems.at[now]).wait()
-
-    for g in range(DEPTH - 1):
-        fetch(g)
-
-    def step(g, carry):
-        settle(g)
-        fetch(g + DEPTH - 1)
-        use(g, held[lax.rem(g, DEPTH)].reshape(GROUP * block, width))
+def arrivals(arrived_ref, held, sems):
+    part = held.shape[0] // BATCHES
+
+    def copy(i):
+        rows = pl.ds(i * part, part)
+        return pltpu.make_async_copy(arrived_ref.at[rows], held.at[rows], sems.at[i])
+
+    return copy
+
+
+def walk_groups(totals_ref, copy, use):
+    def single(g, carry):
+        use(g)
         return carry
 
-    lax.fori_loop(0, total, step, 0)
-    for g in range(DEPTH - 1):
-        settle(total + g)
-
-
-def weight_kernel(slots_ref, blocks_ref, rels_ref, total_ref, arrived_ref, turned_ref, root_ref, own_ref, other_ref, held, acc, sems):
+    def batch(i, first):
+        copy(i).wait()
+        end = totals_ref[i]
+        middle = first + (end - first) // 2 * 2
+
+        def two(j, carry):
+            use(first + 2 * j)
+            use(first + 2 * j + 1)
+            return carry
+
+        lax.fori_loop(0, (end - first) // 2, two, 0)
+        lax.fori_loop(middle, end, single, 0)
+        return end
+
+    lax.fori_loop(0, BATCHES, batch, 0)
+
+
+def weight_kernel(
+    slots_ref, blocks_ref, rels_ref, totals_ref, arrived_ref, turned_any, root_ref, own_ref, other_ref,
+    held, turned, acc, sems, turned_sem,
+):
     rel_count, width, _ = acc.shape
     half = width // 2
+    copy = arrivals(arrived_ref, held, sems)
+    turning = pltpu.make_async_copy(turned_any, turned, turned_sem)
+    turning.start()
+    for i in range(BATCHES):
+        copy(i).start()
     acc[...] = jnp.zeros_like(acc)
-
-    def use(g, rows):
-        left = jnp.concatenate([turned_ref[blocks_ref[g * GROUP + k]] for k in range(GROUP)], axis=1)
-        acc[rels_ref[g]] += jnp.dot(left, rows, preferred_element_type=jnp.float32)
-
-    walk_groups(slots_ref, total_ref[0], arrived_ref, held, sems, use)
+    turning.wait()
+
+    def use(g):
+        left = jnp.concatenate([turned[blocks_ref[g * GROUP + k]] for k in range(GROUP)], axis=1)
+        right = jnp.concatenate([held[slots_ref[g * GROUP + k]] for k in range(GROUP)], axis=0)
+        acc[rels_ref[g]] += jnp.dot(left, right, preferred_element_type=jnp.float32)
+
+    walk_groups(totals_ref, copy, use)
 
     def split(first, second):
         for ref, lanes in ((first, pl.ds(0, half)), (second, pl.ds(half, half))):
@@ -139,26 +155,34 @@
             for r in range(rel_count):
                 ref[pl.ds((1 + r) * width, width)] = acc[r, :, lanes]
 
-    @pl.when(total_ref[1] == 0)
+    @pl.when(totals_ref[BATCHES] == 0)
     def _():
         split(own_ref, other_ref)
 
-    @pl.when(total_ref[1] != 0)
+    @pl.when(totals_ref[BATCHES] != 0)
     def _():
         split(other_ref, own_ref)
 
 
-def feat_kernel(slots_ref, blocks_ref, rels_ref, total_ref, arrived_ref, base_ref, weight_ref, out_ref, held, acc, sems):
+def feat_kernel(
+    slots_ref, blocks_ref, rels_ref, totals_ref, arrived_ref, base_any, weight_ref, out_ref, held, acc, sems, base_sem
+):
     blocks, block, _ = out_ref.shape
-    acc[pl.ds(0, blocks)] = base_ref[...]
+    copy = arrivals(arrived_ref, held, sems)
+    base = pltpu.make_async_copy(base_any, acc.at[pl.ds(0, blocks)], base_sem)
+    base.start()
+    for i in range(BATCHES):
+        copy(i).start()
     acc[blocks] = jnp.zeros(acc.shape[1:], jnp.float32)
-
-    def use(g, rows):
+    base.wait()
+
+    def use(g):
+        rows = jnp.concatenate([held[slots_ref[g * GROUP + k]] for k in range(GROUP)], axis=0)
         part = jnp.dot(rows, weight_ref[rels_ref[g]], preferred_element_type=jnp.float32)
         for k in range(GROUP):
             acc[blocks_ref[g * GROUP + k]] += part[k * block : (k + 1) * block]
 
-    walk_groups(slots_ref, total_ref[0], arrived_ref, held, sems, use)
+    walk_groups(totals_ref, copy, use)
     out_ref[...] = acc[pl.ds(0, blocks)].astype(jnp.bfloat16)
 
 
@@ -173,17 +197,19 @@
         [jnp.where(high >= 0, low % kinds, -1), jnp.where(high > low, high % kinds, -1)], axis=1
     ).reshape(-1)
     slot_total = tags.shape[0]
-    rel = jnp.where(tags >= 0, tags // blocks, rel_count)
+    order = jnp.arange(slot_total, dtype=jnp.int32)
+    rel_kinds = rel_count * BATCHES
+    batch = order // (slot_total // BATCHES)
+    rel = jnp.where(tags >= 0, batch * rel_count + tags // blocks, rel_kinds)
     block_of = tags % blocks
-    order = jnp.arange(slot_total, dtype=jnp.int32)
     ranks = jnp.sum(((rel[None, :] == rel[:, None]) & (order[None, :] < order[:, None])).astype(jnp.int32), axis=1)
-    kinds_of = jnp.arange(rel_count, dtype=jnp.int32)
+    kinds_of = jnp.arange(rel_kinds, dtype=jnp.int32)
     counts = jnp.sum((rel[None, :] == kinds_of[:, None]).astype(jnp.int32), axis=1)
     padded = (counts + GROUP - 1) // GROUP * GROUP
     ends = jnp.sum(jnp.where(kinds_of[None, :] <= kinds_of[:, None], padded[None, :], 0), axis=1)
     starts = ends - padded
     start_of = jnp.sum(jnp.where(rel[:, None] == kinds_of[None, :], starts[None, :], 0), axis=1)
-    places = (-(-slot_total // GROUP) + rel_count + DEPTH - 1) * GROUP
+    places = (-(-slot_total // GROUP) + rel_kinds) * GROUP
     place = jnp.where(tags >= 0, start_of + ranks, places)
     hit = place[None, :] == jnp.arange(places, dtype=jnp.int32)[:, None]
     slot_at = jnp.sum(jnp.where(hit, order[None, :], 0), axis=1)
@@ -193,8 +219,7 @@
     slot_at = jnp.where(filled.reshape(-1, GROUP), by_group, by_group[:, :1]).reshape(-1)
     group_start = jnp.arange(places // GROUP, dtype=jnp.int32) * GROUP
     rel_at = jnp.sum((group_start[:, None] >= ends[None, :]).astype(jnp.int32), axis=1)
-    rel_at = jnp.minimum(rel_at, rel_count - 1)
-    return slot_at, block_at, rel_at, ends[-1:] // GROUP
+    return slot_at, block_at, rel_at % rel_count, ends[rel_count - 1 :: rel_count] // GROUP
 
 
 def shards(features, out_grad, rel_weight, root_weight, tiles, tile_dest, tile_peer, tile_source, tile_rel):
@@ -212,9 +237,10 @@
     peer_list = tile_peer[:, 0]
     grad_blocks = out_grad.reshape(blocks, block, width)
 
-    codes = ((peer_list * rel_count + tile_rel) * blocks + tile_source).astype(jnp.float32)
-    rows = lax.broadcasted_iota(jnp.int32, (dev_count, tile_count), 0)
-    table = lax.psum(jnp.where(rows == me, codes[None, :], 0.0), AXES).astype(jnp.int32)
+    codes = (peer_list * rel_count + tile_rel) * blocks + tile_source
+    table = lax.all_to_all(
+        jnp.broadcast_to(codes[None, None], (dev_count, 1, tile_count)), AXES, split_axis=0, concat_axis=0, tiled=True
+    ).reshape(dev_count, tile_count)
     slot_at, block_at, rel_at, total = plan_groups(table, me, blocks, rel_count)
     total = jnp.concatenate([total, core[None].astype(jnp.int32)])
 
@@ -232,8 +258,8 @@
     slot_at, block_at, rel_at, total, turned, root_grad, base, turned_weight = lax.optimization_barrier(
         (slot_at, block_at, rel_at, total, turned, root_grad, base, turned_weight)
     )
-    ring = [pltpu.VMEM((DEPTH, GROUP, block, width), jnp.bfloat16)]
-    sems = [pltpu.SemaphoreType.DMA((DEPTH,))]
+    room = pltpu.VMEM((slots, block, width), jnp.bfloat16)
+    sems = [pltpu.SemaphoreType.DMA((BATCHES,)), pltpu.SemaphoreType.DMA]
     cost = pl.CostEstimate(
         flops=slots * block * width * width, bytes_accessed=slots * block * width * 2, transcendentals=0
     )
@@ -242,10 +268,11 @@
     own, other = pl.pallas_call(
         weight_kernel,
         out_shape=(half, half),
-        in_specs=[SMEM] * 4 + [ANY, VMEM, VMEM],
+        in_specs=[SMEM] * 4 + [ANY, ANY, VMEM],
         out_specs=(VMEM, VMEM),
-        scratch_shapes=ring + [pltpu.VMEM((rel_count, width, width), jnp.float32)] + sems,
-        compiler_params=pltpu.CompilerParams(vmem_limit_bytes=20 * MIB),
+        scratch_shapes=[room, pltpu.VMEM(turned.shape, jnp.bfloat16), pltpu.VMEM((rel_count, width, width), jnp.float32)]
+        + sems,
+        compiler_params=pltpu.CompilerParams(vmem_limit_bytes=36 * MIB),
         cost_estimate=cost,
     )(slot_at, block_at, rel_at, total, arrived, turned, root_grad)
     swap = [(0, 1), (1, 0)]
@@ -254,10 +281,10 @@
     grad_feat = pl.pallas_call(
         feat_kernel,
         out_shape=jax.ShapeDtypeStruct((blocks, block, width), jnp.bfloat16),
-        in_specs=[SMEM] * 4 + [ANY, VMEM, VMEM],
+        in_specs=[SMEM] * 4 + [ANY, ANY, VMEM],
         out_specs=VMEM,
-        scratch_shapes=ring + [pltpu.VMEM((blocks + 1, block, width), jnp.float32)] + sems,
-        compiler_params=pltpu.CompilerParams(vmem_limit_bytes=28 * MIB),
+        scratch_shapes=[room, pltpu.VMEM((blocks + 1, block, width), jnp.float32)] + sems,
+        compiler_params=pltpu.CompilerParams(vmem_limit_bytes=40 * MIB),
         cost_estimate=cost,
     )(slot_at, block_at, rel_at, total, arrived, base.reshape(blocks, block, width), turned_weight)
 

time: 414 us -> 337 us (0.81)
  waiting for transfers between devices: 299 us -> 206 us
  starting transfers between devices: 27.7 us -> 56.1 us
  between operations: 16.9 us -> 0.85 us
  other arithmetic: 5.33 us -> 9.54 us
    psum x1 -> x0, waiting for transfers between devices: 292 us -> none  [shards(): lax.psum(jnp.where(rows == me, codes[None, :], 0.0), AXES).astype(jnp.int32)]
    all_to_all x1, waiting for transfers between devices: 0.01 us -> 197 us  [shards(): lax.all_to_all(outgoing.reshape(dev_count, cap, block, width), AXES, spli...]
    all_to_all x1, starting transfers between devices: 12.4 us -> 34.3 us  [shards(): spread = lax.all_to_all(own.reshape(shape), CHIPS, 0, 0, tiled=True)]
    all_to_all x0 -> x1, starting transfers between devices: none -> 11.5 us  [shards(): lax.all_to_all(jnp.broadcast_to(codes[None, None], (dev_count, 1, tile_co...]
    div x0 -> x1, other arithmetic: none -> 5.02 us  [plan_groups(): mine = table // kinds == me]
    all_to_all x1, starting transfers between devices: 12 us -> 7.04 us  [shards(): lax.all_to_all(outgoing.reshape(dev_count, cap, block, width), AXES, spli...]
  transfers between devices with their start and end apart: 5 -> 5, of which waited for: 4 -> 5; matrix products, arithmetic and copies ran while one was open for 4% -> 5% of each run, Pallas kernels for 2% -> 5%
where the time goes in v3:
time: 337 us; the launch traced here: 336 us
  waiting for transfers between devices  206 us (61%)
  starting transfers between devices  56.1 us (17%)
  Pallas kernels  26.1 us (8%)
  blocking collectives  23.4 us (7%)
  local copies, waits for them, and re-layouts  10.6 us (3%)
  other arithmetic  9.54 us (3%)
  matrix products  3.53 us (1%)
    all_to_all x1, waiting for transfers between devices, shards(): lax.all_to_all(outgoing.reshape(dev_count, cap, block, width), AXES, spli...  197 us
    all_to_all x1, starting transfers between devices, shards(): spread = lax.all_to_all(own.reshape(shape), CHIPS, 0, 0, tiled=True)  34.3 us
    all_to_all x1, blocking collectives, shards(): lax.all_to_all(jnp.broadcast_to(share[None], shape), CHIPS, 0, 0, tiled=T...  23.4 us
    all_to_all x1, starting transfers between devices, shards(): lax.all_to_all(jnp.broadcast_to(codes[None, None], (dev_count, 1, tile_co...  11.5 us
    pallas_call x1, Pallas kernels, shards(): pl.pallas_call(feat_kernel, out_shape=jax.ShapeDtypeStruct((blocks, block...  10.8 us
    pallas_call x1, Pallas kernels, shards(): pl.pallas_call(weight_kernel, out_shape=(half, half), in_specs=[SMEM] * 4...  8.89 us
    all_to_all x1, starting transfers between devices, shards(): lax.all_to_all(outgoing.reshape(dev_count, cap, block, width), AXES, spli...  7.04 us
  transfers between devices with their start and end apart: 5, of which 5 were waited for; matrix products, arithmetic and copies ran while one was open for 5% of the time, Pallas kernels for 5%

profile of v3, /device:TPU:1, one launch (start us, length us, event | category | flops | bytes accessed | tf_op | source)
XLA Modules:
  0.0 336.1 jit_solution(13970595015685375616)
XLA Ops:
  0.6 0.0 copy-start
  0.6 0.7 multiply_add_fusion
  1.4 0.7 broadcast_in_dim.105
  2.0 11.5 %all-to-all-start = ((s32[128,1,128]{2,1,0:T(1,128)}), s32[128,1,128]{2,1,0:T(1,128)S(1)}, u32[]{:S(2)}, u32[]{:S(2)}) async-start(s32[128,1,128]{2,1,0:T(1,128)} %broadcast_in_dim.105), calls=%async_computation | async-start | bytes 131072 | tf_op jit(solution)/shard_map/all_to_all | solution.py:241
  13.5 6.4 %shard_map.104 = bf16[256,128,256]{2,1,0:T(8,128)(2,1)} custom-call(s32[128]{0:T(128)} %refs_0_.1, s32[128]{0:T(128)} %bitcast.75, bf16[128,128,128]{2,1,0:T(8,128)(2,1)} %refs_2_.1, bf16[32,128,256]{2,1,0:T(8,128)(2,1)} %bitcast.66), custom_call_target="tpu_custom_call" | custom-call | flops 1073741824 | bytes 12582912 | tf_op jit(solution)/shard_map/pallas_call | solution.py:75
  19.9 3.2 all-to-all-done
  23.1 7.0 %all-to-all-start.1 = ((bf16[128,2,128,256]{3,2,1,0:T(8,128)(2,1)}), bf16[128,2,128,256]{3,2,1,0:T(8,128)(2,1)}, u32[]{:S(2)}, u32[]{:S(2)}) async-start(bf16[128,2,128,256]{3,2,1,0:T(8,128)(2,1)} %bitcast.65), calls=%async_computation.1 | async-start | bytes 33554432 | tf_op jit(solution)/shard_map/all_to_all | solution.py:248
  30.1 1.3 copy.35
  31.5 2.9 copy.34
  34.3 2.0 concatenate.11.turned_any
  36.4 0.2 copy-done.2
  36.6 0.6 copy-done.4
  37.2 0.7 fusion.12.root_ref
  37.9 2.8 fusion.13
  40.7 5.0 %div.49 = s32[128,1,128]{2,1,0:T(1,128)S(1)} divide(s32[128,1,128]{2,1,0:T(1,128)S(1)} %all-to-all-done, s32[128,1,128]{2,1,0:T(1,128)S(1)} %bitcast.74) | non-fusion elementwise | flops 16384 | bytes 196608 | tf_op jit(solution)/shard_map/jit(floor_divide)/div | solution.py:192
  45.8 0.2 select_reduce_fusion.2
  46.0 0.1 copy.33
  46.1 0.1 reshape.286
  46.2 0.1 convert_reduce_fusion.1
  46.4 0.1 select_reduce_fusion.5
  46.5 0.1 slice.7
  46.6 0.1 select_reduce_fusion.4
  46.7 0.2 convert_reduce_fusion
  46.9 0.2 select_reduce_fusion
  47.1 0.1 reshape.287
  47.2 0.1 slice_reduce_fusion
  47.3 0.1 broadcast_in_dim.117
  47.4 0.1 broadcast_in_dim.118
  47.5 0.2 fusion
  47.6 0.1 pad_add_fusion.1.totals_ref
  47.7 0.1 convert_reduce_fusion.2
  47.8 197.1 %all-to-all-done.1 = bf16[128,2,128,256]{3,2,1,0:T(8,128)(2,1)} async-done(((bf16[128,2,128,256]{3,2,1,0:T(8,128)(2,1)}), bf16[128,2,128,256]{3,2,1,0:T(8,128)(2,1)}, u32[]{:S(2)}, u32[]{:S(2)}) %all-to-all-start.1) | async-done | bytes 16777248 | tf_op jit(solution)/shard_map/all_to_all | solution.py:248
  244.9 8.9 %shard_map.105 = (f32[1536,128]{1,0:T(8,128)S(1)}, f32[1536,128]{1,0:T(8,128)S(1)}) custom-call(s32[336]{0:T(512)S(1)} %select_n.188.slots_ref, s32[336]{0:T(512)S(1)} %broadcast_add_fusion.blocks_ref, s32[42]{0:T(128)S(1)} %and_select_fusion.1.rels_ref, s32[3]{0:T(128)S(1)} %pad_add_fusion.1.totals_ref, bf16[256,128,256]{2,1,0:T(8,128)(2,1)} %bitcast.17.arrived_ref, ...), custom_call_target="tpu_custom_call" | custom-call | flops 2147483648 | bytes 16777216 | tf_op jit(solution)/shard_map/pallas_call | solution.py:268
  253.8 2.3 collective-permute-start
  256.1 1.9 collective-permute-done
  258.0 1.0 add.155
  259.0 34.3 %all-to-all-start.2 = ((f32[64,24,128]{2,1,0:T(8,128)}), f32[64,24,128]{2,1,0:T(8,128)S(1)}, u32[]{:S(2)}, u32[]{:S(2)}) async-start(f32[64,24,128]{2,1,0:T(8,128)} %bitcast.18), calls=%async_computation.2 | async-start | bytes 1572864 | tf_op jit(solution)/shard_map/all_to_all | solution.py:292
  293.3 2.2 copy-done.1
  295.5 10.8 %shard_map.106 = bf16[32,128,256]{2,1,0:T(8,128)(2,1)} custom-call(s32[336]{0:T(512)S(1)} %select_n.188.slots_ref, s32[336]{0:T(512)S(1)} %broadcast_add_fusion.blocks_ref, s32[42]{0:T(128)S(1)} %and_select_fusion.1.rels_ref, s32[3]{0:T(128)S(1)} %pad_add_fusion.1.totals_ref, bf16[256,128,256]{2,1,0:T(8,128)(2,1)} %bitcast.17.arrived_ref, ...), custom_call_target="tpu_custom_call" | custom-call | flops 2147483648 | bytes 16777216 | tf_op jit(solution)/shard_map/pallas_call | solution.py:281
  306.3 2.4 all-to-all-done.2
  308.7 0.1 reduce_sum.79
  308.8 0.1 broadcast_in_dim.121
  308.9 23.4 %all_to_all.20 = bf16[64,24,128]{2,1,0:T(8,128)(2,1)S(1)} all-to-all(bf16[64,24,128]{2,1,0:T(8,128)(2,1)S(1)} %broadcast_in_dim.121), channel_id=1, replica_groups=mesh['z'=4,'y'=4,'x'=4,'c'=2] {'z','y','x'}, dimensions={0} | all-to-all | bytes 786432 | tf_op jit(solution)/shard_map/all_to_all | solution.py:295
  332.3 1.0 collective-permute-start.1
  333.3 1.3 collective-permute-done.1
  334.7 0.1 broadcast_select_fusion.1
  334.7 0.1 pad_maximum_fusion
  334.8 1.3 convert.2
  (20 shorter events, 0.1 us)
Async XLA Ops:
  0.6 37.3 %copy-start = (bf16[256,256]{1,0:T(8,128)(2,1)S(1)}, bf16[256,256]{1,0:T(8,128)(2,1)}, u32[]{:S(2)}) copy-start(bf16[256,256]{1,0:T(8,128)(2,1)} %param.12) | copy-start | bytes 393220
  2.0 21.0 %all-to-all-start = ((s32[128,1,128]{2,1,0:T(1,128)}), s32[128,1,128]{2,1,0:T(1,128)S(1)}, u32[]{:S(2)}, u32[]{:S(2)}) async-start(s32[128,1,128]{2,1,0:T(1,128)} %broadcast_in_dim.105), calls=%async_computation | async-start | bytes 131072 | tf_op jit(solution)/shard_map/all_to_all | solution.py:241
  23.1 8.4 %copy-start.3 = (bf16[4096,256]{1,0:T(8,128)(2,1)S(1)}, bf16[4096,256]{1,0:T(8,128)(2,1)}, u32[]{:S(2)}) copy-start(bf16[4096,256]{1,0:T(8,128)(2,1)} %param.9) | copy-start | bytes 6291460
  23.1 221.9 %all-to-all-start.1 = ((bf16[128,2,128,256]{3,2,1,0:T(8,128)(2,1)}), bf16[128,2,128,256]{3,2,1,0:T(8,128)(2,1)}, u32[]{:S(2)}, u32[]{:S(2)}) async-start(bf16[128,2,128,256]{3,2,1,0:T(8,128)(2,1)} %bitcast.65), calls=%async_computation.1 | async-start | bytes 33554432 | tf_op jit(solution)/shard_map/all_to_all | solution.py:248
  34.3 2.2 copy-start.2
  34.3 2.9 copy-start.4
  253.8 4.2 %collective-permute-start = (f32[1536,128]{1,0:T(8,128)S(1)}, f32[1536,128]{1,0:T(8,128)S(1)}, u32[]{:S(2)}, u32[]{:S(2)}) collective-permute-start(f32[1536,128]{1,0:T(8,128)S(1)} %get-tuple-element.23), channel_id=1, source_target_pairs={{0,1},{1,0},{2,3},{3,2},{4,5},{5,4},{6,7},{7,6},{8,9},{9,8},{10,11... | collective-permute-start | bytes 2359304 | tf_op jit(solution)/shard_map/ppermute | solution.py:279
  259.0 49.8 %all-to-all-start.2 = ((f32[64,24,128]{2,1,0:T(8,128)}), f32[64,24,128]{2,1,0:T(8,128)S(1)}, u32[]{:S(2)}, u32[]{:S(2)}) async-start(f32[64,24,128]{2,1,0:T(8,128)} %bitcast.18), calls=%async_computation.2 | async-start | bytes 1572864 | tf_op jit(solution)/shard_map/all_to_all | solution.py:292
  293.3 2.2 copy-start.1
  332.3 2.4 collective-permute-start.1

commit v4 on v3

--- a/solution.py
+++ b/solution.py
@@ -129,31 +129,50 @@
 
 
 def weight_kernel(
-    slots_ref, blocks_ref, rels_ref, totals_ref, arrived_ref, turned_any, root_ref, own_ref, other_ref,
-    held, turned, acc, sems, turned_sem,
+    slots_ref, blocks_ref, rels_ref, totals_ref, arrived_ref, feat_any, grad_any, own_ref, other_ref,
+    held, feat, grad, turned, acc, sems, feat_sem, grad_sem,
 ):
-    rel_count, width, _ = acc.shape
+    kinds, width, _ = acc.shape
+    blocks, block, _ = feat.shape
     half = width // 2
     copy = arrivals(arrived_ref, held, sems)
-    turning = pltpu.make_async_copy(turned_any, turned, turned_sem)
-    turning.start()
+    feat_copy = pltpu.make_async_copy(feat_any, feat, feat_sem)
+    grad_copy = pltpu.make_async_copy(grad_any, grad, grad_sem)
+    feat_copy.start()
+    grad_copy.start()
     for i in range(BATCHES):
         copy(i).start()
     acc[...] = jnp.zeros_like(acc)
-    turning.wait()
+    turned[blocks] = jnp.zeros(turned.shape[1:], turned.dtype)
+    feat_copy.wait()
+
+    def turn(b, carry):
+        for k in range(4):
+            turned[b * 4 + k] = feat[b * 4 + k].T
+        return carry
+
+    lax.fori_loop(0, blocks // 4, turn, 0)
+    grad_copy.wait()
+
+    def root(g, carry):
+        left = jnp.concatenate([turned[g * GROUP + k] for k in range(GROUP)], axis=1)
+        right = grad[pl.ds(g * GROUP, GROUP)].reshape(GROUP * block, width)
+        acc[0] += jnp.dot(left, right, preferred_element_type=jnp.float32)
+        return carry
+
+    lax.fori_loop(0, blocks // GROUP, root, 0)
 
     def use(g):
         left = jnp.concatenate([turned[blocks_ref[g * GROUP + k]] for k in range(GROUP)], axis=1)
         right = jnp.concatenate([held[slots_ref[g * GROUP + k]] for k in range(GROUP)], axis=0)
-        acc[rels_ref[g]] += jnp.dot(left, right, preferred_element_type=jnp.float32)
+        acc[1 + rels_ref[g]] += jnp.dot(left, right, preferred_element_type=jnp.float32)
 
     walk_groups(totals_ref, copy, use)
 
     def split(first, second):
         for ref, lanes in ((first, pl.ds(0, half)), (second, pl.ds(half, half))):
-            ref[pl.ds(0, width)] = root_ref[:, lanes]
-            for r in range(rel_count):
-                ref[pl.ds((1 + r) * width, width)] = acc[r, :, lanes]
+            for r in range(kinds):
+                ref[pl.ds(r * width, width)] = acc[r, :, lanes]
 
     @pl.when(totals_ref[BATCHES] == 0)
     def _():
@@ -165,20 +184,30 @@
 
 
 def feat_kernel(
-    slots_ref, blocks_ref, rels_ref, totals_ref, arrived_ref, base_any, weight_ref, out_ref, held, acc, sems, base_sem
+    slots_ref, blocks_ref, rels_ref, totals_ref, arrived_ref, grad_any, root_ref, weight_ref, out_ref,
+    held, grad, acc, sems, grad_sem,
 ):
-    blocks, block, _ = out_ref.shape
+    blocks, block, width = out_ref.shape
     copy = arrivals(arrived_ref, held, sems)
-    base = pltpu.make_async_copy(base_any, acc.at[pl.ds(0, blocks)], base_sem)
-    base.start()
+    grad_copy = pltpu.make_async_copy(grad_any, grad, grad_sem)
+    grad_copy.start()
     for i in range(BATCHES):
         copy(i).start()
     acc[blocks] = jnp.zeros(acc.shape[1:], jnp.float32)
-    base.wait()
+    across = (((1,), (1,)), ((), ()))
+    grad_copy.wait()
+
+    def base(g, carry):
+        rows = grad[pl.ds(g * GROUP, GROUP)].reshape(GROUP * block, width)
+        part = lax.dot_general(rows, root_ref[...], across, preferred_element_type=jnp.float32)
+        acc[pl.ds(g * GROUP, GROUP)] = part.reshape(GROUP, block, width)
+        return carry
+
+    lax.fori_loop(0, blocks // GROUP, base, 0)
 
     def use(g):
         rows = jnp.concatenate([held[slots_ref[g * GROUP + k]] for k in range(GROUP)], axis=0)
-        part = jnp.dot(rows, weight_ref[rels_ref[g]], preferred_element_type=jnp.float32)
+        part = lax.dot_general(rows, weight_ref[rels_ref[g]], across, preferred_element_type=jnp.float32)
         for k in range(GROUP):
             acc[blocks_ref[g * GROUP + k]] += part[k * block : (k + 1) * block]
 
@@ -188,13 +217,13 @@
 
 def plan_groups(table, me, blocks, rel_count):
     senders, tile_count = table.shape
-    kinds = rel_count * blocks
-    mine = (table // kinds) == me
-    key = lax.broadcasted_iota(jnp.int32, table.shape, 1) * kinds + table % kinds
+    kinds = 1 << (rel_count * blocks - 1).bit_length()
+    mine = (table >> (kinds.bit_length() - 1)) == me
+    key = lax.broadcasted_iota(jnp.int32, table.shape, 1) * kinds + (table & (kinds - 1))
     low = jnp.min(jnp.where(mine, key, tile_count * kinds), axis=1)
     high = jnp.max(jnp.where(mine, key, -1), axis=1)
     tags = jnp.stack(
-        [jnp.where(high >= 0, low % kinds, -1), jnp.where(high > low, high % kinds, -1)], axis=1
+        [jnp.where(high >= 0, low & (kinds - 1), -1), jnp.where(high > low, high & (kinds - 1), -1)], axis=1
     ).reshape(-1)
     slot_total = tags.shape[0]
     order = jnp.arange(slot_total, dtype=jnp.int32)
@@ -237,7 +266,8 @@
     peer_list = tile_peer[:, 0]
     grad_blocks = out_grad.reshape(blocks, block, width)
 
-    codes = (peer_list * rel_count + tile_rel) * blocks + tile_source
+    kinds = 1 << (rel_count * blocks - 1).bit_length()
+    codes = peer_list * kinds + tile_rel * blocks + tile_source
     table = lax.all_to_all(
         jnp.broadcast_to(codes[None, None], (dev_count, 1, tile_count)), AXES, split_axis=0, concat_axis=0, tiled=True
     ).reshape(dev_count, tile_count)
@@ -245,21 +275,14 @@
     total = jnp.concatenate([total, core[None].astype(jnp.int32)])
 
     outgoing = make_messages(tile_dest, peer_list, tiles, grad_blocks, slots, cap)
+    outgoing, slot_at, block_at, rel_at, total = lax.optimization_barrier((outgoing, slot_at, block_at, rel_at, total))
     arrived = lax.all_to_all(
         outgoing.reshape(dev_count, cap, block, width), AXES, split_axis=0, concat_axis=0, tiled=True
     ).reshape(slots, block, width)
 
-    turned = jnp.swapaxes(features.reshape(blocks, block, width), 1, 2)
-    turned = jnp.concatenate([turned, jnp.zeros((1, width, block), jnp.bfloat16)], axis=0)
-    root_grad = jnp.einsum("nd,nc->dc", features, out_grad, preferred_element_type=jnp.float32)
-    base = jnp.einsum("nc,dc->nd", out_grad, root_weight, preferred_element_type=jnp.float32)
-    turned_weight = jnp.swapaxes(rel_weight, 1, 2)
-
-    slot_at, block_at, rel_at, total, turned, root_grad, base, turned_weight = lax.optimization_barrier(
-        (slot_at, block_at, rel_at, total, turned, root_grad, base, turned_weight)
-    )
     room = pltpu.VMEM((slots, block, width), jnp.bfloat16)
-    sems = [pltpu.SemaphoreType.DMA((BATCHES,)), pltpu.SemaphoreType.DMA]
+    local = pltpu.VMEM(grad_blocks.shape, jnp.bfloat16)
+    dma = pltpu.SemaphoreType.DMA
     cost = pl.CostEstimate(
         flops=slots * block * width * width, bytes_accessed=slots * block * width * 2, transcendentals=0
     )
@@ -268,25 +291,40 @@
     own, other = pl.pallas_call(
         weight_kernel,
         out_shape=(half, half),
-        in_specs=[SMEM] * 4 + [ANY, ANY, VMEM],
+        in_specs=[SMEM] * 4 + [ANY] * 3,
         out_specs=(VMEM, VMEM),
-        scratch_shapes=[room, pltpu.VMEM(turned.shape, jnp.bfloat16), pltpu.VMEM((rel_count, width, width), jnp.float32)]
-        + sems,
-        compiler_params=pltpu.CompilerParams(vmem_limit_bytes=36 * MIB),
+        scratch_shapes=[
+            room,
+            local,
+            local,
+            pltpu.VMEM((blocks + 1, width, block), jnp.bfloat16),
+            pltpu.VMEM((1 + rel_count, width, width), jnp.float32),
+            dma((BATCHES,)),
+            dma,
+            dma,
+        ],
+        compiler_params=pltpu.CompilerParams(vmem_limit_bytes=56 * MIB),
         cost_estimate=cost,
-    )(slot_at, block_at, rel_at, total, arrived, turned, root_grad)
+    )(slot_at, block_at, rel_at, total, arrived, features.reshape(blocks, block, width), grad_blocks)
+
     swap = [(0, 1), (1, 0)]
     own = own + lax.ppermute(other, "c", swap)
     own, total = lax.optimization_barrier((own, total))
     grad_feat = pl.pallas_call(
         feat_kernel,
         out_shape=jax.ShapeDtypeStruct((blocks, block, width), jnp.bfloat16),
-        in_specs=[SMEM] * 4 + [ANY, ANY, VMEM],
+        in_specs=[SMEM] * 4 + [ANY, ANY, VMEM, VMEM],
         out_specs=VMEM,
-        scratch_shapes=[room, pltpu.VMEM((blocks + 1, block, width), jnp.float32)] + sems,
+        scratch_shapes=[
+            room,
+            local,
+            pltpu.VMEM((blocks + 1, block, width), jnp.float32),
+            dma((BATCHES,)),
+            dma,
+        ],
         compiler_params=pltpu.CompilerParams(vmem_limit_bytes=40 * MIB),
         cost_estimate=cost,
-    )(slot_at, block_at, rel_at, total, arrived, base.reshape(blocks, block, width), turned_weight)
+    )(slot_at, block_at, rel_at, total, arrived, grad_blocks, root_weight, rel_weight)
 
     shape = (chips, half_rows // chips, width // 2)
     spread = lax.all_to_all(own.reshape(shape), CHIPS, 0, 0, tiled=True)

time: 337 us -> 291 us (0.86)
  waiting for transfers between devices: 206 us -> 10.6 us
  blocking collectives: 23.4 us -> 214 us
  starting transfers between devices: 56.1 us -> 24.2 us
  local copies, waits for them, and re-layouts: 10.6 us -> 1.46 us
  Pallas kernels: 26.1 us -> 29.9 us
  matrix products: 3.53 us -> 0 us
    all_to_all x1 -> x0, waiting for transfers between devices: 197 us -> none  [shards(): lax.all_to_all(outgoing.reshape(dev_count, cap, block, width), AXES, spli...]
    all_to_all x0 -> x1, blocking collectives: none -> 195 us  [shards(): lax.all_to_all(outgoing.reshape(dev_count, cap, block, width), AXES, spli...]
    all_to_all x1, starting transfers between devices: 34.3 us -> 8.6 us  [shards(): spread = lax.all_to_all(own.reshape(shape), CHIPS, 0, 0, tiled=True)]
    all_to_all x1 -> x0, starting transfers between devices: 7.04 us -> none  [shards(): lax.all_to_all(outgoing.reshape(dev_count, cap, block, width), AXES, spli...]
    div x1 -> x0, other arithmetic: 5.02 us -> none  [plan_groups(): mine = table // kinds == me]
    unnamed x11 -> x14, local copies, waits for them, and re-layouts: 4.33 us -> 0.04 us
    all_to_all x1, blocking collectives: 23.4 us -> 19.1 us  [shards(): lax.all_to_all(jnp.broadcast_to(share[None], shape), CHIPS, 0, 0, tiled=T...]
    pallas_call x1, Pallas kernels: 8.89 us -> 12.5 us  [shards(): pl.pallas_call(weight_kernel, out_shape=(half, half), in_specs=[SMEM] * 4...]
  transfers between devices with their start and end apart: 5 -> 4, of which waited for: 5 -> 4; matrix products, arithmetic and copies ran while one was open for 5% -> 0% of each run, Pallas kernels for 5% -> 6%
where the time goes in v4:
time: 291 us; the launch traced here: 290 us
  blocking collectives  214 us (74%)
  Pallas kernels  29.9 us (10%)
  starting transfers between devices  24.2 us (8%)
  waiting for transfers between devices  10.6 us (4%)
  other arithmetic  9.01 us (3%)
    all_to_all x1, blocking collectives, shards(): lax.all_to_all(outgoing.reshape(dev_count, cap, block, width), AXES, spli...  195 us
    all_to_all x1, blocking collectives, shards(): lax.all_to_all(jnp.broadcast_to(share[None], shape), CHIPS, 0, 0, tiled=T...  19.1 us
    pallas_call x1, Pallas kernels, shards(): pl.pallas_call(weight_kernel, out_shape=(half, half), in_specs=[SMEM] * 4...  12.5 us
    all_to_all x1, starting transfers between devices, shards(): lax.all_to_all(jnp.broadcast_to(codes[None, None], (dev_count, 1, tile_co...  11.5 us
    pallas_call x1, Pallas kernels, shards(): pl.pallas_call(feat_kernel, out_shape=jax.ShapeDtypeStruct((blocks, block...  11 us
    all_to_all x1, starting transfers between devices, shards(): spread = lax.all_to_all(own.reshape(shape), CHIPS, 0, 0, tiled=True)  8.6 us
    pallas_call x1, Pallas kernels, make_messages(): pl.pallas_call(kernel, out_shape=jax.ShapeDtypeStruct((slots, block, widt...  6.34 us
  transfers between devices with their start and end apart: 4, of which 4 were waited for; matrix products, arithmetic and copies ran while one was open for 0% of the time, Pallas kernels for 6%

profile of v4, /device:TPU:1, one launch (start us, length us, event | category | flops | bytes accessed | tf_op | source)
XLA Modules:
  0.0 289.7 jit_solution(17507457495578200084)
XLA Ops:
  0.6 0.7 add_add_fusion
  1.3 0.7 broadcast_in_dim.106
  2.0 11.5 %all-to-all-start = ((s32[128,1,128]{2,1,0:T(1,128)}), s32[128,1,128]{2,1,0:T(1,128)S(1)}, u32[]{:S(2)}, u32[]{:S(2)}) async-start(s32[128,1,128]{2,1,0:T(1,128)} %broadcast_in_dim.106), calls=%async_computation | async-start | bytes 131072 | tf_op jit(solution)/shard_map/all_to_all | solution.py:271
  13.5 6.3 %shard_map.104 = bf16[256,128,256]{2,1,0:T(8,128)(2,1)} custom-call(s32[128]{0:T(128)} %refs_0_.1, s32[128]{0:T(128)} %bitcast.35, bf16[128,128,128]{2,1,0:T(8,128)(2,1)} %refs_2_.1, bf16[32,128,256]{2,1,0:T(8,128)(2,1)} %bitcast.22), custom_call_target="tpu_custom_call" | custom-call | flops 1073741824 | bytes 12582912 | tf_op jit(solution)/shard_map/pallas_call | solution.py:75
  19.9 3.1 %all-to-all-done = s32[128,1,128]{2,1,0:T(1,128)S(1)} async-done(((s32[128,1,128]{2,1,0:T(1,128)}), s32[128,1,128]{2,1,0:T(1,128)S(1)}, u32[]{:S(2)}, u32[]{:S(2)}) %all-to-all-start) | async-done | bytes 65568 | tf_op jit(solution)/shard_map/all_to_all | solution.py:271
  23.0 0.1 broadcast_and_fusion
  23.1 0.1 select_reduce_fusion.2
  23.2 0.1 copy.18
  23.3 0.1 reshape.257
  23.5 0.1 convert_reduce_fusion.1
  23.6 0.1 select_reduce_fusion.5
  23.8 0.1 slice.7
  23.9 0.2 convert_reduce_fusion
  24.0 0.1 convert_reduce_fusion.2
  24.1 0.6 and_select_fusion.1.rels_ref
  24.7 0.1 select_reduce_fusion.4
  24.8 0.2 fusion
  25.0 0.2 select_reduce_fusion
  25.2 0.6 broadcast_add_fusion.blocks_ref
  25.8 0.1 reshape.258
  25.9 0.1 slice_reduce_fusion
  26.0 0.1 broadcast_in_dim.119
  26.1 0.1 broadcast_in_dim.120
  26.2 0.6 pad_add_fusion.1.totals_ref
  26.7 0.6 select_n.157.slots_ref
  27.3 194.5 %all_to_all.20 = bf16[128,2,128,256]{3,2,1,0:T(8,128)(2,1)} all-to-all(bf16[128,2,128,256]{3,2,1,0:T(8,128)(2,1)} %bitcast.27), channel_id=1, replica_groups=mesh['z'=4,'y'=4,'x'=4,'c'=2] {'z','y','x','c'}, dimensions={0} | all-to-all | bytes 33554432 | tf_op jit(solution)/shard_map/all_to_all | solution.py:279
  221.9 12.5 %shard_map.105 = (f32[1536,128]{1,0:T(8,128)}, f32[1536,128]{1,0:T(8,128)}) custom-call(s32[336]{0:T(512)} %select_n.157.slots_ref, s32[336]{0:T(512)} %broadcast_add_fusion.blocks_ref, s32[42]{0:T(128)} %and_select_fusion.1.rels_ref, s32[3]{0:T(128)} %pad_add_fusion.1.totals_ref, bf16[256,128,256]{2,1,0:T(8,128)(2,1)} %bitcast.25, ...), custom_call_target="tpu_custom_call" | custom-call | flops 2147483648 | bytes 16777216 | tf_op jit(solution)/shard_map/pallas_call | solution.py:291
  234.4 0.0 copy-start
  234.4 0.0 copy-start.1
  234.4 0.0 copy-start.2
  234.5 0.0 copy-start.3
  234.5 0.0 copy-start.4
  234.5 0.0 copy-start.5
  234.5 0.0 copy-start.6
  234.5 0.7 collective-permute-start
  235.2 2.1 collective-permute-done
  237.3 2.1 add.119
  239.4 8.6 %all-to-all-start.2 = ((f32[64,24,128]{2,1,0:T(8,128)}), f32[64,24,128]{2,1,0:T(8,128)}, u32[]{:S(2)}, u32[]{:S(2)}) async-start(f32[64,24,128]{2,1,0:T(8,128)} %bitcast.28), calls=%async_computation.2 | async-start | bytes 1572864 | tf_op jit(solution)/shard_map/all_to_all | solution.py:330
  248.1 11.0 %shard_map.106 = bf16[32,128,256]{2,1,0:T(8,128)(2,1)} custom-call(s32[336]{0:T(512)S(1)} %copy-done.4, s32[336]{0:T(512)S(1)} %copy-done.3, s32[42]{0:T(128)S(1)} %copy-done.5, s32[3]{0:T(128)S(1)} %copy-done.6, bf16[256,128,256]{2,1,0:T(8,128)(2,1)} %bitcast.26, bf16[32,128,256]{2,1,0:T(8,128)(2,1)S(1)} %bitcast.24, bf16[256,256]{1,0:T(8,128)(2,1)S(1)} %copy-done.2, ...), custom_call_target="tpu_custom_call" | custom-call | flops 2147483648 | bytes 16777216 | tf_op jit(solution)/shard_map/pallas_call | solution.py:313
  259.1 3.9 %all-to-all-done.2 = f32[64,24,128]{2,1,0:T(8,128)} async-done(((f32[64,24,128]{2,1,0:T(8,128)}), f32[64,24,128]{2,1,0:T(8,128)}, u32[]{:S(2)}, u32[]{:S(2)}) %all-to-all-start.2) | async-done | bytes 786464 | tf_op jit(solution)/shard_map/all_to_all | solution.py:330
  263.1 1.2 reduce_sum.79
  264.3 0.1 broadcast_in_dim.123
  264.4 19.1 %all_to_all.21 = bf16[64,24,128]{2,1,0:T(8,128)(2,1)S(1)} all-to-all(bf16[64,24,128]{2,1,0:T(8,128)(2,1)S(1)} %broadcast_in_dim.123), channel_id=1, replica_groups=mesh['z'=4,'y'=4,'x'=4,'c'=2] {'z','y','x'}, dimensions={0} | all-to-all | bytes 786432 | tf_op jit(solution)/shard_map/all_to_all | solution.py:333
  283.5 3.4 %collective-permute-start.1 = (bf16[1536,128]{1,0:T(8,128)(2,1)S(1)}, bf16[1536,128]{1,0:T(8,128)(2,1)S(1)}, u32[]{:S(2)}, u32[]{:S(2)}) collective-permute-start(bf16[1536,128]{1,0:T(8,128)(2,1)S(1)} %bitcast.32), channel_id=1, source_target_pairs={{0,1},{1,0},{2,3},{3,2},{4,5},{5,4},{6,7},{7,6},{8,9},{9,8},{10,11... | collective-permute-start | bytes 1179656 | tf_op jit(solution)/shard_map/ppermute | solution.py:334
  286.9 1.3 collective-permute-done.1
  288.2 0.1 broadcast_select_fusion.1
  288.3 0.1 pad_maximum_fusion
  288.4 1.3 convert.2
  (17 shorter events, 0.1 us)
Async XLA Ops:
  2.0 21.0 %all-to-all-start = ((s32[128,1,128]{2,1,0:T(1,128)}), s32[128,1,128]{2,1,0:T(1,128)S(1)}, u32[]{:S(2)}, u32[]{:S(2)}) async-start(s32[128,1,128]{2,1,0:T(1,128)} %broadcast_in_dim.106), calls=%async_computation | async-start | bytes 131072 | tf_op jit(solution)/shard_map/all_to_all | solution.py:271
  234.4 13.6 %copy-start = (bf16[4096,256]{1,0:T(8,128)(2,1)S(1)}, bf16[4096,256]{1,0:T(8,128)(2,1)}, u32[]{:S(2)}) copy-start(bf16[4096,256]{1,0:T(8,128)(2,1)} %param.10) | copy-start | bytes 6291460
  234.4 13.6 %copy-start.1 = (bf16[5,256,256]{2,1,0:T(8,128)(2,1)S(1)}, bf16[5,256,256]{2,1,0:T(8,128)(2,1)}, u32[]{:S(2)}) copy-start(bf16[5,256,256]{2,1,0:T(8,128)(2,1)} %weight_ref.1) | copy-start | bytes 1966084
  234.4 13.6 %copy-start.2 = (bf16[256,256]{1,0:T(8,128)(2,1)S(1)}, bf16[256,256]{1,0:T(8,128)(2,1)}, u32[]{:S(2)}) copy-start(bf16[256,256]{1,0:T(8,128)(2,1)} %root_ref.1) | copy-start | bytes 393220
  234.5 13.6 %copy-start.3 = (s32[336]{0:T(512)S(1)}, s32[336]{0:T(512)}, u32[]{:S(2)}) copy-start(s32[336]{0:T(512)} %broadcast_add_fusion.blocks_ref) | copy-start | bytes 4036
  234.5 13.6 %copy-start.4 = (s32[336]{0:T(512)S(1)}, s32[336]{0:T(512)}, u32[]{:S(2)}) copy-start(s32[336]{0:T(512)} %select_n.157.slots_ref) | copy-start | bytes 4036
  234.5 13.6 %copy-start.5 = (s32[42]{0:T(128)S(1)}, s32[42]{0:T(128)}, u32[]{:S(2)}) copy-start(s32[42]{0:T(128)} %and_select_fusion.1.rels_ref) | copy-start | bytes 508
  234.5 13.6 %copy-start.6 = (s32[3]{0:T(128)S(1)}, s32[3]{0:T(128)}, u32[]{:S(2)}) copy-start(s32[3]{0:T(128)} %pad_add_fusion.1.totals_ref) | copy-start | bytes 40
  234.5 2.8 collective-permute-start
  239.4 23.7 %all-to-all-start.2 = ((f32[64,24,128]{2,1,0:T(8,128)}), f32[64,24,128]{2,1,0:T(8,128)}, u32[]{:S(2)}, u32[]{:S(2)}) async-start(f32[64,24,128]{2,1,0:T(8,128)} %bitcast.28), calls=%async_computation.2 | async-start | bytes 1572864 | tf_op jit(solution)/shard_map/all_to_all | solution.py:330
  283.5 4.7 %collective-permute-start.1 = (bf16[1536,128]{1,0:T(8,128)(2,1)S(1)}, bf16[1536,128]{1,0:T(8,128)(2,1)S(1)}, u32[]{:S(2)}, u32[]{:S(2)}) collective-permute-start(bf16[1536,128]{1,0:T(8,128)(2,1)S(1)} %bitcast.32), channel_id=1, source_target_pairs={{0,1},{1,0},{2,3},{3,2},{4,5},{5,4},{6,7},{7,6},{8,9},{9,8},{10,11... | collective-permute-start | bytes 1179656 | tf_op jit(solution)/shard_map/ppermute | solution.py:334

commit v5 on v4

v5 whole, which is shorter than its diff:
```python
import math

import jax
import jax.numpy as jnp
from jax import lax
from jax.experimental import pallas as pl
from jax.experimental.pallas import tpu as pltpu
from jax.sharding import Mesh
from jax.sharding import PartitionSpec as P

AXES = ("z", "y", "x", "c")
CHIPS = ("z", "y", "x")
VMEM = pl.BlockSpec(memory_space=pltpu.VMEM)
ANY = pl.BlockSpec(memory_space=pl.ANY)
SMEM = pl.BlockSpec(memory_space=pltpu.SMEM)
MIB = 1024 * 1024
CAP = 2
GROUP = 8
BATCHES = 2
LANES = 128
TAG_ROWS = 16


def message_kernel(
    blocks, parts, dest_any, peer_any, rel_any, source_any, tiles_ref, grad_any, out_ref,
    dest, peers, rels, sources, count, grad, held, made, marks, tags, sems, out_sem,
):
    tile_count, block, _ = tiles_ref.shape
    part = tile_count // parts
    size = 2 * block
    pairs = ((dest_any, dest), (peer_any, peers), (rel_any, rels), (source_any, sources), (grad_any, grad))
    early = [pltpu.make_async_copy(src, dst, sems.at[parts + i]) for i, (src, dst) in enumerate(pairs)]
    for copy in early:
        copy.start()

    def fetch(i):
        rows = pl.ds(i * part, part)
        return pltpu.make_async_copy(tiles_ref.at[rows], held.at[rows], sems.at[i])

    for i in range(parts):
        fetch(i).start()

    def clear(i, carry):
        count[i] = 0
        return carry

    lax.fori_loop(0, count.shape[0], clear, 0)
    marks[...] = jnp.full(marks.shape, -1.0, jnp.float32)
    side = lax.broadcasted_iota(jnp.int32, marks.shape[1:], 1) // (LANES // CAP)
    for copy in early:
        copy.wait()

    for i in range(parts):
        fetch(i).wait()

        def step(j, carry):
            for k in range(16):
                t = i * part + j * 16 + k
                peer = peers[t]
                rank = count[peer]
                count[peer] = rank + 1
                mark = (rels[t] * blocks + sources[t]).astype(jnp.float32)
                marks[peer] = jnp.where(side == rank, mark, marks[peer])
                message = lax.dot_general(
                    held[t], grad[dest[t]], (((0,), (0,)), ((), ())), preferred_element_type=jnp.float32
                ).astype(jnp.bfloat16)
                made[t, pl.ds(0, block)] = message[:, :LANES]
                made[t, pl.ds(block, block)] = message[:, LANES:]
                rows = pl.ds(pl.multiple_of(rank * size, size), size)
                pltpu.make_async_copy(made.at[t], out_ref.at[peer, rows], out_sem).start()
            return carry

        lax.fori_loop(0, part // 16, step, 0)

    tags[...] = jnp.concatenate([marks[...], marks[...]], axis=1).astype(jnp.bfloat16)
    tag_copy = pltpu.make_async_copy(tags, out_ref.at[:, pl.ds(CAP * size, TAG_ROWS)], sems.at[0])
    tag_copy.start()
    pltpu.make_async_copy(made, out_ref.at[pl.ds(0, tile_count), pl.ds(0, size)], out_sem).wait()
    tag_copy.wait()


def make_messages(tile_dest, peer_list, tile_rel, tile_source, tiles, grad_blocks, dev_count):
    tile_count, block, _ = tiles.shape
    blocks, _, width = grad_blocks.shape
    parts = 8
    numbers = pltpu.SMEM((tile_count,), jnp.int32)

    def kernel(*refs):
        message_kernel(blocks, parts, *refs)

    return pl.pallas_call(
        kernel,
        out_shape=jax.ShapeDtypeStruct((dev_count, CAP * 2 * block + TAG_ROWS, LANES), jnp.bfloat16),
        in_specs=[ANY] * 6,
        out_specs=ANY,
        scratch_shapes=[
            numbers,
            numbers,
            numbers,
            numbers,
            pltpu.SMEM((dev_count,), jnp.int32),
            pltpu.VMEM(grad_blocks.shape, jnp.bfloat16),
            pltpu.VMEM(tiles.shape, jnp.bfloat16),
            pltpu.VMEM((tile_count, 2 * block, LANES), jnp.bfloat16),
            pltpu.VMEM((dev_count, TAG_ROWS // 2, LANES), jnp.float32),
            pltpu.VMEM((dev_count, TAG_ROWS, LANES), jnp.bfloat16),
            pltpu.SemaphoreType.DMA((parts + 5,)),
            pltpu.SemaphoreType.DMA,
        ],
        compiler_params=pltpu.CompilerParams(vmem_limit_bytes=58 * MIB),
        cost_estimate=pl.CostEstimate(
            flops=2 * tile_count * block * block * width,
            bytes_accessed=tile_count * block * (block + width) * 2,
            transcendentals=0,
        ),
    )(tile_dest, peer_list, tile_rel, tile_source, tiles, grad_blocks)


def make_plan(marks, blocks, rel_count):
    senders = marks.shape[0]
    places = plan_places(senders * CAP, rel_count)
    square = (senders, senders)
    row, lane = lax.broadcasted_iota(jnp.int32, square, 0), lax.broadcasted_iota(jnp.int32, square, 1)
    below = (lane < row).astype(jnp.float32)
    ahead = (row < lane).astype(jnp.float32)
    sender = lax.broadcasted_iota(jnp.int32, (senders, 1), 0).astype(jnp.float32)
    batch = jnp.floor(sender * (BATCHES / senders))
    kind_lane = lane.astype(jnp.float32)
    tag = [marks[:, 0:1], marks[:, LANES // CAP : LANES // CAP + 1]]
    rel = [jnp.floor(t * (1.0 / blocks)) for t in tag]
    block_of = [t - r * blocks for t, r in zip(tag, rel)]
    used = [jnp.where((kind_lane == batch * rel_count + r) & (t >= 0), 1.0, 0.0) for t, r in zip(tag, rel)]
    totals = [jnp.sum(u, axis=0, keepdims=True) for u in used]
    before = [jnp.dot(below, u, preferred_element_type=jnp.float32) for u in used]
    before[1] = before[1] + totals[0]
    groups = jnp.floor((totals[0] + totals[1] + (GROUP - 1)) * (1.0 / GROUP))
    first = jnp.dot(jnp.broadcast_to(groups, (8, senders)), ahead, preferred_element_type=jnp.float32)[0:1]
    place = [jnp.sum(u * (b + first * GROUP), axis=1, keepdims=True) for u, b in zip(used, before)]
    place = [jnp.where(t >= 0, p, -1.0) for t, p in zip(tag, place)]
    at_int = lax.broadcasted_iota(jnp.int32, (senders, places), 1)
    at, at_group = at_int.astype(jnp.float32), (at_int // GROUP * GROUP).astype(jnp.float32)
    here = [jnp.where(p == at, 1.0, 0.0) for p in place]
    leads = [jnp.where(p == at_group, 1.0, 0.0) for p in place]

    def gather(hits, values):
        return jnp.sum(hits[0] * values[0] + hits[1] * values[1], axis=0, keepdims=True)

    name = [sender * CAP, sender * CAP + 1]
    message = jnp.where(gather(here, [1.0, 1.0]) > 0, gather(here, name), gather(leads, name))
    source = gather(here, [b - blocks for b in block_of]) + blocks
    relation = gather(leads, rel)
    kind_row = kind_lane[0:1]
    ends = [
        jnp.sum(jnp.where(kind_row < rel_count * (i + 1), groups, 0.0), axis=1, keepdims=True) for i in range(BATCHES)
    ]
    rows = [message, source, relation] + [jnp.broadcast_to(e, (1, places)) for e in ends]
    rows.append(jnp.zeros((8 - len(rows), places), jnp.float32))
    return jnp.concatenate(rows, axis=0).astype(jnp.int32)


def plan_places(slots, rel_count):
    return -(-(-(-slots // GROUP) + rel_count * BATCHES) * GROUP // LANES) * LANES


def arrivals(arrived_ref, held, sems):
    part = held.shape[0] // BATCHES

    def copy(i):
        rows = pl.ds(i * part, part)
        return pltpu.make_async_copy(arrived_ref.at[rows, pl.ds(0, held.shape[1])], held.at[rows], sems.at[i])

    return copy


def take(held, message, block):
    top = pl.multiple_of((message % CAP) * (2 * block), 2 * block)
    sender = message // CAP
    return jnp.concatenate([held[sender, pl.ds(top, block)], held[sender, pl.ds(top + block, block)]], axis=1)


def walk_groups(plan_ref, copy, use):
    def single(g, carry):
        use(g)
        return carry

    def batch(i, first):
        copy(i).wait()
        end = plan_ref[3 + i, 0]
        middle = first + (end - first) // 2 * 2

        def two(j, carry):
            use(first + 2 * j)
            use(first + 2 * j + 1)
            return carry

        lax.fori_loop(0, (end - first) // 2, two, 0)
        lax.fori_loop(middle, end, single, 0)
        return end

    lax.fori_loop(0, BATCHES, batch, 0)


def weight_kernel(
    arrived_ref, feat_any, grad_any, core_ref, own_ref, other_ref, plan_ref,
    held, feat, grad, turned, acc, tags, plan, sems, feat_sem, grad_sem, tag_sem,
):
    kinds, width, _ = acc.shape
    blocks, block, _ = feat.shape
    half = width // 2
    tag_copy = pltpu.make_async_copy(arrived_ref.at[:, pl.ds(held.shape[1], TAG_ROWS)], tags, tag_sem)
    feat_copy = pltpu.make_async_copy(feat_any, feat, feat_sem)
    grad_copy = pltpu.make_async_copy(grad_any, grad, grad_sem)
    tag_copy.start()
    feat_copy.start()
    grad_copy.start()
    copy = arrivals(arrived_ref, held, sems)
    for i in range(BATCHES):
        copy(i).start()
    acc[...] = jnp.zeros_like(acc)
    turned[blocks] = jnp.zeros(turned.shape[1:], turned.dtype)
    tag_copy.wait()
    plan_ref[...] = make_plan(jnp.max(tags[...].astype(jnp.float32), axis=1), blocks, kinds - 1)
    plan_copy = pltpu.make_async_copy(plan_ref, plan, tag_sem)
    plan_copy.start()
    feat_copy.wait()

    def turn(b, carry):
        for k in range(4):
            turned[b * 4 + k] = feat[b * 4 + k].T
        return carry

    lax.fori_loop(0, blocks // 4, turn, 0)
    grad_copy.wait()

    def root(g, carry):
        left = jnp.concatenate([turned[g * GROUP + k] for k in range(GROUP)], axis=1)
        right = grad[pl.ds(g * GROUP, GROUP)].reshape(GROUP * block, width)
        acc[0] += jnp.dot(left, right, preferred_element_type=jnp.float32)
        return carry

    lax.fori_loop(0, blocks // GROUP, root, 0)
    plan_copy.wait()

    def use(g):
        left = jnp.concatenate([turned[plan[1, g * GROUP + k]] for k in range(GROUP)], axis=1)
        right = jnp.concatenate([take(held, plan[0, g * GROUP + k], block) for k in range(GROUP)], axis=0)
        acc[1 + plan[2, g * GROUP]] += jnp.dot(left, right, preferred_element_type=jnp.float32)

    walk_groups(plan, copy, use)

    def split(first, second):
        for ref, lanes in ((first, pl.ds(0, half)), (second, pl.ds(half, half))):
            for r in range(kinds):
                ref[pl.ds(r * width, width)] = acc[r, :, lanes]

    @pl.when(core_ref[0] == 0)
    def _():
        split(own_ref, other_ref)

    @pl.when(core_ref[0] != 0)
    def _():
        split(other_ref, own_ref)


def feat_kernel(plan_ref, arrived_ref, grad_any, root_ref, weight_ref, out_ref, held, grad, acc, sems, grad_sem):
    blocks, block, width = out_ref.shape
    copy = arrivals(arrived_ref, held, sems)
    grad_copy = pltpu.make_async_copy(grad_any, grad, grad_sem)
    grad_copy.start()
    for i in range(BATCHES):
        copy(i).start()
    acc[blocks] = jnp.zeros(acc.shape[1:], jnp.float32)
    across = (((1,), (1,)), ((), ()))
    grad_copy.wait()

    def base(g, carry):
        rows = grad[pl.ds(g * GROUP, GROUP)].reshape(GROUP * block, width)
        part = lax.dot_general(rows, root_ref[...], across, preferred_element_type=jnp.float32)
        acc[pl.ds(g * GROUP, GROUP)] = part.reshape(GROUP, block, width)
        return carry

    lax.fori_loop(0, blocks // GROUP, base, 0)

    def use(g):
        rows = jnp.concatenate([take(held, plan_ref[0, g * GROUP + k], block) for k in range(GROUP)], axis=0)
        part = lax.dot_general(rows, weight_ref[plan_ref[2, g * GROUP]], across, preferred_element_type=jnp.float32)
        for k in range(GROUP):
            acc[plan_ref[1, g * GROUP + k]] += part[k * block : (k + 1) * block]

    walk_groups(plan_ref, copy, use)
    out_ref[...] = acc[pl.ds(0, blocks)].astype(jnp.bfloat16)


def shards(features, out_grad, rel_weight, root_weight, tiles, tile_dest, tile_peer, tile_source, tile_rel):
    dev_count = lax.axis_size(AXES)
    chips = lax.axis_size(CHIPS)
    core = lax.axis_index("c")
    block = tiles.shape[1]
    width = features.shape[1]
    rel_count = rel_weight.shape[0]
    blocks = features.shape[0] // block
    slots = dev_count * CAP
    scale = 1.0 / math.sqrt(features.shape[0] * dev_count)
    grad_blocks = out_grad.reshape(blocks, block, width)

    outgoing = make_messages(tile_dest, tile_peer[:, 0], tile_rel, tile_source, tiles, grad_blocks, dev_count)
    arrived = lax.all_to_all(outgoing, AXES, split_axis=0, concat_axis=0, tiled=True)

    room = pltpu.VMEM((dev_count, CAP * 2 * block, LANES), jnp.bfloat16)
    local = pltpu.VMEM(grad_blocks.shape, jnp.bfloat16)
    dma = pltpu.SemaphoreType.DMA
    cost = pl.CostEstimate(
        flops=slots * block * width * width, bytes_accessed=slots * block * width * 2, transcendentals=0
    )
    half_rows = (1 + rel_count) * width
    half = jax.ShapeDtypeStruct((half_rows, width // 2), jnp.float32)
    plan_type = jax.ShapeDtypeStruct((8, plan_places(slots, rel_count)), jnp.int32)
    own, other, plan = pl.pallas_call(
        weight_kernel,
        out_shape=(half, half, plan_type),
        in_specs=[ANY] * 3 + [SMEM],
        out_specs=(VMEM, VMEM, VMEM),
        scratch_shapes=[
            room,
            local,
            local,
            pltpu.VMEM((blocks + 1, width, block), jnp.bfloat16),
            pltpu.VMEM((1 + rel_count, width, width), jnp.float32),
            pltpu.VMEM((dev_count, TAG_ROWS, LANES), jnp.bfloat16),
            pltpu.SMEM(plan_type.shape, jnp.int32),
            dma((BATCHES,)),
            dma,
            dma,
            dma,
        ],
        compiler_params=pltpu.CompilerParams(vmem_limit_bytes=36 * MIB),
        cost_estimate=cost,
    )(arrived, features.reshape(blocks, block, width), grad_blocks, core[None].astype(jnp.int32))

    swap = [(0, 1), (1, 0)]
    own = own + lax.ppermute(other, "c", swap)
    own, plan = lax.optimization_barrier((own, plan))
    grad_feat = pl.pallas_call(
        feat_kernel,
        out_shape=jax.ShapeDtypeStruct((blocks, block, width), jnp.bfloat16),
        in_specs=[SMEM, ANY, ANY, VMEM, VMEM],
        out_specs=VMEM,
        scratch_shapes=[
            room,
            local,
            pltpu.VMEM((blocks + 1, block, width), jnp.float32),
            dma((BATCHES,)),
            dma,
        ],
        compiler_params=pltpu.CompilerParams(vmem_limit_bytes=32 * MIB),
        cost_estimate=cost,
    )(plan, arrived, grad_blocks, root_weight, rel_weight)

    shape = (chips, half_rows // chips, width // 2)
    spread = lax.all_to_all(own.reshape(shape), CHIPS, 0, 0, tiled=True)
    spread, grad_feat = lax.optimization_barrier((spread, grad_feat))
    share = (spread.sum(axis=0) * scale).astype(jnp.bfloat16)
    own = lax.all_to_all(jnp.broadcast_to(share[None], shape), CHIPS, 0, 0, tiled=True).reshape(half.shape)
    other = lax.ppermute(own, "c", swap)
    left = jnp.where(core == 0, own, other).astype(jnp.float32)
    right = jnp.where(core == 0, other, own).astype(jnp.float32)
    grad_weights = jnp.concatenate([left, right], axis=1).reshape(1 + rel_count, width, width)
    return grad_feat.reshape(features.shape), grad_weights


def solution(mesh):
    sizes = (4, 4, 4, 2)
    fine = Mesh(mesh.devices.reshape(sizes), AXES)
    return jax.shard_map(
        shards,
        mesh=fine,
        in_specs=(
            P(AXES, None),
            P(AXES, None),
            P(),
            P(),
            P(AXES, None, None),
            P(AXES),
            P(AXES, None),
            P(AXES),
            P(AXES),
        ),
        out_specs=(P(AXES, None), P()),
        check_vma=False,
    )
```

time: 291 us -> 335 us (1.15); the launches traced: 290 us -> 337 us
  waiting for transfers between devices: 10.6 us -> 230 us
  blocking collectives: 214 us -> 22.2 us
  starting transfers between devices: 24.2 us -> 51.2 us
  other arithmetic: 9.01 us -> 3.63 us
    all_to_all x1, waiting for transfers between devices: 3.14 us -> 223 us  [shards(): lax.all_to_all(outgoing, AXES, split_axis=0, concat_axis=0, tiled=True)]
    all_to_all x1 -> x0, blocking collectives: 195 us -> none  [shards(): lax.all_to_all(outgoing.reshape(dev_count, cap, block, width), AXES, spli...]
    all_to_all x1, starting transfers between devices: 8.6 us -> 32.1 us  [shards(): spread = lax.all_to_all(own.reshape(shape), CHIPS, 0, 0, tiled=True)]
    ppermute x1, starting transfers between devices: 0.7 us -> 5.78 us  [shards(): own = own + lax.ppermute(other, 'c', swap)]
  transfers between devices with their start and end apart: 4 -> 4, of which waited for: 4 -> 4; matrix products, arithmetic and copies ran while one was open for 0% -> 0% of each run, Pallas kernels for 6% -> 3%
where the time goes in v5:
time: 335 us; the launch traced here: 337 us
  waiting for transfers between devices  230 us (69%)
  starting transfers between devices  51.2 us (15%)
  Pallas kernels  27.8 us (8%)
  blocking collectives  22.2 us (7%)
  other arithmetic  3.63 us (1%)
    all_to_all x1, waiting for transfers between devices, shards(): lax.all_to_all(outgoing, AXES, split_axis=0, concat_axis=0, tiled=True)  223 us
    all_to_all x1, starting transfers between devices, shards(): spread = lax.all_to_all(own.reshape(shape), CHIPS, 0, 0, tiled=True)  32.1 us
    all_to_all x1, blocking collectives, shards(): lax.all_to_all(jnp.broadcast_to(share[None], shape), CHIPS, 0, 0, tiled=T...  22.2 us
    all_to_all x1, starting transfers between devices, shards(): lax.all_to_all(outgoing, AXES, split_axis=0, concat_axis=0, tiled=True)  11.9 us
    pallas_call x1, Pallas kernels, shards(): pl.pallas_call(feat_kernel, out_shape=jax.ShapeDtypeStruct((blocks, block...  11.4 us
    pallas_call x1, Pallas kernels, shards(): pl.pallas_call(weight_kernel, out_shape=(half, half, plan_type), in_specs...  9.79 us
  transfers between devices with their start and end apart: 4, of which 4 were waited for; matrix products, arithmetic and copies ran while one was open for 0% of the time, Pallas kernels for 3%

profile of v5, /device:TPU:1, one launch (start us, length us, event | category | flops | bytes accessed | tf_op | source)
XLA Modules:
  0.0 337.2 jit_solution(17687514885262074924)
XLA Ops:
  0.6 6.6 %shard_map.104 = bf16[128,528,128]{2,1,0:T(8,128)(2,1)} custom-call(s32[128]{0:T(128)} %refs_0_.1, s32[128]{0:T(128)} %bitcast.19, s32[128]{0:T(128)} %refs_2_.1, s32[128]{0:T(128)} %refs_3_.1, bf16[128,128,128]{2,1,0:T(8,128)(2,1)} %refs_4_.1, bf16[32,128,256]{2,1,0:T(8,128)(2,1)} %bitcast.11), custom_call_target="tpu_custom_call" | custom-call | flops 1073741824 | bytes 12582912 | tf_op jit(solution)/shard_map/pallas_call | solution.py:91
  7.2 0.0 copy-start
  7.2 11.9 %all-to-all-start = ((bf16[128,528,128]{2,1,0:T(8,128)(2,1)}), bf16[128,528,128]{2,1,0:T(8,128)(2,1)}, u32[]{:S(2)}, u32[]{:S(2)}) async-start(bf16[128,528,128]{2,1,0:T(8,128)(2,1)} %shard_map.104), calls=%async_computation | async-start | bytes 34603008 | tf_op jit(solution)/shard_map/all_to_all | solution.py:307
  19.2 222.8 %all-to-all-done.arrived_ref = bf16[128,528,128]{2,1,0:T(8,128)(2,1)} async-done(((bf16[128,528,128]{2,1,0:T(8,128)(2,1)}), bf16[128,528,128]{2,1,0:T(8,128)(2,1)}, u32[]{:S(2)}, u32[]{:S(2)}) %all-to-all-start) | async-done | bytes 17301536 | tf_op jit(solution)/shard_map/all_to_all | solution.py:307
  242.0 0.0 copy-done
  242.0 0.0 copy-start.1
  242.0 1.6 copy-done.1
  243.6 9.8 %shard_map.105 = (f32[1536,128]{1,0:T(8,128)S(1)}, f32[1536,128]{1,0:T(8,128)S(1)}, s32[8,384]{1,0:T(8,128)S(1)}) custom-call(bf16[128,528,128]{2,1,0:T(8,128)(2,1)} %all-to-all-done.arrived_ref, bf16[32,128,256]{2,1,0:T(8,128)(2,1)S(1)} %bitcast.14, bf16[32,128,256]{2,1,0:T(8,128)(2,1)S(1)} %bitcast.12, s32[1]{0:T(128)} %bitcast.3.core_ref), custom_call_target="tpu_custom_call" | custom-call | flops 2147483648 | bytes 16777216 | tf_op jit(solution)/shard_map/pallas_call | solution.py:318
  253.4 0.0 copy-start.2
  253.4 0.0 copy-start.3
  253.4 5.8 %collective-permute-start = (f32[1536,128]{1,0:T(8,128)S(1)}, f32[1536,128]{1,0:T(8,128)S(1)}, u32[]{:S(2)}, u32[]{:S(2)}) collective-permute-start(f32[1536,128]{1,0:T(8,128)S(1)} %get-tuple-element.10), channel_id=1, source_target_pairs={{0,1},{1,0},{2,3},{3,2},{4,5},{5,4},{6,7},{7,6},{8,9},{9,8},{10,11... | collective-permute-start | bytes 2359304 | tf_op jit(solution)/shard_map/ppermute | solution.py:341
  259.2 1.9 collective-permute-done
  261.1 1.0 add.3
  262.0 32.1 %all-to-all-start.1 = ((f32[64,24,128]{2,1,0:T(8,128)}), f32[64,24,128]{2,1,0:T(8,128)}, u32[]{:S(2)}, u32[]{:S(2)}) async-start(f32[64,24,128]{2,1,0:T(8,128)} %bitcast.15), calls=%async_computation.1 | async-start | bytes 1572864 | tf_op jit(solution)/shard_map/all_to_all | solution.py:360
  294.1 0.0 copy-done.2
  294.2 0.0 copy-done.3
  294.2 11.4 %shard_map.106 = bf16[32,128,256]{2,1,0:T(8,128)(2,1)} custom-call(s32[8,384]{1,0:T(8,128)S(1)} %get-tuple-element.13.plan_ref, bf16[128,528,128]{2,1,0:T(8,128)(2,1)} %all-to-all-done.arrived_ref, bf16[32,128,256]{2,1,0:T(8,128)(2,1)S(1)} %bitcast.13, bf16[256,256]{1,0:T(8,128)(2,1)S(1)} %copy-done.3, bf16[5,256,256]{2,1,0:T(8,128)(2,1)S(1)} %copy-done.2), custom_call_target="tpu_custom_call" | custom-call | flops 2147483648 | bytes 16777216 | tf_op jit(solution)/shard_map/pallas_call | solution.py:343
  305.6 3.9 %all-to-all-done.1 = f32[64,24,128]{2,1,0:T(8,128)} async-done(((f32[64,24,128]{2,1,0:T(8,128)}), f32[64,24,128]{2,1,0:T(8,128)}, u32[]{:S(2)}, u32[]{:S(2)}) %all-to-all-start.1) | async-done | bytes 786464 | tf_op jit(solution)/shard_map/all_to_all | solution.py:360
  309.5 1.2 reduce_sum.9
  310.7 0.1 broadcast_in_dim.10
  310.8 22.2 %all_to_all.15 = bf16[64,24,128]{2,1,0:T(8,128)(2,1)S(1)} all-to-all(bf16[64,24,128]{2,1,0:T(8,128)(2,1)S(1)} %broadcast_in_dim.10), channel_id=1, replica_groups=mesh['z'=4,'y'=4,'x'=4,'c'=2] {'z','y','x'}, dimensions={0} | all-to-all | bytes 786432 | tf_op jit(solution)/shard_map/all_to_all | solution.py:363
  332.9 1.4 collective-permute-start.1
  334.3 1.3 collective-permute-done.1
  335.7 0.1 broadcast_select_fusion.1
  335.8 0.1 pad_maximum_fusion
  335.9 1.3 convert.2
  (1 shorter events, 0.0 us)
Async XLA Ops:
  7.2 234.7 %copy-start = (bf16[4096,256]{1,0:T(8,128)(2,1)S(1)}, bf16[4096,256]{1,0:T(8,128)(2,1)}, u32[]{:S(2)}) copy-start(bf16[4096,256]{1,0:T(8,128)(2,1)} %param.10) | copy-start | bytes 6291460
  7.2 234.7 %all-to-all-start = ((bf16[128,528,128]{2,1,0:T(8,128)(2,1)}), bf16[128,528,128]{2,1,0:T(8,128)(2,1)}, u32[]{:S(2)}, u32[]{:S(2)}) async-start(bf16[128,528,128]{2,1,0:T(8,128)(2,1)} %shard_map.104), calls=%async_computation | async-start | bytes 34603008 | tf_op jit(solution)/shard_map/all_to_all | solution.py:307
  242.0 1.6 copy-start.1
  253.4 40.8 %copy-start.2 = (bf16[5,256,256]{2,1,0:T(8,128)(2,1)S(1)}, bf16[5,256,256]{2,1,0:T(8,128)(2,1)}, u32[]{:S(2)}) copy-start(bf16[5,256,256]{2,1,0:T(8,128)(2,1)} %weight_ref.1) | copy-start | bytes 1966084
  253.4 40.8 %copy-start.3 = (bf16[256,256]{1,0:T(8,128)(2,1)S(1)}, bf16[256,256]{1,0:T(8,128)(2,1)}, u32[]{:S(2)}) copy-start(bf16[256,256]{1,0:T(8,128)(2,1)} %root_ref.1) | copy-start | bytes 393220
  253.4 7.7 %collective-permute-start = (f32[1536,128]{1,0:T(8,128)S(1)}, f32[1536,128]{1,0:T(8,128)S(1)}, u32[]{:S(2)}, u32[]{:S(2)}) collective-permute-start(f32[1536,128]{1,0:T(8,128)S(1)} %get-tuple-element.10), channel_id=1, source_target_pairs={{0,1},{1,0},{2,3},{3,2},{4,5},{5,4},{6,7},{7,6},{8,9},{9,8},{10,11... | collective-permute-start | bytes 2359304 | tf_op jit(solution)/shard_map/ppermute | solution.py:341
  262.0 47.4 %all-to-all-start.1 = ((f32[64,24,128]{2,1,0:T(8,128)}), f32[64,24,128]{2,1,0:T(8,128)}, u32[]{:S(2)}, u32[]{:S(2)}) async-start(f32[64,24,128]{2,1,0:T(8,128)} %bitcast.15), calls=%async_computation.1 | async-start | bytes 1572864 | tf_op jit(solution)/shard_map/all_to_all | solution.py:360
  332.9 2.8 collective-permute-start.1

commit v6 on v5

--- a/solution.py
+++ b/solution.py
@@ -304,6 +304,7 @@
     grad_blocks = out_grad.reshape(blocks, block, width)
 
     outgoing = make_messages(tile_dest, tile_peer[:, 0], tile_rel, tile_source, tiles, grad_blocks, dev_count)
+    outgoing, core = lax.optimization_barrier((outgoing, core[None].astype(jnp.int32)))
     arrived = lax.all_to_all(outgoing, AXES, split_axis=0, concat_axis=0, tiled=True)
 
     room = pltpu.VMEM((dev_count, CAP * 2 * block, LANES), jnp.bfloat16)
@@ -333,9 +334,9 @@
             dma,
             dma,
         ],
-        compiler_params=pltpu.CompilerParams(vmem_limit_bytes=36 * MIB),
+        compiler_params=pltpu.CompilerParams(vmem_limit_bytes=57 * MIB),
         cost_estimate=cost,
-    )(arrived, features.reshape(blocks, block, width), grad_blocks, core[None].astype(jnp.int32))
+    )(arrived, features.reshape(blocks, block, width), grad_blocks, core)
 
     swap = [(0, 1), (1, 0)]
     own = own + lax.ppermute(other, "c", swap)
@@ -352,7 +353,7 @@
             dma((BATCHES,)),
             dma,
         ],
-        compiler_params=pltpu.CompilerParams(vmem_limit_bytes=32 * MIB),
+        compiler_params=pltpu.CompilerParams(vmem_limit_bytes=57 * MIB),
         cost_estimate=cost,
     )(plan, arrived, grad_blocks, root_weight, rel_weight)
 
@@ -362,6 +363,7 @@
     share = (spread.sum(axis=0) * scale).astype(jnp.bfloat16)
     own = lax.all_to_all(jnp.broadcast_to(share[None], shape), CHIPS, 0, 0, tiled=True).reshape(half.shape)
     other = lax.ppermute(own, "c", swap)
+    core = core[0]
     left = jnp.where(core == 0, own, other).astype(jnp.float32)
     right = jnp.where(core == 0, other, own).astype(jnp.float32)
     grad_weights = jnp.concatenate([left, right], axis=1).reshape(1 + rel_count, width, width)

time: 335 us -> 284 us (0.85)
  waiting for transfers between devices: 230 us -> 5.01 us
  blocking collectives: 22.2 us -> 228 us
  starting transfers between devices: 51.2 us -> 12.9 us
  Pallas kernels: 27.8 us -> 33.5 us
    all_to_all x1 -> x0, waiting for transfers between devices: 223 us -> none  [shards(): lax.all_to_all(outgoing, AXES, split_axis=0, concat_axis=0, tiled=True)]
    all_to_all x0 -> x1, blocking collectives: none -> 205 us  [shards(): lax.all_to_all(outgoing, AXES, split_axis=0, concat_axis=0, tiled=True)]
    all_to_all x1, starting transfers between devices: 32.1 us -> 8.7 us  [shards(): spread = lax.all_to_all(own.reshape(shape), CHIPS, 0, 0, tiled=True)]
    all_to_all x1 -> x0, starting transfers between devices: 11.9 us -> none  [shards(): lax.all_to_all(outgoing, AXES, split_axis=0, concat_axis=0, tiled=True)]
    ppermute x1, starting transfers between devices: 5.78 us -> 1.11 us  [shards(): own = own + lax.ppermute(other, 'c', swap)]
    pallas_call x1, Pallas kernels: 9.79 us -> 13.3 us  [shards(): pl.pallas_call(weight_kernel, out_shape=(half, half, plan_type), in_specs...]
  transfers between devices with their start and end apart: 4 -> 3, of which waited for: 4 -> 3; matrix products, arithmetic and copies ran while one was open for 0% -> 0% of each run, Pallas kernels for 3% -> 5%
where the time goes in v6:
time: 284 us
  blocking collectives  228 us (80%)
  Pallas kernels  33.5 us (12%)
  starting transfers between devices  12.9 us (5%)
  waiting for transfers between devices  5.01 us (2%)
  other arithmetic  3.63 us (1%)
    all_to_all x1, blocking collectives, shards(): lax.all_to_all(outgoing, AXES, split_axis=0, concat_axis=0, tiled=True)  205 us
    all_to_all x1, blocking collectives, shards(): lax.all_to_all(jnp.broadcast_to(share[None], shape), CHIPS, 0, 0, tiled=T...  22.8 us
    pallas_call x1, Pallas kernels, shards(): pl.pallas_call(feat_kernel, out_shape=jax.ShapeDtypeStruct((blocks, block...  13.6 us
    pallas_call x1, Pallas kernels, shards(): pl.pallas_call(weight_kernel, out_shape=(half, half, plan_type), in_specs...  13.3 us
    all_to_all x1, starting transfers between devices, shards(): spread = lax.all_to_all(own.reshape(shape), CHIPS, 0, 0, tiled=True)  8.7 us
    pallas_call x1, Pallas kernels, make_messages(): pl.pallas_call(kernel, out_shape=jax.ShapeDtypeStruct((dev_count, CAP * 2...  6.56 us
  transfers between devices with their start and end apart: 3, of which 3 were waited for; matrix products, arithmetic and copies ran while one was open for 0% of the time, Pallas kernels for 5%

profile of v6, /device:TPU:1, one launch (start us, length us, event | category | flops | bytes accessed | tf_op | source)
XLA Modules:
  0.0 283.7 jit_solution(2684899991127871414)
XLA Ops:
  0.6 6.6 %shard_map.104 = bf16[128,528,128]{2,1,0:T(8,128)(2,1)} custom-call(s32[128]{0:T(128)} %refs_0_.1, s32[128]{0:T(128)} %bitcast.19, s32[128]{0:T(128)} %refs_2_.1, s32[128]{0:T(128)} %refs_3_.1, bf16[128,128,128]{2,1,0:T(8,128)(2,1)} %refs_4_.1, bf16[32,128,256]{2,1,0:T(8,128)(2,1)} %bitcast.12), custom_call_target="tpu_custom_call" | custom-call | flops 1073741824 | bytes 12582912 | tf_op jit(solution)/shard_map/pallas_call | solution.py:91
  7.2 205.1 %all_to_all.15.arrived_ref = bf16[128,528,128]{2,1,0:T(8,128)(2,1)} all-to-all(bf16[128,528,128]{2,1,0:T(8,128)(2,1)} %shard_map.104), channel_id=1, replica_groups=mesh['z'=4,'y'=4,'x'=4,'c'=2] {'z','y','x','c'}, dimensions={0} | all-to-all | bytes 34603008 | tf_op jit(solution)/shard_map/all_to_all | solution.py:308
  212.3 13.3 %shard_map.105 = (f32[1536,128]{1,0:T(8,128)}, f32[1536,128]{1,0:T(8,128)}, s32[8,384]{1,0:T(8,128)}) custom-call(bf16[128,528,128]{2,1,0:T(8,128)(2,1)} %all_to_all.15.arrived_ref, bf16[32,128,256]{2,1,0:T(8,128)(2,1)} %bitcast.16, bf16[32,128,256]{2,1,0:T(8,128)(2,1)} %bitcast.13, s32[1]{0:T(128)} %bitcast.2.core_ref), custom_call_target="tpu_custom_call" | custom-call | flops 2147483648 | bytes 16777216 | tf_op jit(solution)/shard_map/pallas_call | solution.py:319
  225.7 1.1 collective-permute-start
  226.8 2.1 collective-permute-done
  228.9 2.1 add.3
  231.0 8.7 %all-to-all-start.1 = ((f32[64,24,128]{2,1,0:T(8,128)}), f32[64,24,128]{2,1,0:T(8,128)S(1)}, u32[]{:S(2)}, u32[]{:S(2)}) async-start(f32[64,24,128]{2,1,0:T(8,128)} %bitcast.4), calls=%async_computation.1 | async-start | bytes 1572864 | tf_op jit(solution)/shard_map/all_to_all | solution.py:361
  239.7 13.6 %shard_map.106 = bf16[32,128,256]{2,1,0:T(8,128)(2,1)} custom-call(s32[8,384]{1,0:T(8,128)} %get-tuple-element.17.plan_ref, bf16[128,528,128]{2,1,0:T(8,128)(2,1)} %all_to_all.15.arrived_ref, bf16[32,128,256]{2,1,0:T(8,128)(2,1)} %bitcast.14, bf16[256,256]{1,0:T(8,128)(2,1)} %root_ref.1, bf16[5,256,256]{2,1,0:T(8,128)(2,1)} %weight_ref.1), custom_call_target="tpu_custom_call" | custom-call | flops 2147483648 | bytes 16777216 | tf_op jit(solution)/shard_map/pallas_call | solution.py:344
  253.3 1.5 all-to-all-done.1
  254.9 0.1 reduce_sum.9
  255.0 0.1 broadcast_in_dim.10
  255.0 22.8 %all_to_all.16 = bf16[64,24,128]{2,1,0:T(8,128)(2,1)S(1)} all-to-all(bf16[64,24,128]{2,1,0:T(8,128)(2,1)S(1)} %broadcast_in_dim.10), channel_id=1, replica_groups=mesh['z'=4,'y'=4,'x'=4,'c'=2] {'z','y','x'}, dimensions={0} | all-to-all | bytes 786432 | tf_op jit(solution)/shard_map/all_to_all | solution.py:364
  277.8 3.1 %collective-permute-start.1 = (bf16[1536,128]{1,0:T(8,128)(2,1)S(1)}, bf16[1536,128]{1,0:T(8,128)(2,1)S(1)}, u32[]{:S(2)}, u32[]{:S(2)}) collective-permute-start(bf16[1536,128]{1,0:T(8,128)(2,1)S(1)} %bitcast.18), channel_id=1, source_target_pairs={{0,1},{1,0},{2,3},{3,2},{4,5},{5,4},{6,7},{7,6},{8,9},{9,8},{10,11... | collective-permute-start | bytes 1179656 | tf_op jit(solution)/shard_map/ppermute | solution.py:365
  280.9 1.3 collective-permute-done.1
  282.2 0.1 broadcast_select_fusion.1
  282.3 0.1 pad_maximum_fusion
  282.4 1.3 convert.2
  (1 shorter events, 0.0 us)
Async XLA Ops:
  225.7 3.2 %collective-permute-start = (f32[1536,128]{1,0:T(8,128)}, f32[1536,128]{1,0:T(8,128)S(1)}, u32[]{:S(2)}, u32[]{:S(2)}) collective-permute-start(f32[1536,128]{1,0:T(8,128)} %get-tuple-element.14), channel_id=1, source_target_pairs={{0,1},{1,0},{2,3},{3,2},{4,5},{5,4},{6,7},{7,6},{8,9},{9,8},{10,11... | collective-permute-start | bytes 2359304 | tf_op jit(solution)/shard_map/ppermute | solution.py:342
  231.0 23.9 %all-to-all-start.1 = ((f32[64,24,128]{2,1,0:T(8,128)}), f32[64,24,128]{2,1,0:T(8,128)S(1)}, u32[]{:S(2)}, u32[]{:S(2)}) async-start(f32[64,24,128]{2,1,0:T(8,128)} %bitcast.4), calls=%async_computation.1 | async-start | bytes 1572864 | tf_op jit(solution)/shard_map/all_to_all | solution.py:361
  277.8 4.4 %collective-permute-start.1 = (bf16[1536,128]{1,0:T(8,128)(2,1)S(1)}, bf16[1536,128]{1,0:T(8,128)(2,1)S(1)}, u32[]{:S(2)}, u32[]{:S(2)}) collective-permute-start(bf16[1536,128]{1,0:T(8,128)(2,1)S(1)} %bitcast.18), channel_id=1, source_target_pairs={{0,1},{1,0},{2,3},{3,2},{4,5},{5,4},{6,7},{7,6},{8,9},{9,8},{10,11... | collective-permute-start | bytes 1179656 | tf_op jit(solution)/shard_map/ppermute | solution.py:365

commit v7 on v6

--- a/solution.py
+++ b/solution.py
@@ -11,7 +11,7 @@
 AXES = ("z", "y", "x", "c")
 CHIPS = ("z", "y", "x")
 VMEM = pl.BlockSpec(memory_space=pltpu.VMEM)
-ANY = pl.BlockSpec(memory_space=pl.ANY)
+HBM = pl.BlockSpec(memory_space=pltpu.HBM)
 SMEM = pl.BlockSpec(memory_space=pltpu.SMEM)
 MIB = 1024 * 1024
 CAP = 2
@@ -91,8 +91,8 @@
     return pl.pallas_call(
         kernel,
         out_shape=jax.ShapeDtypeStruct((dev_count, CAP * 2 * block + TAG_ROWS, LANES), jnp.bfloat16),
-        in_specs=[ANY] * 6,
-        out_specs=ANY,
+        in_specs=[HBM] * 6,
+        out_specs=HBM,
         scratch_shapes=[
             numbers,
             numbers,
@@ -178,26 +178,19 @@
     return jnp.concatenate([held[sender, pl.ds(top, block)], held[sender, pl.ds(top + block, block)]], axis=1)
 
 
-def walk_groups(plan_ref, copy, use):
+def walk_groups(first, end, use):
     def single(g, carry):
         use(g)
         return carry
 
-    def batch(i, first):
-        copy(i).wait()
-        end = plan_ref[3 + i, 0]
-        middle = first + (end - first) // 2 * 2
-
-        def two(j, carry):
-            use(first + 2 * j)
-            use(first + 2 * j + 1)
-            return carry
-
-        lax.fori_loop(0, (end - first) // 2, two, 0)
-        lax.fori_loop(middle, end, single, 0)
-        return end
-
-    lax.fori_loop(0, BATCHES, batch, 0)
+    def two(j, carry):
+        use(first + 2 * j)
+        use(first + 2 * j + 1)
+        return carry
+
+    pairs = (end - first) // 2
+    lax.fori_loop(0, pairs, two, 0)
+    lax.fori_loop(first + 2 * pairs, end, single, 0)
 
 
 def weight_kernel(
@@ -210,12 +203,11 @@
     tag_copy = pltpu.make_async_copy(arrived_ref.at[:, pl.ds(held.shape[1], TAG_ROWS)], tags, tag_sem)
     feat_copy = pltpu.make_async_copy(feat_any, feat, feat_sem)
     grad_copy = pltpu.make_async_copy(grad_any, grad, grad_sem)
+    copy = arrivals(arrived_ref, held, sems)
     tag_copy.start()
     feat_copy.start()
     grad_copy.start()
-    copy = arrivals(arrived_ref, held, sems)
-    for i in range(BATCHES):
-        copy(i).start()
+    copy(0).start()
     acc[...] = jnp.zeros_like(acc)
     turned[blocks] = jnp.zeros(turned.shape[1:], turned.dtype)
     tag_copy.wait()
@@ -223,6 +215,8 @@
     plan_copy = pltpu.make_async_copy(plan_ref, plan, tag_sem)
     plan_copy.start()
     feat_copy.wait()
+    for i in range(1, BATCHES):
+        copy(i).start()
 
     def turn(b, carry):
         for k in range(4):
@@ -246,7 +240,13 @@
         right = jnp.concatenate([take(held, plan[0, g * GROUP + k], block) for k in range(GROUP)], axis=0)
         acc[1 + plan[2, g * GROUP]] += jnp.dot(left, right, preferred_element_type=jnp.float32)
 
-    walk_groups(plan, copy, use)
+    def batch(i, first):
+        copy(i).wait()
+        end = plan[3 + i, 0]
+        walk_groups(first, end, use)
+        return end
+
+    lax.fori_loop(0, BATCHES, batch, 0)
 
     def split(first, second):
         for ref, lanes in ((first, pl.ds(0, half)), (second, pl.ds(half, half))):
@@ -262,33 +262,74 @@
         split(other_ref, own_ref)
 
 
-def feat_kernel(plan_ref, arrived_ref, grad_any, root_ref, weight_ref, out_ref, held, grad, acc, sems, grad_sem):
-    blocks, block, width = out_ref.shape
-    copy = arrivals(arrived_ref, held, sems)
-    grad_copy = pltpu.make_async_copy(grad_any, grad, grad_sem)
-    grad_copy.start()
-    for i in range(BATCHES):
-        copy(i).start()
+def feat_kernel(batch, plan_ref, arrived_ref, base_any, root_ref, weight_ref, out_any, held, acc, sem, base_sem, *grad):
+    blocks, block, width = out_any.shape
+    senders = held.shape[0]
+    part = pl.ds(batch * senders, senders)
+    copy = pltpu.make_async_copy(arrived_ref.at[part, pl.ds(0, held.shape[1])], held, sem)
+    inside = acc.at[pl.ds(0, blocks)]
+    base_copy = pltpu.make_async_copy(base_any, inside if batch else grad[0], base_sem)
+    base_copy.start()
+    copy.start()
     acc[blocks] = jnp.zeros(acc.shape[1:], jnp.float32)
     across = (((1,), (1,)), ((), ()))
-    grad_copy.wait()
+    base_copy.wait()
 
     def base(g, carry):
-        rows = grad[pl.ds(g * GROUP, GROUP)].reshape(GROUP * block, width)
+        rows = grad[0][pl.ds(g * GROUP, GROUP)].reshape(GROUP * block, width)
         part = lax.dot_general(rows, root_ref[...], across, preferred_element_type=jnp.float32)
         acc[pl.ds(g * GROUP, GROUP)] = part.reshape(GROUP, block, width)
         return carry
 
-    lax.fori_loop(0, blocks // GROUP, base, 0)
+    if batch == 0:
+        lax.fori_loop(0, blocks // GROUP, base, 0)
+    copy.wait()
 
     def use(g):
-        rows = jnp.concatenate([take(held, plan_ref[0, g * GROUP + k], block) for k in range(GROUP)], axis=0)
+        rows = jnp.concatenate(
+            [take(held, plan_ref[0, g * GROUP + k] - batch * senders * CAP, block) for k in range(GROUP)], axis=0
+        )
         part = lax.dot_general(rows, weight_ref[plan_ref[2, g * GROUP]], across, preferred_element_type=jnp.float32)
         for k in range(GROUP):
             acc[plan_ref[1, g * GROUP + k]] += part[k * block : (k + 1) * block]
 
-    walk_groups(plan_ref, copy, use)
-    out_ref[...] = acc[pl.ds(0, blocks)].astype(jnp.bfloat16)
+    walk_groups(plan_ref[2 + batch, 0] if batch else 0, plan_ref[3 + batch, 0], use)
+    if batch + 1 < BATCHES:
+        out_copy = pltpu.make_async_copy(inside, out_any, base_sem)
+        out_copy.start()
+        out_copy.wait()
+    else:
+        out_any[...] = acc[pl.ds(0, blocks)].astype(jnp.bfloat16)
+
+
+def add_batch(batch, plan, arrived, base, root_weight, rel_weight):
+    blocks, block, width = base.shape
+    senders = arrived.shape[0] // BATCHES
+    dma = pltpu.SemaphoreType.DMA
+    last = batch + 1 == BATCHES
+
+    def kernel(*refs):
+        feat_kernel(batch, *refs)
+
+    return pl.pallas_call(
+        kernel,
+        out_shape=jax.ShapeDtypeStruct(base.shape, jnp.bfloat16 if last else jnp.float32),
+        in_specs=[SMEM, HBM, HBM, VMEM, VMEM],
+        out_specs=VMEM if last else HBM,
+        scratch_shapes=[
+            pltpu.VMEM((senders, CAP * 2 * block, LANES), jnp.bfloat16),
+            pltpu.VMEM((blocks + 1, block, width), jnp.float32),
+            dma,
+            dma,
+        ]
+        + ([] if batch else [pltpu.VMEM(base.shape, base.dtype)]),
+        compiler_params=pltpu.CompilerParams(vmem_limit_bytes=56 * MIB),
+        cost_estimate=pl.CostEstimate(
+            flops=senders * CAP * block * width * width * 2,
+            bytes_accessed=senders * CAP * block * width * 2,
+            transcendentals=0,
+        ),
+    )(plan, arrived, base, root_weight, rel_weight)
 
 
 def shards(features, out_grad, rel_weight, root_weight, tiles, tile_dest, tile_peer, tile_source, tile_rel):
@@ -319,7 +360,7 @@
     own, other, plan = pl.pallas_call(
         weight_kernel,
         out_shape=(half, half, plan_type),
-        in_specs=[ANY] * 3 + [SMEM],
+        in_specs=[HBM] * 3 + [SMEM],
         out_specs=(VMEM, VMEM, VMEM),
         scratch_shapes=[
             room,
@@ -334,34 +375,21 @@
             dma,
             dma,
         ],
-        compiler_params=pltpu.CompilerParams(vmem_limit_bytes=57 * MIB),
+        compiler_params=pltpu.CompilerParams(vmem_limit_bytes=36 * MIB),
         cost_estimate=cost,
     )(arrived, features.reshape(blocks, block, width), grad_blocks, core)
 
     swap = [(0, 1), (1, 0)]
     own = own + lax.ppermute(other, "c", swap)
     own, plan = lax.optimization_barrier((own, plan))
-    grad_feat = pl.pallas_call(
-        feat_kernel,
-        out_shape=jax.ShapeDtypeStruct((blocks, block, width), jnp.bfloat16),
-        in_specs=[SMEM, ANY, ANY, VMEM, VMEM],
-        out_specs=VMEM,
-        scratch_shapes=[
-            room,
-            local,
-            pltpu.VMEM((blocks + 1, block, width), jnp.float32),
-            dma((BATCHES,)),
-            dma,
-        ],
-        compiler_params=pltpu.CompilerParams(vmem_limit_bytes=57 * MIB),
-        cost_estimate=cost,
-    )(plan, arrived, grad_blocks, root_weight, rel_weight)
-
+    partial = add_batch(0, plan, arrived, grad_blocks, root_weight, rel_weight)
     shape = (chips, half_rows // chips, width // 2)
     spread = lax.all_to_all(own.reshape(shape), CHIPS, 0, 0, tiled=True)
-    spread, grad_feat = lax.optimization_barrier((spread, grad_feat))
+    spread, partial, plan = lax.optimization_barrier((spread, partial, plan))
     share = (spread.sum(axis=0) * scale).astype(jnp.bfloat16)
     own = lax.all_to_all(jnp.broadcast_to(share[None], shape), CHIPS, 0, 0, tiled=True).reshape(half.shape)
+    grad_feat = add_batch(1, plan, arrived, partial, root_weight, rel_weight)
+    own, grad_feat = lax.optimization_barrier((own, grad_feat))
     other = lax.ppermute(own, "c", swap)
     core = core[0]
     left = jnp.where(core == 0, own, other).astype(jnp.float32)

time: 284 us -> 275 us (0.968)
  blocking collectives: 228 us -> 205 us
  starting transfers between devices: 12.9 us -> 19.2 us
  waiting for transfers between devices: 5.01 us -> 9.47 us
    all_to_all x1 -> x0, blocking collectives: 22.8 us -> none  [shards(): lax.all_to_all(jnp.broadcast_to(share[None], shape), CHIPS, 0, 0, tiled=T...]
    all_to_all x0 -> x1, starting transfers between devices: none -> 7.15 us  [shards(): lax.all_to_all(jnp.broadcast_to(share[None], shape), CHIPS, 0, 0, tiled=T...]
    pallas_call x1 -> x2, Pallas kernels: 13.6 us -> 19.9 us  [add_batch(): pl.pallas_call(kernel, out_shape=jax.ShapeDtypeStruct(base.shape, jnp.bfl...]
    all_to_all x1, waiting for transfers between devices: 1.54 us -> 5.31 us  [shards(): spread = lax.all_to_all(own.reshape(shape), CHIPS, 0, 0, tiled=True)]
    pallas_call x1, Pallas kernels: 13.3 us -> 9.62 us  [shards(): pl.pallas_call(weight_kernel, out_shape=(half, half, plan_type), in_specs...]
  transfers between devices with their start and end apart: 3 -> 4, of which waited for: 3 -> 4; matrix products, arithmetic and copies ran while one was open for 0% -> 0% of each run, Pallas kernels for 5% -> 7%
where the time goes in v7:
time: 275 us; the launch traced here: 274 us
  blocking collectives  205 us (75%)
  Pallas kernels  36.2 us (13%)
  starting transfers between devices  19.2 us (7%)
  waiting for transfers between devices  9.47 us (3%)
    all_to_all x1, blocking collectives, shards(): lax.all_to_all(outgoing, AXES, split_axis=0, concat_axis=0, tiled=True)  205 us
    pallas_call x2, Pallas kernels, add_batch(): pl.pallas_call(kernel, out_shape=jax.ShapeDtypeStruct(base.shape, jnp.bfl...  19.9 us
    pallas_call x1, Pallas kernels, shards(): pl.pallas_call(weight_kernel, out_shape=(half, half, plan_type), in_specs...  9.62 us
    all_to_all x1, starting transfers between devices, shards(): spread = lax.all_to_all(own.reshape(shape), CHIPS, 0, 0, tiled=True)  9.46 us
    all_to_all x1, starting transfers between devices, shards(): lax.all_to_all(jnp.broadcast_to(share[None], shape), CHIPS, 0, 0, tiled=T...  7.15 us
    pallas_call x1, Pallas kernels, make_messages(): pl.pallas_call(kernel, out_shape=jax.ShapeDtypeStruct((dev_count, CAP * 2...  6.6 us
  transfers between devices with their start and end apart: 4, of which 4 were waited for; matrix products, arithmetic and copies ran while one was open for 0% of the time, Pallas kernels for 7%

profile of v7, /device:TPU:1, one launch (start us, length us, event | category | flops | bytes accessed | tf_op | source)
XLA Modules:
  0.0 273.9 jit_solution(14424900386280354944)
XLA Ops:
  0.6 6.6 %shard_map.104 = bf16[128,528,128]{2,1,0:T(8,128)(2,1)} custom-call(s32[128]{0:T(128)} %refs_0_.1, s32[128]{0:T(128)} %bitcast.18, s32[128]{0:T(128)} %refs_2_.1, s32[128]{0:T(128)} %refs_3_.3, bf16[128,128,128]{2,1,0:T(8,128)(2,1)} %refs_4_.3, bf16[32,128,256]{2,1,0:T(8,128)(2,1)} %bitcast.10), custom_call_target="tpu_custom_call" | custom-call | flops 1073741824 | bytes 12582912 | tf_op jit(solution)/shard_map/pallas_call | solution.py:91
  7.2 0.0 copy-start
  7.3 0.0 copy-start.1
  7.3 205.1 %all_to_all.15.arrived_ref.refs_1_ = bf16[128,528,128]{2,1,0:T(8,128)(2,1)} all-to-all(bf16[128,528,128]{2,1,0:T(8,128)(2,1)} %shard_map.104), channel_id=1, replica_groups=mesh['z'=4,'y'=4,'x'=4,'c'=2] {'z','y','x','c'}, dimensions={0} | all-to-all | bytes 34603008 | tf_op jit(solution)/shard_map/all_to_all | solution.py:349
  212.3 0.0 copy-done
  212.3 0.0 copy-done.1
  212.3 9.6 %shard_map.105 = (f32[1536,128]{1,0:T(8,128)S(1)}, f32[1536,128]{1,0:T(8,128)S(1)}, s32[8,384]{1,0:T(8,128)S(1)}) custom-call(bf16[128,528,128]{2,1,0:T(8,128)(2,1)} %all_to_all.15.arrived_ref.refs_1_, bf16[32,128,256]{2,1,0:T(8,128)(2,1)S(1)} %bitcast.13, bf16[32,128,256]{2,1,0:T(8,128)(2,1)S(1)} %bitcast.12, s32[1]{0:T(128)} %bitcast.2.core_ref), custom_call_target="tpu_custom_call" | custom-call | flops 2147483648 | bytes 16777216 | tf_op jit(solution)/shard_map/pallas_call | solution.py:360
  222.0 0.0 copy-start.2
  222.0 0.6 collective-permute-start
  222.6 1.9 collective-permute-done
  224.5 1.0 add.3
  225.5 0.0 copy-done.2
  225.5 9.5 %all-to-all-start.1 = ((f32[64,24,128]{2,1,0:T(8,128)}), f32[64,24,128]{2,1,0:T(8,128)S(1)}, u32[]{:S(2)}, u32[]{:S(2)}) async-start(f32[64,24,128]{2,1,0:T(8,128)} %bitcast.4), calls=%async_computation.1 | async-start | bytes 1572864 | tf_op jit(solution)/shard_map/all_to_all | solution.py:387
  235.0 9.9 %shard_map.106.refs_2_ = f32[32,128,256]{2,1,0:T(8,128)} custom-call(s32[8,384]{1,0:T(8,128)} %copy-done.2, bf16[128,528,128]{2,1,0:T(8,128)(2,1)} %all_to_all.15.arrived_ref.refs_1_, bf16[32,128,256]{2,1,0:T(8,128)(2,1)} %bitcast.11, bf16[256,256]{1,0:T(8,128)(2,1)} %refs_3_.5, bf16[5,256,256]{2,1,0:T(8,128)(2,1)} %refs_4_.5), custom_call_target="tpu_custom_call" | custom-call | flops 2147483648 | bytes 8388608 | tf_op jit(solution)/shard_map/pallas_call | solution.py:314
  244.8 5.3 %all-to-all-done.1 = f32[64,24,128]{2,1,0:T(8,128)S(1)} async-done(((f32[64,24,128]{2,1,0:T(8,128)}), f32[64,24,128]{2,1,0:T(8,128)S(1)}, u32[]{:S(2)}, u32[]{:S(2)}) %all-to-all-start.1) | async-done | bytes 786464 | tf_op jit(solution)/shard_map/all_to_all | solution.py:387
  250.2 0.1 reduce_sum.9
  250.3 0.8 broadcast_in_dim.10
  251.1 7.2 %all-to-all-start.2 = ((bf16[64,24,128]{2,1,0:T(8,128)(2,1)}), bf16[64,24,128]{2,1,0:T(8,128)(2,1)S(1)}, u32[]{:S(2)}, u32[]{:S(2)}) async-start(bf16[64,24,128]{2,1,0:T(8,128)(2,1)} %broadcast_in_dim.10), calls=%async_computation.2 | async-start | bytes 786432 | tf_op jit(solution)/shard_map/all_to_all | solution.py:390
  258.2 10.1 %shard_map.107 = bf16[32,128,256]{2,1,0:T(8,128)(2,1)} custom-call(s32[8,384]{1,0:T(8,128)} %copy-done.2, bf16[128,528,128]{2,1,0:T(8,128)(2,1)} %all_to_all.15.arrived_ref.refs_1_, f32[32,128,256]{2,1,0:T(8,128)} %shard_map.106.refs_2_, bf16[256,256]{1,0:T(8,128)(2,1)} %refs_3_.5, bf16[5,256,256]{2,1,0:T(8,128)(2,1)} %refs_4_.5), custom_call_target="tpu_custom_call" | custom-call | flops 2147483648 | bytes 8388608 | tf_op jit(solution)/shard_map/pallas_call | solution.py:314
  268.3 0.9 all-to-all-done.2
  269.2 2.0 collective-permute-start.1
  271.1 1.3 collective-permute-done.1
  272.5 0.1 broadcast_select_fusion.1
  272.6 0.1 pad_maximum_fusion
  272.6 1.3 convert.2
  (1 shorter events, 0.0 us)
Async XLA Ops:
  7.2 205.1 %copy-start = (bf16[4096,256]{1,0:T(8,128)(2,1)S(1)}, bf16[4096,256]{1,0:T(8,128)(2,1)}, u32[]{:S(2)}) copy-start(bf16[4096,256]{1,0:T(8,128)(2,1)} %param.10) | copy-start | bytes 6291460
  7.3 205.1 %copy-start.1 = (bf16[4096,256]{1,0:T(8,128)(2,1)S(1)}, bf16[4096,256]{1,0:T(8,128)(2,1)}, u32[]{:S(2)}) copy-start(bf16[4096,256]{1,0:T(8,128)(2,1)} %param.9) | copy-start | bytes 6291460
  222.0 3.5 %copy-start.2 = (s32[8,384]{1,0:T(8,128)}, s32[8,384]{1,0:T(8,128)S(1)}, u32[]{:S(2)}) copy-start(s32[8,384]{1,0:T(8,128)S(1)} %get-tuple-element.22.refs_0_) | copy-start | bytes 36868
  222.0 2.5 collective-permute-start
  225.5 24.7 %all-to-all-start.1 = ((f32[64,24,128]{2,1,0:T(8,128)}), f32[64,24,128]{2,1,0:T(8,128)S(1)}, u32[]{:S(2)}, u32[]{:S(2)}) async-start(f32[64,24,128]{2,1,0:T(8,128)} %bitcast.4), calls=%async_computation.1 | async-start | bytes 1572864 | tf_op jit(solution)/shard_map/all_to_all | solution.py:387
  251.1 18.1 %all-to-all-start.2 = ((bf16[64,24,128]{2,1,0:T(8,128)(2,1)}), bf16[64,24,128]{2,1,0:T(8,128)(2,1)S(1)}, u32[]{:S(2)}, u32[]{:S(2)}) async-start(bf16[64,24,128]{2,1,0:T(8,128)(2,1)} %broadcast_in_dim.10), calls=%async_computation.2 | async-start | bytes 786432 | tf_op jit(solution)/shard_map/all_to_all | solution.py:390
  269.2 3.3 %collective-permute-start.1 = (bf16[1536,128]{1,0:T(8,128)(2,1)S(1)}, bf16[1536,128]{1,0:T(8,128)(2,1)S(1)}, u32[]{:S(2)}, u32[]{:S(2)}) collective-permute-start(bf16[1536,128]{1,0:T(8,128)(2,1)S(1)} %bitcast.16), channel_id=1, source_target_pairs={{0,1},{1,0},{2,3},{3,2},{4,5},{5,4},{6,7},{7,6},{8,9},{9,8},{10,11... | collective-permute-start | bytes 1179656 | tf_op jit(solution)/shard_map/ppermute | solution.py:393

commit v8 on v7

--- a/solution.py
+++ b/solution.py
@@ -162,16 +162,6 @@
     return -(-(-(-slots // GROUP) + rel_count * BATCHES) * GROUP // LANES) * LANES
 
 
-def arrivals(arrived_ref, held, sems):
-    part = held.shape[0] // BATCHES
-
-    def copy(i):
-        rows = pl.ds(i * part, part)
-        return pltpu.make_async_copy(arrived_ref.at[rows, pl.ds(0, held.shape[1])], held.at[rows], sems.at[i])
-
-    return copy
-
-
 def take(held, message, block):
     top = pl.multiple_of((message % CAP) * (2 * block), 2 * block)
     sender = message // CAP
@@ -194,29 +184,17 @@
 
 
 def weight_kernel(
-    arrived_ref, feat_any, grad_any, core_ref, own_ref, other_ref, plan_ref,
-    held, feat, grad, turned, acc, tags, plan, sems, feat_sem, grad_sem, tag_sem,
+    arrived_ref, feat, grad, core_ref, own_ref, other_ref, plan_ref, turned, acc, plan, plan_sem
 ):
     kinds, width, _ = acc.shape
     blocks, block, _ = feat.shape
     half = width // 2
-    tag_copy = pltpu.make_async_copy(arrived_ref.at[:, pl.ds(held.shape[1], TAG_ROWS)], tags, tag_sem)
-    feat_copy = pltpu.make_async_copy(feat_any, feat, feat_sem)
-    grad_copy = pltpu.make_async_copy(grad_any, grad, grad_sem)
-    copy = arrivals(arrived_ref, held, sems)
-    tag_copy.start()
-    feat_copy.start()
-    grad_copy.start()
-    copy(0).start()
+    tags = arrived_ref[:, pl.ds(CAP * 2 * block, TAG_ROWS)].astype(jnp.float32)
+    plan_ref[...] = make_plan(jnp.max(tags, axis=1), blocks, kinds - 1)
+    plan_copy = pltpu.make_async_copy(plan_ref, plan, plan_sem)
+    plan_copy.start()
     acc[...] = jnp.zeros_like(acc)
     turned[blocks] = jnp.zeros(turned.shape[1:], turned.dtype)
-    tag_copy.wait()
-    plan_ref[...] = make_plan(jnp.max(tags[...].astype(jnp.float32), axis=1), blocks, kinds - 1)
-    plan_copy = pltpu.make_async_copy(plan_ref, plan, tag_sem)
-    plan_copy.start()
-    feat_copy.wait()
-    for i in range(1, BATCHES):
-        copy(i).start()
 
     def turn(b, carry):
         for k in range(4):
@@ -224,7 +202,6 @@
         return carry
 
     lax.fori_loop(0, blocks // 4, turn, 0)
-    grad_copy.wait()
 
     def root(g, carry):
         left = jnp.concatenate([turned[g * GROUP + k] for k in range(GROUP)], axis=1)
@@ -237,16 +214,10 @@
 
     def use(g):
         left = jnp.concatenate([turned[plan[1, g * GROUP + k]] for k in range(GROUP)], axis=1)
-        right = jnp.concatenate([take(held, plan[0, g * GROUP + k], block) for k in range(GROUP)], axis=0)
+        right = jnp.concatenate([take(arrived_ref, plan[0, g * GROUP + k], block) for k in range(GROUP)], axis=0)
         acc[1 + plan[2, g * GROUP]] += jnp.dot(left, right, preferred_element_type=jnp.float32)
 
-    def batch(i, first):
-        copy(i).wait()
-        end = plan[3 + i, 0]
-        walk_groups(first, end, use)
-        return end
-
-    lax.fori_loop(0, BATCHES, batch, 0)
+    walk_groups(0, plan[2 + BATCHES, 0], use)
 
     def split(first, second):
         for ref, lanes in ((first, pl.ds(0, half)), (second, pl.ds(half, half))):
@@ -348,8 +319,6 @@
     outgoing, core = lax.optimization_barrier((outgoing, core[None].astype(jnp.int32)))
     arrived = lax.all_to_all(outgoing, AXES, split_axis=0, concat_axis=0, tiled=True)
 
-    room = pltpu.VMEM((dev_count, CAP * 2 * block, LANES), jnp.bfloat16)
-    local = pltpu.VMEM(grad_blocks.shape, jnp.bfloat16)
     dma = pltpu.SemaphoreType.DMA
     cost = pl.CostEstimate(
         flops=slots * block * width * width, bytes_accessed=slots * block * width * 2, transcendentals=0
@@ -360,22 +329,15 @@
     own, other, plan = pl.pallas_call(
         weight_kernel,
         out_shape=(half, half, plan_type),
-        in_specs=[HBM] * 3 + [SMEM],
+        in_specs=[VMEM] * 3 + [SMEM],
         out_specs=(VMEM, VMEM, VMEM),
         scratch_shapes=[
-            room,
-            local,
-            local,
             pltpu.VMEM((blocks + 1, width, block), jnp.bfloat16),
             pltpu.VMEM((1 + rel_count, width, width), jnp.float32),
-            pltpu.VMEM((dev_count, TAG_ROWS, LANES), jnp.bfloat16),
             pltpu.SMEM(plan_type.shape, jnp.int32),
-            dma((BATCHES,)),
-            dma,
-            dma,
             dma,
         ],
-        compiler_params=pltpu.CompilerParams(vmem_limit_bytes=36 * MIB),
+        compiler_params=pltpu.CompilerParams(vmem_limit_bytes=16 * MIB),
         cost_estimate=cost,
     )(arrived, features.reshape(blocks, block, width), grad_blocks, core)
 

time: 275 us -> 273 us (level)
  Pallas kernels: 36.2 us -> 44.3 us
  starting transfers between devices: 19.2 us -> 12.6 us
  waiting for transfers between devices: 9.47 us -> 6.57 us
    pallas_call x2, Pallas kernels: 19.9 us -> 24.9 us  [add_batch(): pl.pallas_call(kernel, out_shape=jax.ShapeDtypeStruct(base.shape, jnp.bfl...]
    all_to_all x1, starting transfers between devices: 9.46 us -> 5.45 us  [shards(): spread = lax.all_to_all(own.reshape(shape), CHIPS, 0, 0, tiled=True)]
    pallas_call x1, Pallas kernels: 9.62 us -> 12.8 us  [shards(): pl.pallas_call(weight_kernel, out_shape=(half, half, plan_type), in_specs...]
  transfers between devices with their start and end apart: 4 -> 4, of which waited for: 4 -> 3; matrix products, arithmetic and copies ran while one was open for 0% -> 0% of each run, Pallas kernels for 7% -> 9%
where the time goes in v8:
time: 273 us; the launch traced here: 272 us
  blocking collectives  205 us (75%)
  Pallas kernels  44.3 us (16%)
  starting transfers between devices  12.6 us (5%)
  waiting for transfers between devices  6.57 us (2%)
    all_to_all x1, blocking collectives, shards(): lax.all_to_all(outgoing, AXES, split_axis=0, concat_axis=0, tiled=True)  205 us
    pallas_call x2, Pallas kernels, add_batch(): pl.pallas_call(kernel, out_shape=jax.ShapeDtypeStruct(base.shape, jnp.bfl...  24.9 us
    pallas_call x1, Pallas kernels, shards(): pl.pallas_call(weight_kernel, out_shape=(half, half, plan_type), in_specs...  12.8 us
    all_to_all x1, starting transfers between devices, shards(): lax.all_to_all(jnp.broadcast_to(share[None], shape), CHIPS, 0, 0, tiled=T...  6.69 us
    pallas_call x1, Pallas kernels, make_messages(): pl.pallas_call(kernel, out_shape=jax.ShapeDtypeStruct((dev_count, CAP * 2...  6.58 us
  transfers between devices with their start and end apart: 4, of which 3 were waited for; matrix products, arithmetic and copies ran while one was open for 0% of the time, Pallas kernels for 9%

profile of v8, /device:TPU:1, one launch (start us, length us, event | category | flops | bytes accessed | tf_op | source)
XLA Modules:
  0.0 272.5 jit_solution(6042662588786569925)
XLA Ops:
  0.6 6.6 %shard_map.104 = bf16[128,528,128]{2,1,0:T(8,128)(2,1)} custom-call(s32[128]{0:T(128)} %refs_0_.1, s32[128]{0:T(128)} %bitcast.18, s32[128]{0:T(128)} %refs_2_.1, s32[128]{0:T(128)} %refs_3_.3, bf16[128,128,128]{2,1,0:T(8,128)(2,1)} %refs_4_.3, bf16[32,128,256]{2,1,0:T(8,128)(2,1)} %bitcast.10), custom_call_target="tpu_custom_call" | custom-call | flops 1073741824 | bytes 12582912 | tf_op jit(solution)/shard_map/pallas_call | solution.py:91
  7.2 0.0 copy-start.1
  7.2 0.0 copy-start.2
  7.2 205.0 %all_to_all.15.arrived_ref.refs_1_ = bf16[128,528,128]{2,1,0:T(8,128)(2,1)S(1)} all-to-all(bf16[128,528,128]{2,1,0:T(8,128)(2,1)} %shard_map.104), channel_id=1, replica_groups=mesh['z'=4,'y'=4,'x'=4,'c'=2] {'z','y','x','c'}, dimensions={0} | all-to-all | bytes 34603008 | tf_op jit(solution)/shard_map/all_to_all | solution.py:320
  212.2 0.0 copy-start
  212.2 0.0 copy-done.1
  212.2 0.0 copy-done.2
  212.2 12.8 %shard_map.105 = (f32[1536,128]{1,0:T(8,128)S(1)}, f32[1536,128]{1,0:T(8,128)S(1)}, s32[8,384]{1,0:T(8,128)S(1)}) custom-call(bf16[128,528,128]{2,1,0:T(8,128)(2,1)S(1)} %all_to_all.15.arrived_ref.refs_1_, bf16[32,128,256]{2,1,0:T(8,128)(2,1)S(1)} %bitcast.13, bf16[32,128,256]{2,1,0:T(8,128)(2,1)S(1)} %bitcast.12, s32[1]{0:T(128)} %bitcast.2.core_ref), custom_call_target="tpu_custom_call" | custom-call | flops 2147483648 | bytes 16777216 | tf_op jit(solution)/shard_map/pallas_call | solution.py:329
  225.0 0.0 copy-done
  225.0 0.0 copy-start.3
  225.1 0.1 collective-permute-start
  225.1 2.3 collective-permute-done
  227.4 1.0 add.3
  228.4 0.0 copy-done.3
  228.4 5.4 %all-to-all-start.1 = ((f32[64,24,128]{2,1,0:T(8,128)}), f32[64,24,128]{2,1,0:T(8,128)S(1)}, u32[]{:S(2)}, u32[]{:S(2)}) async-start(f32[64,24,128]{2,1,0:T(8,128)} %bitcast.4), calls=%async_computation.1 | async-start | bytes 1572864 | tf_op jit(solution)/shard_map/all_to_all | solution.py:349
  233.9 12.3 %shard_map.106.refs_2_ = f32[32,128,256]{2,1,0:T(8,128)} custom-call(s32[8,384]{1,0:T(8,128)} %copy-done.3, bf16[128,528,128]{2,1,0:T(8,128)(2,1)} %copy-done, bf16[32,128,256]{2,1,0:T(8,128)(2,1)} %bitcast.11, bf16[256,256]{1,0:T(8,128)(2,1)} %refs_3_.5, bf16[5,256,256]{2,1,0:T(8,128)(2,1)} %refs_4_.5), custom_call_target="tpu_custom_call" | custom-call | flops 2147483648 | bytes 8388608 | tf_op jit(solution)/shard_map/pallas_call | solution.py:285
  246.2 2.8 %all-to-all-done.1 = f32[64,24,128]{2,1,0:T(8,128)S(1)} async-done(((f32[64,24,128]{2,1,0:T(8,128)}), f32[64,24,128]{2,1,0:T(8,128)S(1)}, u32[]{:S(2)}, u32[]{:S(2)}) %all-to-all-start.1) | async-done | bytes 786464 | tf_op jit(solution)/shard_map/all_to_all | solution.py:349
  249.0 0.1 reduce_sum.9
  249.1 0.8 broadcast_in_dim.10
  249.9 6.7 %all-to-all-start.2 = ((bf16[64,24,128]{2,1,0:T(8,128)(2,1)}), bf16[64,24,128]{2,1,0:T(8,128)(2,1)S(1)}, u32[]{:S(2)}, u32[]{:S(2)}) async-start(bf16[64,24,128]{2,1,0:T(8,128)(2,1)} %broadcast_in_dim.10), calls=%async_computation.2 | async-start | bytes 786432 | tf_op jit(solution)/shard_map/all_to_all | solution.py:352
  256.6 12.6 %shard_map.107 = bf16[32,128,256]{2,1,0:T(8,128)(2,1)} custom-call(s32[8,384]{1,0:T(8,128)} %copy-done.3, bf16[128,528,128]{2,1,0:T(8,128)(2,1)} %copy-done, f32[32,128,256]{2,1,0:T(8,128)} %shard_map.106.refs_2_, bf16[256,256]{1,0:T(8,128)(2,1)} %refs_3_.5, bf16[5,256,256]{2,1,0:T(8,128)(2,1)} %refs_4_.5), custom_call_target="tpu_custom_call" | custom-call | flops 2147483648 | bytes 8388608 | tf_op jit(solution)/shard_map/pallas_call | solution.py:285
  269.2 0.0 all-to-all-done.2
  269.2 0.3 collective-permute-start.1
  269.6 1.5 collective-permute-done.1
  271.0 0.1 broadcast_select_fusion.1
  271.1 0.1 pad_maximum_fusion
  271.2 1.3 convert.2
  (1 shorter events, 0.0 us)
Async XLA Ops:
  7.2 205.0 %copy-start.1 = (bf16[4096,256]{1,0:T(8,128)(2,1)S(1)}, bf16[4096,256]{1,0:T(8,128)(2,1)}, u32[]{:S(2)}) copy-start(bf16[4096,256]{1,0:T(8,128)(2,1)} %param.10) | copy-start | bytes 6291460
  7.2 205.0 %copy-start.2 = (bf16[4096,256]{1,0:T(8,128)(2,1)S(1)}, bf16[4096,256]{1,0:T(8,128)(2,1)}, u32[]{:S(2)}) copy-start(bf16[4096,256]{1,0:T(8,128)(2,1)} %param.9) | copy-start | bytes 6291460
  212.2 12.8 %copy-start = (bf16[128,528,128]{2,1,0:T(8,128)(2,1)}, bf16[128,528,128]{2,1,0:T(8,128)(2,1)S(1)}, u32[]{:S(2)}) copy-start(bf16[128,528,128]{2,1,0:T(8,128)(2,1)S(1)} %all_to_all.15.arrived_ref.refs_1_) | copy-start | bytes 51904516
  225.0 3.4 %copy-start.3 = (s32[8,384]{1,0:T(8,128)}, s32[8,384]{1,0:T(8,128)S(1)}, u32[]{:S(2)}) copy-start(s32[8,384]{1,0:T(8,128)S(1)} %get-tuple-element.22.refs_0_) | copy-start | bytes 36868
  225.1 2.4 collective-permute-start
  228.4 20.6 %all-to-all-start.1 = ((f32[64,24,128]{2,1,0:T(8,128)}), f32[64,24,128]{2,1,0:T(8,128)S(1)}, u32[]{:S(2)}, u32[]{:S(2)}) async-start(f32[64,24,128]{2,1,0:T(8,128)} %bitcast.4), calls=%async_computation.1 | async-start | bytes 1572864 | tf_op jit(solution)/shard_map/all_to_all | solution.py:349
  249.9 19.3 %all-to-all-start.2 = ((bf16[64,24,128]{2,1,0:T(8,128)(2,1)}), bf16[64,24,128]{2,1,0:T(8,128)(2,1)S(1)}, u32[]{:S(2)}, u32[]{:S(2)}) async-start(bf16[64,24,128]{2,1,0:T(8,128)(2,1)} %broadcast_in_dim.10), calls=%async_computation.2 | async-start | bytes 786432 | tf_op jit(solution)/shard_map/all_to_all | solution.py:352
  269.2 1.8 collective-permute-start.1

commit v9 on v8

--- a/solution.py
+++ b/solution.py
@@ -1,3 +1,4 @@
+import functools
 import math
 
 import jax
@@ -163,8 +164,8 @@
 
 
 def take(held, message, block):
-    top = pl.multiple_of((message % CAP) * (2 * block), 2 * block)
-    sender = message // CAP
+    top = pl.multiple_of(lax.shift_left(message & (CAP - 1), (2 * block).bit_length() - 1), 2 * block)
+    sender = lax.shift_right_logical(message, CAP.bit_length() - 1)
     return jnp.concatenate([held[sender, pl.ds(top, block)], held[sender, pl.ds(top + block, block)]], axis=1)
 
 
@@ -178,7 +179,7 @@
         use(first + 2 * j + 1)
         return carry
 
-    pairs = (end - first) // 2
+    pairs = lax.shift_right_logical(end - first, 1)
     lax.fori_loop(0, pairs, two, 0)
     lax.fori_loop(first + 2 * pairs, end, single, 0)
 
@@ -301,6 +302,12 @@
             transcendentals=0,
         ),
     )(plan, arrived, base, root_weight, rel_weight)
+
+
+def share_kernel(scale, spread_ref, share_ref):
+    share = (jnp.sum(spread_ref[...], axis=0) * scale).astype(jnp.bfloat16)
+    for i in range(share_ref.shape[0]):
+        share_ref[i] = share
 
 
 def shards(features, out_grad, rel_weight, root_weight, tiles, tile_dest, tile_peer, tile_source, tile_rel):
@@ -348,8 +355,14 @@
     shape = (chips, half_rows // chips, width // 2)
     spread = lax.all_to_all(own.reshape(shape), CHIPS, 0, 0, tiled=True)
     spread, partial, plan = lax.optimization_barrier((spread, partial, plan))
-    share = (spread.sum(axis=0) * scale).astype(jnp.bfloat16)
-    own = lax.all_to_all(jnp.broadcast_to(share[None], shape), CHIPS, 0, 0, tiled=True).reshape(half.shape)
+    share = pl.pallas_call(
+        functools.partial(share_kernel, scale),
+        out_shape=jax.ShapeDtypeStruct(shape, jnp.bfloat16),
+        in_specs=[VMEM],
+        out_specs=VMEM,
+        compiler_params=pltpu.CompilerParams(vmem_limit_bytes=8 * MIB),
+    )(spread)
+    own = lax.all_to_all(share, CHIPS, 0, 0, tiled=True).reshape(half.shape)
     grad_feat = add_batch(1, plan, arrived, partial, root_weight, rel_weight)
     own, grad_feat = lax.optimization_barrier((own, grad_feat))
     other = lax.ppermute(own, "c", swap)

time: 273 us -> 273 us (level)
  Pallas kernels: 44.3 us -> 37.4 us
  waiting for transfers between devices: 6.57 us -> 10.1 us
  starting transfers between devices: 12.6 us -> 16.1 us
    pallas_call x2, Pallas kernels: 24.9 us -> 20.7 us  [add_batch(): pl.pallas_call(kernel, out_shape=jax.ShapeDtypeStruct(base.shape, jnp.bfl...]
    pallas_call x1, Pallas kernels: 12.8 us -> 9.27 us  [shards(): pl.pallas_call(weight_kernel, out_shape=(half, half, plan_type), in_specs...]
    all_to_all x1, starting transfers between devices: 5.45 us -> 8.52 us  [shards(): spread = lax.all_to_all(own.reshape(shape), CHIPS, 0, 0, tiled=True)]
  transfers between devices with their start and end apart: 4 -> 4, of which waited for: 3 -> 4; matrix products, arithmetic and copies ran while one was open for 0% -> 0% of each run, Pallas kernels for 9% -> 8%
where the time goes in v9:
time: 273 us; the launch traced here: 272 us
  blocking collectives  205 us (75%)
  Pallas kernels  37.4 us (14%)
  starting transfers between devices  16.1 us (6%)
  waiting for transfers between devices  10.1 us (4%)
    all_to_all x1, blocking collectives, shards(): lax.all_to_all(outgoing, AXES, split_axis=0, concat_axis=0, tiled=True)  205 us
    pallas_call x2, Pallas kernels, add_batch(): pl.pallas_call(kernel, out_shape=jax.ShapeDtypeStruct(base.shape, jnp.bfl...  20.7 us
    pallas_call x1, Pallas kernels, shards(): pl.pallas_call(weight_kernel, out_shape=(half, half, plan_type), in_specs...  9.27 us
    all_to_all x1, starting transfers between devices, shards(): spread = lax.all_to_all(own.reshape(shape), CHIPS, 0, 0, tiled=True)  8.52 us
    pallas_call x1, Pallas kernels, make_messages(): pl.pallas_call(kernel, out_shape=jax.ShapeDtypeStruct((dev_count, CAP * 2...  6.56 us
    all_to_all x1, starting transfers between devices, shards(): own = lax.all_to_all(share, CHIPS, 0, 0, tiled=True).reshape(half.shape)  6.26 us
  transfers between devices with their start and end apart: 4, of which 4 were waited for; matrix products, arithmetic and copies ran while one was open for 0% of the time, Pallas kernels for 8%

profile of v9, /device:TPU:1, one launch (start us, length us, event | category | flops | bytes accessed | tf_op | source)
XLA Modules:
  0.0 271.7 jit_solution(10846123021446342968)
XLA Ops:
  0.6 6.6 %shard_map.104 = bf16[128,528,128]{2,1,0:T(8,128)(2,1)} custom-call(s32[128]{0:T(128)} %refs_0_.1, s32[128]{0:T(128)} %bitcast.18, s32[128]{0:T(128)} %refs_2_.1, s32[128]{0:T(128)} %refs_3_.3, bf16[128,128,128]{2,1,0:T(8,128)(2,1)} %refs_4_.3, bf16[32,128,256]{2,1,0:T(8,128)(2,1)} %bitcast.10), custom_call_target="tpu_custom_call" | custom-call | flops 1073741824 | bytes 12582912 | tf_op jit(solution)/shard_map/pallas_call | solution.py:92
  7.2 0.0 copy-start.1
  7.2 0.0 copy-start.2
  7.2 205.0 %all_to_all.15.arrived_ref.refs_1_ = bf16[128,528,128]{2,1,0:T(8,128)(2,1)S(1)} all-to-all(bf16[128,528,128]{2,1,0:T(8,128)(2,1)} %shard_map.104), channel_id=1, replica_groups=mesh['z'=4,'y'=4,'x'=4,'c'=2] {'z','y','x','c'}, dimensions={0} | all-to-all | bytes 34603008 | tf_op jit(solution)/shard_map/all_to_all | solution.py:327
  212.2 0.0 copy-start
  212.2 0.0 copy-done.1
  212.2 0.0 copy-done.2
  212.2 9.3 %shard_map.105 = (f32[1536,128]{1,0:T(8,128)S(1)}, f32[1536,128]{1,0:T(8,128)S(1)}, s32[8,384]{1,0:T(8,128)S(1)}) custom-call(bf16[128,528,128]{2,1,0:T(8,128)(2,1)S(1)} %all_to_all.15.arrived_ref.refs_1_, bf16[32,128,256]{2,1,0:T(8,128)(2,1)S(1)} %bitcast.13, bf16[32,128,256]{2,1,0:T(8,128)(2,1)S(1)} %bitcast.12, s32[1]{0:T(128)} %bitcast.2.core_ref), custom_call_target="tpu_custom_call" | custom-call | flops 2147483648 | bytes 16777216 | tf_op jit(solution)/shard_map/pallas_call | solution.py:336
  221.5 0.0 copy-done
  221.5 0.0 copy-start.3
  221.5 0.1 collective-permute-start
  221.7 2.2 collective-permute-done
  223.9 1.0 add.3
  224.9 0.0 copy-done.3
  224.9 8.5 %all-to-all-start.1 = ((f32[64,24,128]{2,1,0:T(8,128)}), f32[64,24,128]{2,1,0:T(8,128)S(1)}, u32[]{:S(2)}, u32[]{:S(2)}) async-start(f32[64,24,128]{2,1,0:T(8,128)} %bitcast.4), calls=%async_computation.1 | async-start | bytes 1572864 | tf_op jit(solution)/shard_map/all_to_all | solution.py:356
  233.4 10.4 %shard_map.106.refs_2_ = f32[32,128,256]{2,1,0:T(8,128)} custom-call(s32[8,384]{1,0:T(8,128)} %copy-done.3, bf16[128,528,128]{2,1,0:T(8,128)(2,1)} %copy-done, bf16[32,128,256]{2,1,0:T(8,128)(2,1)} %bitcast.11, bf16[256,256]{1,0:T(8,128)(2,1)} %refs_3_.5, bf16[5,256,256]{2,1,0:T(8,128)(2,1)} %refs_4_.5), custom_call_target="tpu_custom_call" | custom-call | flops 2147483648 | bytes 8388608 | tf_op jit(solution)/shard_map/pallas_call | solution.py:286
  243.8 5.0 %all-to-all-done.1.spread_ref = f32[64,24,128]{2,1,0:T(8,128)S(1)} async-done(((f32[64,24,128]{2,1,0:T(8,128)}), f32[64,24,128]{2,1,0:T(8,128)S(1)}, u32[]{:S(2)}, u32[]{:S(2)}) %all-to-all-start.1) | async-done | bytes 786464 | tf_op jit(solution)/shard_map/all_to_all | solution.py:356
  248.9 0.9 shard_map.107
  249.7 6.3 %all-to-all-start.2 = ((bf16[64,24,128]{2,1,0:T(8,128)(2,1)}), bf16[64,24,128]{2,1,0:T(8,128)(2,1)S(1)}, u32[]{:S(2)}, u32[]{:S(2)}) async-start(bf16[64,24,128]{2,1,0:T(8,128)(2,1)} %shard_map.107), calls=%async_computation.2 | async-start | bytes 786432 | tf_op jit(solution)/shard_map/all_to_all | solution.py:365
  256.0 10.3 %shard_map.108 = bf16[32,128,256]{2,1,0:T(8,128)(2,1)} custom-call(s32[8,384]{1,0:T(8,128)} %copy-done.3, bf16[128,528,128]{2,1,0:T(8,128)(2,1)} %copy-done, f32[32,128,256]{2,1,0:T(8,128)} %shard_map.106.refs_2_, bf16[256,256]{1,0:T(8,128)(2,1)} %refs_3_.5, bf16[5,256,256]{2,1,0:T(8,128)(2,1)} %refs_4_.5), custom_call_target="tpu_custom_call" | custom-call | flops 2147483648 | bytes 8388608 | tf_op jit(solution)/shard_map/pallas_call | solution.py:286
  266.3 1.5 all-to-all-done.2
  267.8 1.1 collective-permute-start.1
  268.9 1.3 collective-permute-done.1
  270.3 0.1 broadcast_select_fusion.1
  270.3 0.1 pad_maximum_fusion
  270.4 1.3 convert.2
Async XLA Ops:
  7.2 205.0 %copy-start.1 = (bf16[4096,256]{1,0:T(8,128)(2,1)S(1)}, bf16[4096,256]{1,0:T(8,128)(2,1)}, u32[]{:S(2)}) copy-start(bf16[4096,256]{1,0:T(8,128)(2,1)} %param.10) | copy-start | bytes 6291460
  7.2 205.0 %copy-start.2 = (bf16[4096,256]{1,0:T(8,128)(2,1)S(1)}, bf16[4096,256]{1,0:T(8,128)(2,1)}, u32[]{:S(2)}) copy-start(bf16[4096,256]{1,0:T(8,128)(2,1)} %param.9) | copy-start | bytes 6291460
  212.2 9.3 %copy-start = (bf16[128,528,128]{2,1,0:T(8,128)(2,1)}, bf16[128,528,128]{2,1,0:T(8,128)(2,1)S(1)}, u32[]{:S(2)}) copy-start(bf16[128,528,128]{2,1,0:T(8,128)(2,1)S(1)} %all_to_all.15.arrived_ref.refs_1_) | copy-start | bytes 51904516
  221.5 3.4 %copy-start.3 = (s32[8,384]{1,0:T(8,128)}, s32[8,384]{1,0:T(8,128)S(1)}, u32[]{:S(2)}) copy-start(s32[8,384]{1,0:T(8,128)S(1)} %get-tuple-element.22.refs_0_) | copy-start | bytes 36868
  221.5 2.4 collective-permute-start
  224.9 24.0 %all-to-all-start.1 = ((f32[64,24,128]{2,1,0:T(8,128)}), f32[64,24,128]{2,1,0:T(8,128)S(1)}, u32[]{:S(2)}, u32[]{:S(2)}) async-start(f32[64,24,128]{2,1,0:T(8,128)} %bitcast.4), calls=%async_computation.1 | async-start | bytes 1572864 | tf_op jit(solution)/shard_map/all_to_all | solution.py:356
  249.7 18.1 %all-to-all-start.2 = ((bf16[64,24,128]{2,1,0:T(8,128)(2,1)}), bf16[64,24,128]{2,1,0:T(8,128)(2,1)S(1)}, u32[]{:S(2)}, u32[]{:S(2)}) async-start(bf16[64,24,128]{2,1,0:T(8,128)(2,1)} %shard_map.107), calls=%async_computation.2 | async-start | bytes 786432 | tf_op jit(solution)/shard_map/all_to_all | solution.py:365
  267.8 2.5 collective-permute-start.1

commit v10 on v9

--- a/solution.py
+++ b/solution.py
@@ -234,74 +234,41 @@
         split(other_ref, own_ref)
 
 
-def feat_kernel(batch, plan_ref, arrived_ref, base_any, root_ref, weight_ref, out_any, held, acc, sem, base_sem, *grad):
-    blocks, block, width = out_any.shape
-    senders = held.shape[0]
-    part = pl.ds(batch * senders, senders)
-    copy = pltpu.make_async_copy(arrived_ref.at[part, pl.ds(0, held.shape[1])], held, sem)
-    inside = acc.at[pl.ds(0, blocks)]
-    base_copy = pltpu.make_async_copy(base_any, inside if batch else grad[0], base_sem)
-    base_copy.start()
-    copy.start()
+def feat_kernel(plan_ref, arrived_ref, grad_ref, root_ref, weight_ref, out_ref, held, acc, sems):
+    blocks, block, width = out_ref.shape
+    senders = held.shape[0] // BATCHES
+
+    def copy(i):
+        part = pl.ds(i * senders, senders)
+        return pltpu.make_async_copy(arrived_ref.at[part, pl.ds(0, held.shape[1])], held.at[part], sems.at[i])
+
+    for i in range(BATCHES):
+        copy(i).start()
     acc[blocks] = jnp.zeros(acc.shape[1:], jnp.float32)
     across = (((1,), (1,)), ((), ()))
-    base_copy.wait()
 
     def base(g, carry):
-        rows = grad[0][pl.ds(g * GROUP, GROUP)].reshape(GROUP * block, width)
+        rows = grad_ref[pl.ds(g * GROUP, GROUP)].reshape(GROUP * block, width)
         part = lax.dot_general(rows, root_ref[...], across, preferred_element_type=jnp.float32)
         acc[pl.ds(g * GROUP, GROUP)] = part.reshape(GROUP, block, width)
         return carry
 
-    if batch == 0:
-        lax.fori_loop(0, blocks // GROUP, base, 0)
-    copy.wait()
+    lax.fori_loop(0, blocks // GROUP, base, 0)
 
     def use(g):
-        rows = jnp.concatenate(
-            [take(held, plan_ref[0, g * GROUP + k] - batch * senders * CAP, block) for k in range(GROUP)], axis=0
-        )
+        rows = jnp.concatenate([take(held, plan_ref[0, g * GROUP + k], block) for k in range(GROUP)], axis=0)
         part = lax.dot_general(rows, weight_ref[plan_ref[2, g * GROUP]], across, preferred_element_type=jnp.float32)
         for k in range(GROUP):
             acc[plan_ref[1, g * GROUP + k]] += part[k * block : (k + 1) * block]
 
-    walk_groups(plan_ref[2 + batch, 0] if batch else 0, plan_ref[3 + batch, 0], use)
-    if batch + 1 < BATCHES:
-        out_copy = pltpu.make_async_copy(inside, out_any, base_sem)
-        out_copy.start()
-        out_copy.wait()
-    else:
-        out_any[...] = acc[pl.ds(0, blocks)].astype(jnp.bfloat16)
-
-
-def add_batch(batch, plan, arrived, base, root_weight, rel_weight):
-    blocks, block, width = base.shape
-    senders = arrived.shape[0] // BATCHES
-    dma = pltpu.SemaphoreType.DMA
-    last = batch + 1 == BATCHES
-
-    def kernel(*refs):
-        feat_kernel(batch, *refs)
-
-    return pl.pallas_call(
-        kernel,
-        out_shape=jax.ShapeDtypeStruct(base.shape, jnp.bfloat16 if last else jnp.float32),
-        in_specs=[SMEM, HBM, HBM, VMEM, VMEM],
-        out_specs=VMEM if last else HBM,
-        scratch_shapes=[
-            pltpu.VMEM((senders, CAP * 2 * block, LANES), jnp.bfloat16),
-            pltpu.VMEM((blocks + 1, block, width), jnp.float32),
-            dma,
-            dma,
-        ]
-        + ([] if batch else [pltpu.VMEM(base.shape, base.dtype)]),
-        compiler_params=pltpu.CompilerParams(vmem_limit_bytes=56 * MIB),
-        cost_estimate=pl.CostEstimate(
-            flops=senders * CAP * block * width * width * 2,
-            bytes_accessed=senders * CAP * block * width * 2,
-            transcendentals=0,
-        ),
-    )(plan, arrived, base, root_weight, rel_weight)
+    def batch(i, first):
+        copy(i).wait()
+        end = plan_ref[3 + i, 0]
+        walk_groups(first, end, use)
+        return end
+
+    lax.fori_loop(0, BATCHES, batch, 0)
+    out_ref[...] = acc[pl.ds(0, blocks)].astype(jnp.bfloat16)
 
 
 def share_kernel(scale, spread_ref, share_ref):
@@ -351,10 +318,22 @@
     swap = [(0, 1), (1, 0)]
     own = own + lax.ppermute(other, "c", swap)
     own, plan = lax.optimization_barrier((own, plan))
-    partial = add_batch(0, plan, arrived, grad_blocks, root_weight, rel_weight)
+    grad_feat = pl.pallas_call(
+        feat_kernel,
+        out_shape=jax.ShapeDtypeStruct(grad_blocks.shape, jnp.bfloat16),
+        in_specs=[SMEM, HBM, VMEM, VMEM, VMEM],
+        out_specs=VMEM,
+        scratch_shapes=[
+            pltpu.VMEM((dev_count, CAP * 2 * block, LANES), jnp.bfloat16),
+            pltpu.VMEM((blocks + 1, block, width), jnp.float32),
+            dma((BATCHES,)),
+        ],
+        compiler_params=pltpu.CompilerParams(vmem_limit_bytes=44 * MIB),
+        cost_estimate=cost,
+    )(plan, arrived, grad_blocks, root_weight, rel_weight)
     shape = (chips, half_rows // chips, width // 2)
     spread = lax.all_to_all(own.reshape(shape), CHIPS, 0, 0, tiled=True)
-    spread, partial, plan = lax.optimization_barrier((spread, partial, plan))
+    spread, grad_feat = lax.optimization_barrier((spread, grad_feat))
     share = pl.pallas_call(
         functools.partial(share_kernel, scale),
         out_shape=jax.ShapeDtypeStruct(shape, jnp.bfloat16),
@@ -363,8 +342,6 @@
         compiler_params=pltpu.CompilerParams(vmem_limit_bytes=8 * MIB),
     )(spread)
     own = lax.all_to_all(share, CHIPS, 0, 0, tiled=True).reshape(half.shape)
-    grad_feat = add_batch(1, plan, arrived, partial, root_weight, rel_weight)
-    own, grad_feat = lax.optimization_barrier((own, grad_feat))
     other = lax.ppermute(own, "c", swap)
     core = core[0]
     left = jnp.where(core == 0, own, other).astype(jnp.float32)

time: 273 us -> 276 us (1.011)
  blocking collectives: 205 us -> 227 us
  Pallas kernels: 37.4 us -> 26.2 us
  starting transfers between devices: 16.1 us -> 12.4 us
  waiting for transfers between devices: 10.1 us -> 6.43 us
    all_to_all x0 -> x1, blocking collectives: none -> 21.7 us  [shards(): own = lax.all_to_all(share, CHIPS, 0, 0, tiled=True).reshape(half.shape)]
    pallas_call x2 -> x1, Pallas kernels: 20.7 us -> 11.1 us  [shards(): pl.pallas_call(feat_kernel, out_shape=jax.ShapeDtypeStruct(grad_blocks.sh...]
    all_to_all x1 -> x0, starting transfers between devices: 6.26 us -> none  [shards(): own = lax.all_to_all(share, CHIPS, 0, 0, tiled=True).reshape(half.shape)]
  transfers between devices with their start and end apart: 4 -> 3, of which waited for: 4 -> 3; matrix products, arithmetic and copies ran while one was open for 0% -> 0% of each run, Pallas kernels for 8% -> 4%
where the time goes in v10:
time: 276 us
  blocking collectives  227 us (82%)
  Pallas kernels  26.2 us (9%)
  starting transfers between devices  12.4 us (4%)
  waiting for transfers between devices  6.43 us (2%)
    all_to_all x1, blocking collectives, shards(): lax.all_to_all(outgoing, AXES, split_axis=0, concat_axis=0, tiled=True)  205 us
    all_to_all x1, blocking collectives, shards(): own = lax.all_to_all(share, CHIPS, 0, 0, tiled=True).reshape(half.shape)  21.7 us
    pallas_call x1, Pallas kernels, shards(): pl.pallas_call(feat_kernel, out_shape=jax.ShapeDtypeStruct(grad_blocks.sh...  11.1 us
    all_to_all x1, starting transfers between devices, shards(): spread = lax.all_to_all(own.reshape(shape), CHIPS, 0, 0, tiled=True)  8.72 us
    pallas_call x1, Pallas kernels, shards(): pl.pallas_call(weight_kernel, out_shape=(half, half, plan_type), in_specs...  8.47 us
    pallas_call x1, Pallas kernels, make_messages(): pl.pallas_call(kernel, out_shape=jax.ShapeDtypeStruct((dev_count, CAP * 2...  6.53 us
  transfers between devices with their start and end apart: 3, of which 3 were waited for; matrix products, arithmetic and copies ran while one was open for 0% of the time, Pallas kernels for 4%

profile of v10, /device:TPU:1, one launch (start us, length us, event | category | flops | bytes accessed | tf_op | source)
XLA Modules:
  0.0 275.9 jit_solution(9508524255730211502)
XLA Ops:
  0.6 6.5 %shard_map.104 = bf16[128,528,128]{2,1,0:T(8,128)(2,1)} custom-call(s32[128]{0:T(128)} %refs_0_.1, s32[128]{0:T(128)} %bitcast.20, s32[128]{0:T(128)} %refs_2_.1, s32[128]{0:T(128)} %refs_3_.1, bf16[128,128,128]{2,1,0:T(8,128)(2,1)} %refs_4_.1, bf16[32,128,256]{2,1,0:T(8,128)(2,1)} %bitcast.12), custom_call_target="tpu_custom_call" | custom-call | flops 1073741824 | bytes 12582912 | tf_op jit(solution)/shard_map/pallas_call | solution.py:92
  7.2 0.0 copy-start.1
  7.2 0.0 copy-start.2
  7.2 205.1 %all_to_all.15.arrived_ref = bf16[128,528,128]{2,1,0:T(8,128)(2,1)S(1)} all-to-all(bf16[128,528,128]{2,1,0:T(8,128)(2,1)} %shard_map.104), channel_id=1, replica_groups=mesh['z'=4,'y'=4,'x'=4,'c'=2] {'z','y','x','c'}, dimensions={0} | all-to-all | bytes 34603008 | tf_op jit(solution)/shard_map/all_to_all | solution.py:294
  212.3 0.0 copy-start
  212.3 0.0 copy-done.1
  212.3 0.0 copy-done.2
  212.3 8.5 %shard_map.105 = (f32[1536,128]{1,0:T(8,128)S(1)}, f32[1536,128]{1,0:T(8,128)S(1)}, s32[8,384]{1,0:T(8,128)S(1)}) custom-call(bf16[128,528,128]{2,1,0:T(8,128)(2,1)S(1)} %all_to_all.15.arrived_ref, bf16[32,128,256]{2,1,0:T(8,128)(2,1)S(1)} %bitcast.15, bf16[32,128,256]{2,1,0:T(8,128)(2,1)S(1)} %bitcast.13, s32[1]{0:T(128)} %bitcast.2.core_ref), custom_call_target="tpu_custom_call" | custom-call | flops 2147483648 | bytes 16777216 | tf_op jit(solution)/shard_map/pallas_call | solution.py:303
  220.7 0.0 copy-done
  220.8 0.0 copy-start.3
  220.8 1.3 collective-permute-start
  222.0 1.9 collective-permute-done
  223.9 1.0 add.3
  224.9 8.7 %all-to-all-start.1 = ((f32[64,24,128]{2,1,0:T(8,128)}), f32[64,24,128]{2,1,0:T(8,128)S(1)}, u32[]{:S(2)}, u32[]{:S(2)}) async-start(f32[64,24,128]{2,1,0:T(8,128)} %bitcast.16), calls=%async_computation.1 | async-start | bytes 1572864 | tf_op jit(solution)/shard_map/all_to_all | solution.py:335
  233.6 0.0 copy-done.3
  233.6 0.0 copy-start.4
  233.7 0.9 copy-done.4
  234.5 11.1 %shard_map.106 = bf16[32,128,256]{2,1,0:T(8,128)(2,1)} custom-call(s32[8,384]{1,0:T(8,128)S(1)} %get-tuple-element.17.plan_ref, bf16[128,528,128]{2,1,0:T(8,128)(2,1)} %copy-done, bf16[32,128,256]{2,1,0:T(8,128)(2,1)S(1)} %bitcast.14, bf16[256,256]{1,0:T(8,128)(2,1)S(1)} %copy-done.4, bf16[5,256,256]{2,1,0:T(8,128)(2,1)S(1)} %copy-done.3), custom_call_target="tpu_custom_call" | custom-call | flops 2147483648 | bytes 16777216 | tf_op jit(solution)/shard_map/pallas_call | solution.py:321
  245.6 3.2 %all-to-all-done.1.spread_ref = f32[64,24,128]{2,1,0:T(8,128)S(1)} async-done(((f32[64,24,128]{2,1,0:T(8,128)}), f32[64,24,128]{2,1,0:T(8,128)S(1)}, u32[]{:S(2)}, u32[]{:S(2)}) %all-to-all-start.1) | async-done | bytes 786464 | tf_op jit(solution)/shard_map/all_to_all | solution.py:335
  248.8 0.1 shard_map.107
  248.9 21.7 %all_to_all.16 = bf16[64,24,128]{2,1,0:T(8,128)(2,1)S(1)} all-to-all(bf16[64,24,128]{2,1,0:T(8,128)(2,1)S(1)} %shard_map.107), channel_id=1, replica_groups=mesh['z'=4,'y'=4,'x'=4,'c'=2] {'z','y','x'}, dimensions={0} | all-to-all | bytes 786432 | tf_op jit(solution)/shard_map/all_to_all | solution.py:344
  270.7 2.5 collective-permute-start.1
  273.1 1.3 collective-permute-done.1
  274.5 0.1 broadcast_select_fusion.1
  274.6 0.1 pad_maximum_fusion
  274.6 1.3 convert.2
Async XLA Ops:
  7.2 205.1 %copy-start.1 = (bf16[4096,256]{1,0:T(8,128)(2,1)S(1)}, bf16[4096,256]{1,0:T(8,128)(2,1)}, u32[]{:S(2)}) copy-start(bf16[4096,256]{1,0:T(8,128)(2,1)} %param.10) | copy-start | bytes 6291460
  7.2 205.1 %copy-start.2 = (bf16[4096,256]{1,0:T(8,128)(2,1)S(1)}, bf16[4096,256]{1,0:T(8,128)(2,1)}, u32[]{:S(2)}) copy-start(bf16[4096,256]{1,0:T(8,128)(2,1)} %param.9) | copy-start | bytes 6291460
  212.3 8.5 %copy-start = (bf16[128,528,128]{2,1,0:T(8,128)(2,1)}, bf16[128,528,128]{2,1,0:T(8,128)(2,1)S(1)}, u32[]{:S(2)}) copy-start(bf16[128,528,128]{2,1,0:T(8,128)(2,1)S(1)} %all_to_all.15.arrived_ref) | copy-start | bytes 51904516
  220.8 12.9 %copy-start.3 = (bf16[5,256,256]{2,1,0:T(8,128)(2,1)S(1)}, bf16[5,256,256]{2,1,0:T(8,128)(2,1)}, u32[]{:S(2)}) copy-start(bf16[5,256,256]{2,1,0:T(8,128)(2,1)} %weight_ref.1) | copy-start | bytes 1966084
  220.8 3.2 %collective-permute-start = (f32[1536,128]{1,0:T(8,128)S(1)}, f32[1536,128]{1,0:T(8,128)S(1)}, u32[]{:S(2)}, u32[]{:S(2)}) collective-permute-start(f32[1536,128]{1,0:T(8,128)S(1)} %get-tuple-element.14), channel_id=1, source_target_pairs={{0,1},{1,0},{2,3},{3,2},{4,5},{5,4},{6,7},{7,6},{8,9},{9,8},{10,11... | collective-permute-start | bytes 2359304 | tf_op jit(solution)/shard_map/ppermute | solution.py:319
  224.9 23.9 %all-to-all-start.1 = ((f32[64,24,128]{2,1,0:T(8,128)}), f32[64,24,128]{2,1,0:T(8,128)S(1)}, u32[]{:S(2)}, u32[]{:S(2)}) async-start(f32[64,24,128]{2,1,0:T(8,128)} %bitcast.16), calls=%async_computation.1 | async-start | bytes 1572864 | tf_op jit(solution)/shard_map/all_to_all | solution.py:335
  233.6 0.9 copy-start.4
  270.7 3.8 %collective-permute-start.1 = (bf16[1536,128]{1,0:T(8,128)(2,1)S(1)}, bf16[1536,128]{1,0:T(8,128)(2,1)S(1)}, u32[]{:S(2)}, u32[]{:S(2)}) collective-permute-start(bf16[1536,128]{1,0:T(8,128)(2,1)S(1)} %bitcast.19), channel_id=1, source_target_pairs={{0,1},{1,0},{2,3},{3,2},{4,5},{5,4},{6,7},{7,6},{8,9},{9,8},{10,11... | collective-permute-start | bytes 1179656 | tf_op jit(solution)/shard_map/ppermute | solution.py:345

commit v11 on v10

v11 whole, which is shorter than its diff:
```python
import functools
import math

import jax
import jax.numpy as jnp
from jax import lax
from jax.experimental import pallas as pl
from jax.experimental.pallas import tpu as pltpu
from jax.sharding import Mesh
from jax.sharding import PartitionSpec as P

AXES = ("z", "y", "x", "c")
CHIPS = ("z", "y", "x")
VMEM = pl.BlockSpec(memory_space=pltpu.VMEM)
HBM = pl.BlockSpec(memory_space=pltpu.HBM)
SMEM = pl.BlockSpec(memory_space=pltpu.SMEM)
MIB = 1024 * 1024
GROUP = 8
LANES = 128
TAG_ROWS = 16
FIELD = 16


def message_kernel(
    blocks, parts, dest_any, peer_any, rel_any, source_any, tiles_ref, grad_any, out_ref, later_ref,
    dest, peers, rels, sources, count, seconds, flag, grad, held, made, marks, tags, sems, out_sem,
):
    tile_count, block, _ = tiles_ref.shape
    part = tile_count // parts
    pairs = ((dest_any, dest), (peer_any, peers), (rel_any, rels), (source_any, sources), (grad_any, grad))
    early = [pltpu.make_async_copy(src, dst, sems.at[parts + i]) for i, (src, dst) in enumerate(pairs)]
    for copy in early:
        copy.start()

    def fetch(i):
        rows = pl.ds(i * part, part)
        return pltpu.make_async_copy(tiles_ref.at[rows], held.at[rows], sems.at[i])

    for i in range(parts):
        fetch(i).start()

    def clear(i, carry):
        count[2 * i] = 0
        count[2 * i + 1] = 0
        seconds[i] = 0
        return carry

    lax.fori_loop(0, seconds.shape[0], clear, 0)
    flag[0] = 0
    marks[...] = jnp.full(marks.shape, -1.0, jnp.float32)
    field = lax.broadcasted_iota(jnp.int32, marks.shape[1:], 1) // FIELD
    left, right = pl.ds(0, block), pl.ds(block, block)
    half = pl.ds(2 * block, block)

    def send(src, dst):
        pltpu.make_async_copy(src, dst, out_sem).start()

    def place(t, carry):
        peer = peers[t]
        rank = count[peer]
        count[peer] = rank + 1
        mark = (rels[t] * blocks + sources[t]).astype(jnp.float32)

        @pl.when(rank == 0)
        def _():
            marks[peer] = jnp.where(field == 0, mark, marks[peer])
            send(made.at[t], out_ref.at[peer, pl.ds(0, 2 * block)])

        @pl.when(rank != 0)
        def _():
            chip = lax.shift_right_logical(peer, 1)
            later = seconds[chip]
            seconds[chip] = later + 1
            core = (peer & 1).astype(jnp.float32)
            first = 2 * chip
            for side in range(2):
                old = marks[first + side]
                old = jnp.where(field == 2 + 2 * later, core, old)
                marks[first + side] = jnp.where(field == 1 + 2 * later, mark, old)

            @pl.when(later == 0)
            def _():
                send(made.at[t, left], out_ref.at[first, half])
                send(made.at[t, right], out_ref.at[first + 1, half])

            @pl.when(later != 0)
            def _():
                flag[0] = 1
                send(made.at[t, left], later_ref.at[first])
                send(made.at[t, right], later_ref.at[first + 1])

        return carry

    for copy in early:
        copy.wait()

    for i in range(parts):
        fetch(i).wait()
        for t in range(i * part, (i + 1) * part):
            message = lax.dot_general(
                held[t], grad[dest[t]], (((0,), (0,)), ((), ())), preferred_element_type=jnp.float32
            ).astype(jnp.bfloat16)
            made[t, left] = message[:, :LANES]
            made[t, right] = message[:, LANES:]
        lax.fori_loop(i * part, (i + 1) * part, place, 0)

    any_later = flag[0].astype(jnp.float32)
    all_marks = jnp.where(field[None] == 5, any_later, marks[...])
    tags[...] = jnp.concatenate([all_marks, all_marks], axis=1).astype(jnp.bfloat16)
    tag_copy = pltpu.make_async_copy(tags, out_ref.at[:, pl.ds(3 * block, TAG_ROWS)], sems.at[0])
    tag_copy.start()
    pltpu.make_async_copy(made, out_ref.at[pl.ds(0, tile_count), pl.ds(0, 2 * block)], out_sem).wait()
    tag_copy.wait()


def make_messages(tile_dest, peer_list, tile_rel, tile_source, tiles, grad_blocks, dev_count):
    tile_count, block, _ = tiles.shape
    blocks, _, width = grad_blocks.shape
    parts = 8
    numbers = pltpu.SMEM((tile_count,), jnp.int32)

    def kernel(*refs):
        message_kernel(blocks, parts, *refs)

    return pl.pallas_call(
        kernel,
        out_shape=(
            jax.ShapeDtypeStruct((dev_count, 3 * block + TAG_ROWS, LANES), jnp.bfloat16),
            jax.ShapeDtypeStruct((dev_count, block, LANES), jnp.bfloat16),
        ),
        in_specs=[HBM] * 6,
        out_specs=(HBM, HBM),
        scratch_shapes=[
            numbers,
            numbers,
            numbers,
            numbers,
            pltpu.SMEM((dev_count,), jnp.int32),
            pltpu.SMEM((dev_count // 2,), jnp.int32),
            pltpu.SMEM((1,), jnp.int32),
            pltpu.VMEM(grad_blocks.shape, jnp.bfloat16),
            pltpu.VMEM(tiles.shape, jnp.bfloat16),
            pltpu.VMEM((tile_count, 2 * block, LANES), jnp.bfloat16),
            pltpu.VMEM((dev_count, TAG_ROWS // 2, LANES), jnp.float32),
            pltpu.VMEM((dev_count, TAG_ROWS, LANES), jnp.bfloat16),
            pltpu.SemaphoreType.DMA((parts + 5,)),
            pltpu.SemaphoreType.DMA,
        ],
        compiler_params=pltpu.CompilerParams(vmem_limit_bytes=58 * MIB),
        cost_estimate=pl.CostEstimate(
            flops=2 * tile_count * block * block * width,
            bytes_accessed=tile_count * block * (block + width) * 2,
            transcendentals=0,
        ),
    )(tile_dest, peer_list, tile_rel, tile_source, tiles, grad_blocks)


def plan_places(senders, rel_count):
    return -(-(senders + (GROUP - 1) * rel_count) // LANES) * LANES


def make_plan(tag, shift, blocks, rel_count):
    senders = tag.shape[0]
    places = plan_places(senders, rel_count)
    square = (senders, senders)
    row, lane = lax.broadcasted_iota(jnp.int32, square, 0), lax.broadcasted_iota(jnp.int32, square, 1)
    below = (lane < row).astype(jnp.float32)
    ahead = (row < lane).astype(jnp.float32)
    sender = lax.broadcasted_iota(jnp.int32, (senders, 1), 0).astype(jnp.float32)
    rel = jnp.floor(tag * (1.0 / blocks))
    block_of = tag - rel * blocks + shift
    used = jnp.where((lane.astype(jnp.float32) == rel) & (tag >= 0), 1.0, 0.0)
    totals = jnp.sum(used, axis=0, keepdims=True)
    before = jnp.dot(below, used, preferred_element_type=jnp.float32)
    groups = jnp.floor((totals + (GROUP - 1)) * (1.0 / GROUP))
    first = jnp.dot(jnp.broadcast_to(groups, (8, senders)), ahead, preferred_element_type=jnp.float32)[0:1]
    place = jnp.sum(used * (before + first * GROUP), axis=1, keepdims=True)
    place = jnp.where(tag >= 0, place, -1.0)
    at = lax.broadcasted_iota(jnp.int32, (senders, places), 1)
    here = jnp.where(place == at.astype(jnp.float32), 1.0, 0.0)
    leads = jnp.where(place == (at // GROUP * GROUP).astype(jnp.float32), 1.0, 0.0)

    def gather(hits, values):
        return jnp.sum(hits * values, axis=0, keepdims=True)

    message = jnp.where(gather(here, 1.0) > 0, gather(here, sender), gather(leads, sender))
    source = gather(here, block_of - 2 * blocks) + 2 * blocks
    total = jnp.broadcast_to(jnp.sum(groups, axis=1, keepdims=True), (1, places))
    return [message, source, gather(leads, rel), total]


def make_plans(tags, core, blocks, rel_count):
    def column(i):
        return tags[:, i * FIELD : i * FIELD + 1]

    rows = make_plan(column(0), jnp.zeros_like(column(0)), blocks, rel_count)
    for i in (1, 3):
        rows += make_plan(column(i), jnp.where(column(i + 1) == core, 0.0, float(blocks)), blocks, rel_count)
    any_later = jnp.max(jnp.where(column(5) > 0, 1.0, 0.0), axis=0, keepdims=True)
    rows += [jnp.broadcast_to(any_later, rows[0].shape)] * 4
    return jnp.concatenate(rows, axis=0).astype(jnp.int32)


def walk_groups(end, use):
    def single(g, carry):
        use(g)
        return carry

    def two(j, carry):
        use(2 * j)
        use(2 * j + 1)
        return carry

    pairs = lax.shift_right_logical(end, 1)
    lax.fori_loop(0, pairs, two, 0)
    lax.fori_loop(2 * pairs, end, single, 0)


def whole(ref, sender, block):
    return jnp.concatenate([ref[sender, pl.ds(0, block)], ref[sender, pl.ds(block, block)]], axis=1)


def turn_blocks(feat, mate, turned):
    blocks = feat.shape[0]
    turned[2 * blocks] = jnp.zeros(turned.shape[1:], turned.dtype)

    def turn(b, carry):
        for k in range(4):
            turned[b * 4 + k] = feat[b * 4 + k].T
            turned[blocks + b * 4 + k] = mate[b * 4 + k].T
        return carry

    lax.fori_loop(0, blocks // 4, turn, 0)


def weight_kernel(
    arrived_ref, feat, mate, grad, core_ref, own_ref, other_ref, plan_ref, turned, acc, part, plan, plan_sem
):
    kinds, width, _ = acc.shape
    blocks, block, _ = feat.shape
    half = width // 2
    tags = jnp.max(arrived_ref[:, pl.ds(3 * block, TAG_ROWS)].astype(jnp.float32), axis=1)
    plan_ref[...] = make_plans(tags, core_ref[0].astype(jnp.float32), blocks, kinds - 1)
    plan_copy = pltpu.make_async_copy(plan_ref, plan, plan_sem)
    plan_copy.start()
    acc[...] = jnp.zeros_like(acc)
    part[...] = jnp.zeros_like(part)
    turn_blocks(feat, mate, turned)

    def root(g, carry):
        left = jnp.concatenate([turned[g * GROUP + k] for k in range(GROUP)], axis=1)
        right = grad[pl.ds(g * GROUP, GROUP)].reshape(GROUP * block, width)
        acc[0] += jnp.dot(left, right, preferred_element_type=jnp.float32)
        return carry

    lax.fori_loop(0, blocks // GROUP, root, 0)
    plan_copy.wait()

    def lefts(g, row):
        return jnp.concatenate([turned[plan[row + 1, g * GROUP + k]] for k in range(GROUP)], axis=1)

    def use(g):
        right = jnp.concatenate([whole(arrived_ref, plan[0, g * GROUP + k], block) for k in range(GROUP)], axis=0)
        acc[1 + plan[2, g * GROUP]] += jnp.dot(lefts(g, 0), right, preferred_element_type=jnp.float32)

    def use_half(g):
        right = jnp.concatenate(
            [arrived_ref[plan[4, g * GROUP + k], pl.ds(2 * block, block)] for k in range(GROUP)], axis=0
        )
        part[plan[6, g * GROUP]] += jnp.dot(lefts(g, 4), right, preferred_element_type=jnp.float32)

    walk_groups(plan[3, 0], use)
    walk_groups(plan[7, 0], use_half)

    def split(own, other):
        for r in range(kinds):
            rows = pl.ds(r * width, width)
            own_ref[rows] = acc[r, :, own] + part[r - 1] if r else acc[r, :, own]
            other_ref[rows] = acc[r, :, other]

    first, second = pl.ds(0, half), pl.ds(half, half)

    @pl.when(core_ref[0] == 0)
    def _():
        split(first, second)

    @pl.when(core_ref[0] != 0)
    def _():
        split(second, first)


def later_kernel(plan, later, feat, mate, before_ref, own_ref, turned):
    width = feat.shape[2]
    turn_blocks(feat, mate, turned)
    own_ref[...] = before_ref[...]

    def use(g):
        left = jnp.concatenate([turned[plan[9, g * GROUP + k]] for k in range(GROUP)], axis=1)
        right = jnp.concatenate([later[plan[8, g * GROUP + k]] for k in range(GROUP)], axis=0)
        rows = pl.ds(pl.multiple_of((1 + plan[10, g * GROUP]) * width, width), width)
        own_ref[rows] += jnp.dot(left, right, preferred_element_type=jnp.float32)

    walk_groups(plan[11, 0], use)


def feat_kernel(
    plan_ref, core_ref, arrived_ref, later_any, grad_ref, root_ref, weight_ref, own_any, mate_ref,
    held, halves, later, acc, sems, later_sem,
):
    blocks, block, width = mate_ref.shape
    half = width // 2
    whole_copy = pltpu.make_async_copy(arrived_ref.at[:, pl.ds(0, 2 * block)], held, sems.at[0])
    half_copy = pltpu.make_async_copy(arrived_ref.at[:, pl.ds(2 * block, block)], halves, sems.at[1])
    whole_copy.start()
    half_copy.start()
    acc[pl.ds(blocks, blocks + 1)] = jnp.zeros((blocks + 1, block, width), jnp.float32)
    across = (((1,), (1,)), ((), ()))

    def base(g, carry):
        rows = grad_ref[pl.ds(g * GROUP, GROUP)].reshape(GROUP * block, width)
        part = lax.dot_general(rows, root_ref[...], across, preferred_element_type=jnp.float32)
        acc[pl.ds(g * GROUP, GROUP)] = part.reshape(GROUP, block, width)
        return carry

    lax.fori_loop(0, blocks // GROUP, base, 0)
    whole_copy.wait()

    def add(g, row, part):
        for k in range(GROUP):
            acc[plan_ref[row + 1, g * GROUP + k]] += part[k * block : (k + 1) * block]

    def use(g):
        rows = jnp.concatenate([whole(held, plan_ref[0, g * GROUP + k], block) for k in range(GROUP)], axis=0)
        add(g, 0, lax.dot_general(rows, weight_ref[plan_ref[2, g * GROUP]], across, preferred_element_type=jnp.float32))

    def from_half(ref, row):
        lanes = pl.ds(pl.multiple_of(core_ref[0] * half, half), half)

        def use_half(g):
            rows = jnp.concatenate([ref[plan_ref[row, g * GROUP + k]] for k in range(GROUP)], axis=0)
            weight = weight_ref[plan_ref[row + 2, g * GROUP], :, lanes]
            add(g, row, lax.dot_general(rows, weight, across, preferred_element_type=jnp.float32))

        return use_half

    walk_groups(plan_ref[3, 0], use)
    half_copy.wait()
    walk_groups(plan_ref[7, 0], from_half(halves, 4))

    @pl.when(plan_ref[11, 0] > 0)
    def _():
        copy = pltpu.make_async_copy(later_any, later, later_sem)
        copy.start()
        copy.wait()
        walk_groups(plan_ref[11, 0], from_half(later, 8))

    own_copy = pltpu.make_async_copy(acc.at[pl.ds(0, blocks)], own_any, later_sem)
    own_copy.start()
    mate_ref[...] = acc[pl.ds(blocks, blocks)].astype(jnp.bfloat16)
    own_copy.wait()


def share_kernel(scale, spread_ref, share_ref):
    share = (jnp.sum(spread_ref[...], axis=0) * scale).astype(jnp.bfloat16)
    for i in range(share_ref.shape[0]):
        share_ref[i] = share


def shards(features, out_grad, rel_weight, root_weight, tiles, tile_dest, tile_peer, tile_source, tile_rel):
    dev_count = lax.axis_size(AXES)
    chips = lax.axis_size(CHIPS)
    core = lax.axis_index("c")
    block = tiles.shape[1]
    width = features.shape[1]
    rel_count = rel_weight.shape[0]
    blocks = features.shape[0] // block
    scale = 1.0 / math.sqrt(features.shape[0] * dev_count)
    swap = [(0, 1), (1, 0)]
    grad_blocks = out_grad.reshape(blocks, block, width)
    feat_blocks = features.reshape(blocks, block, width)

    mate_blocks = lax.ppermute(feat_blocks, "c", swap)
    outgoing, later = make_messages(tile_dest, tile_peer[:, 0], tile_rel, tile_source, tiles, grad_blocks, dev_count)
    outgoing, later, core, mate_blocks = lax.optimization_barrier(
        (outgoing, later, core[None].astype(jnp.int32), mate_blocks)
    )

    def exchange(array):
        return lax.all_to_all(array, AXES, split_axis=0, concat_axis=0, tiled=True)

    arrived = exchange(outgoing)

    dma = pltpu.SemaphoreType.DMA
    cost = pl.CostEstimate(
        flops=2 * dev_count * block * width * width, bytes_accessed=dev_count * block * width * 3, transcendentals=0
    )
    half_rows = (1 + rel_count) * width
    half = jax.ShapeDtypeStruct((half_rows, width // 2), jnp.float32)
    turned = pltpu.VMEM((2 * blocks + 1, width, block), jnp.bfloat16)
    plan_type = jax.ShapeDtypeStruct((16, plan_places(dev_count, rel_count)), jnp.int32)
    own, other, plan = pl.pallas_call(
        weight_kernel,
        out_shape=(half, half, plan_type),
        in_specs=[VMEM, VMEM, VMEM, VMEM, SMEM],
        out_specs=(VMEM, VMEM, VMEM),
        scratch_shapes=[
            turned,
            pltpu.VMEM((1 + rel_count, width, width), jnp.float32),
            pltpu.VMEM((rel_count, width, width // 2), jnp.float32),
            pltpu.SMEM(plan_type.shape, jnp.int32),
            dma,
        ],
        compiler_params=pltpu.CompilerParams(vmem_limit_bytes=20 * MIB),
        cost_estimate=cost,
    )(arrived, feat_blocks, mate_blocks, grad_blocks, core)

    def take_later(later, own):
        later = exchange(later)
        own = pl.pallas_call(
            later_kernel,
            out_shape=half,
            in_specs=[SMEM] + [VMEM] * 4,
            out_specs=VMEM,
            scratch_shapes=[turned],
            compiler_params=pltpu.CompilerParams(vmem_limit_bytes=24 * MIB),
        )(plan, later, feat_blocks, mate_blocks, own)
        return later, own

    later, own = lax.cond(plan[12, 0] > 0, take_later, lambda later, own: (later, own), later, own)

    own = own + lax.ppermute(other, "c", swap)
    own, plan = lax.optimization_barrier((own, plan))
    own_feat, mate_feat = pl.pallas_call(
        feat_kernel,
        out_shape=(
            jax.ShapeDtypeStruct(grad_blocks.shape, jnp.float32),
            jax.ShapeDtypeStruct(grad_blocks.shape, jnp.bfloat16),
        ),
        in_specs=[SMEM, SMEM, HBM, HBM, VMEM, VMEM, VMEM],
        out_specs=(HBM, VMEM),
        scratch_shapes=[
            pltpu.VMEM((dev_count, 2 * block, LANES), jnp.bfloat16),
            pltpu.VMEM((dev_count, block, LANES), jnp.bfloat16),
            pltpu.VMEM((dev_count, block, LANES), jnp.bfloat16),
            pltpu.VMEM((2 * blocks + 1, block, width), jnp.float32),
            dma((2,)),
            dma,
        ],
        compiler_params=pltpu.CompilerParams(vmem_limit_bytes=49 * MIB),
        cost_estimate=cost,
    )(plan, core, arrived, later, grad_blocks, root_weight, rel_weight)
    shape = (chips, half_rows // chips, width // 2)
    spread = lax.all_to_all(own.reshape(shape), CHIPS, 0, 0, tiled=True)
    spread, own_feat, mate_feat = lax.optimization_barrier((spread, own_feat, mate_feat))
    share = pl.pallas_call(
        functools.partial(share_kernel, scale),
        out_shape=jax.ShapeDtypeStruct(shape, jnp.bfloat16),
        in_specs=[VMEM],
        out_specs=VMEM,
        compiler_params=pltpu.CompilerParams(vmem_limit_bytes=8 * MIB),
    )(spread)
    own = lax.all_to_all(share, CHIPS, 0, 0, tiled=True).reshape(half.shape)
    grad_feat = (own_feat + lax.ppermute(mate_feat, "c", swap).astype(jnp.float32)).astype(jnp.bfloat16)
    own, grad_feat = lax.optimization_barrier((own, grad_feat))
    other = lax.ppermute(own, "c", swap)
    core = core[0]
    left = jnp.where(core == 0, own, other).astype(jnp.float32)
    right = jnp.where(core == 0, other, own).astype(jnp.float32)
    grad_weights = jnp.concatenate([left, right], axis=1).reshape(1 + rel_count, width, width)
    return grad_feat.reshape(features.shape), grad_weights


def solution(mesh):
    sizes = (4, 4, 4, 2)
    fine = Mesh(mesh.devices.reshape(sizes), AXES)
    return jax.shard_map(
        shards,
        mesh=fine,
        in_specs=(
            P(AXES, None),
            P(AXES, None),
            P(),
            P(),
            P(AXES, None, None),
            P(AXES),
            P(AXES, None),
            P(AXES),
            P(AXES),
        ),
        out_specs=(P(AXES, None), P()),
        check_vma=False,
    )
```

time: 276 us -> 247 us (0.89)
  blocking collectives: 227 us -> 159 us
  Pallas kernels: 26.2 us -> 47.1 us
  starting transfers between devices: 12.4 us -> 19 us
  other arithmetic: 2.41 us -> 7.96 us
  waiting for transfers between devices: 6.43 us -> 9.6 us
    all_to_all x2 -> x1, blocking collectives: 227 us -> 159 us  [exchange(): return lax.all_to_all(array, AXES, split_axis=0, concat_axis=0, tiled=True)]
    pallas_call x1, Pallas kernels: 8.47 us -> 20.5 us  [shards(): pl.pallas_call(weight_kernel, out_shape=(half, half, plan_type), in_specs...]
    all_to_all x0 -> x1, starting transfers between devices: none -> 10.3 us  [shards(): own = lax.all_to_all(share, CHIPS, 0, 0, tiled=True).reshape(half.shape)]
    pallas_call x2, Pallas kernels: 17.6 us -> 25.8 us  [the longest x1 16.5 us: shards(): pl.pallas_call(feat_kernel, out_shape=(jax.ShapeDtypeStruct(grad_blocks.s...]
    all_to_all x0 -> x1, waiting for transfers between devices: none -> 7.26 us  [shards(): own = lax.all_to_all(share, CHIPS, 0, 0, tiled=True).reshape(half.shape)]
    convert_element_type x0 -> x1, other arithmetic: none -> 4.2 us  [shards(): (own_feat + lax.ppermute(mate_feat, 'c', swap).astype(jnp.float32)).astyp...]
    all_to_all x1, starting transfers between devices: 8.72 us -> 5.26 us  [shards(): spread = lax.all_to_all(own.reshape(shape), CHIPS, 0, 0, tiled=True)]
    all_to_all x1, waiting for transfers between devices: 3.17 us -> 0.01 us  [shards(): spread = lax.all_to_all(own.reshape(shape), CHIPS, 0, 0, tiled=True)]
  transfers between devices with their start and end apart: 3 -> 6, of which waited for: 3 -> 3; matrix products, arithmetic and copies ran while one was open for 0% -> 2% of each run, Pallas kernels for 4% -> 11%
where the time goes in v11:
time: 247 us
  blocking collectives  159 us (64%)
  Pallas kernels  47.1 us (19%)
  starting transfers between devices  19 us (8%)
  waiting for transfers between devices  9.6 us (4%)
  other arithmetic  7.96 us (3%)
  local copies, waits for them, and re-layouts  2.81 us (1%)
    all_to_all x1, blocking collectives, exchange(): return lax.all_to_all(array, AXES, split_axis=0, concat_axis=0, tiled=True)  159 us
    pallas_call x1, Pallas kernels, shards(): pl.pallas_call(weight_kernel, out_shape=(half, half, plan_type), in_specs...  20.5 us
    pallas_call x1, Pallas kernels, shards(): pl.pallas_call(feat_kernel, out_shape=(jax.ShapeDtypeStruct(grad_blocks.s...  16.5 us
    all_to_all x1, starting transfers between devices, shards(): own = lax.all_to_all(share, CHIPS, 0, 0, tiled=True).reshape(half.shape)  10.3 us
    pallas_call x1, Pallas kernels, make_messages(): pl.pallas_call(kernel, out_shape=(jax.ShapeDtypeStruct((dev_count, 3 * bl...  9.24 us
    all_to_all x1, waiting for transfers between devices, shards(): own = lax.all_to_all(share, CHIPS, 0, 0, tiled=True).reshape(half.shape)  7.26 us
    all_to_all x1, starting transfers between devices, shards(): spread = lax.all_to_all(own.reshape(shape), CHIPS, 0, 0, tiled=True)  5.26 us
  transfers between devices with their start and end apart: 6, of which 3 were waited for; matrix products, arithmetic and copies ran while one was open for 2% of the time, Pallas kernels for 11%

profile of v11, /device:TPU:1, one launch (start us, length us, event | category | flops | bytes accessed | tf_op | source)
XLA Modules:
  0.0 246.7 jit_solution(1440439784017392649)
XLA Ops:
  0.6 1.5 collective-permute-start
  2.1 9.2 %shard_map.104 = (bf16[128,400,128]{2,1,0:T(8,128)(2,1)}, bf16[128,128,128]{2,1,0:T(8,128)(2,1)}) custom-call(s32[128]{0:T(128)} %refs_0_.1, s32[128]{0:T(128)} %bitcast.19, s32[128]{0:T(128)} %refs_2_.1, s32[128]{0:T(128)} %refs_3_.1, bf16[128,128,128]{2,1,0:T(8,128)(2,1)} %refs_4_.1, bf16[32,128,256]{2,1,0:T(8,128)(2,1)} %bitcast.11), custom_call_target="tpu_custom_call" | custom-call | flops 1073741824 | bytes 12582912 | tf_op jit(solution)/shard_map/pallas_call | solution.py:125
  11.4 0.0 collective-permute-done.mate
  11.4 0.0 copy-start.1
  11.4 158.8 %all_to_all.19.arrived_ref = bf16[128,400,128]{2,1,0:T(8,128)(2,1)S(1)} all-to-all(bf16[128,400,128]{2,1,0:T(8,128)(2,1)} %get-tuple-element.43), channel_id=1, replica_groups=mesh['z'=4,'y'=4,'x'=4,'c'=2] {'z','y','x','c'}, dimensions={0} | all-to-all | bytes 26214400 | tf_op jit(solution)/shard_map/all_to_all | solution.py:389
  170.2 0.0 copy-done.1
  170.2 0.0 copy-start
  170.2 20.5 %shard_map.105 = (f32[1536,128]{1,0:T(8,128)}, f32[1536,128]{1,0:T(8,128)}, s32[16,256]{1,0:T(8,128)S(1)}) custom-call(bf16[128,400,128]{2,1,0:T(8,128)(2,1)S(1)} %all_to_all.19.arrived_ref, bf16[32,128,256]{2,1,0:T(8,128)(2,1)} %bitcast.3.feat, bf16[32,128,256]{2,1,0:T(8,128)(2,1)} %collective-permute-done.mate, bf16[32,128,256]{2,1,0:T(8,128)(2,1)S(1)} %bitcast.12, ...), custom_call_target="tpu_custom_call" | custom-call | flops 2147483648 | bytes 12582912 | tf_op jit(solution)/shard_map/pallas_call | solution.py:401
  190.6 0.0 copy-done
  190.7 0.4 collective-permute-start.1
  191.1 0.6 slice.3
  192.4 0.0 copy-start.2
  192.4 1.0 collective-permute-done.1
  193.4 2.3 add.6
  195.7 5.3 %all-to-all-start.2 = ((f32[64,24,128]{2,1,0:T(8,128)}), f32[64,24,128]{2,1,0:T(8,128)S(1)}, u32[]{:S(2)}, u32[]{:S(2)}) async-start(f32[64,24,128]{2,1,0:T(8,128)} %bitcast.14), calls=%async_computation.2 | async-start | bytes 1572864 | tf_op jit(solution)/shard_map/all_to_all | solution.py:453
  201.0 0.0 copy-done.2
  201.0 0.0 copy-start.3
  201.0 0.9 copy-done.3
  201.9 16.5 %shard_map.106 = (f32[32,128,256]{2,1,0:T(8,128)}, bf16[32,128,256]{2,1,0:T(8,128)(2,1)S(1)}) custom-call(s32[16,256]{1,0:T(8,128)S(1)} %get-tuple-element.52.plan_ref, s32[1]{0:T(128)} %bitcast.2.core_ref, bf16[128,400,128]{2,1,0:T(8,128)(2,1)} %copy-done, bf16[128,128,128]{2,1,0:T(8,128)(2,1)} %get-tuple-element.53.later_any, ...), custom_call_target="tpu_custom_call" | custom-call | flops 2147483648 | bytes 12582912 | tf_op jit(solution)/shard_map/pallas_call | solution.py:433
  218.4 0.0 copy-start.4
  218.4 1.3 copy-done.4
  219.7 0.0 all-to-all-done.2.spread_ref
  219.7 0.1 collective-permute-start.2
  219.8 0.9 shard_map.107
  220.7 10.3 %all-to-all-start.3 = ((bf16[64,24,128]{2,1,0:T(8,128)(2,1)}), bf16[64,24,128]{2,1,0:T(8,128)(2,1)S(1)}, u32[]{:S(2)}, u32[]{:S(2)}) async-start(bf16[64,24,128]{2,1,0:T(8,128)(2,1)} %shard_map.107), calls=%async_computation.3 | async-start | bytes 786432 | tf_op jit(solution)/shard_map/all_to_all | solution.py:462
  230.9 0.0 collective-permute-done.2
  231.0 4.2 %add_convert_fusion = bf16[32,128,256]{2,1,0:T(8,128)(2,1)} fusion(f32[32,128,256]{2,1,0:T(8,128)} %get-tuple-element.57, bf16[32,128,256]{2,1,0:T(8,128)(2,1)S(1)} %collective-permute-done.2), kind=kLoop, calls=%fused_computation | loop fusion | flops 3145728 | bytes 8388608 | tf_op jit(solution)/shard_map/convert_element_type | solution.py:463
  235.2 7.3 %all-to-all-done.3 = bf16[64,24,128]{2,1,0:T(8,128)(2,1)S(1)} async-done(((bf16[64,24,128]{2,1,0:T(8,128)(2,1)}), bf16[64,24,128]{2,1,0:T(8,128)(2,1)S(1)}, u32[]{:S(2)}, u32[]{:S(2)}) %all-to-all-start.3) | async-done | bytes 393248 | tf_op jit(solution)/shard_map/all_to_all | solution.py:462
  242.4 1.5 collective-permute-start.3
  243.9 1.3 collective-permute-done.3
  245.2 0.1 broadcast_select_fusion.1
  245.3 0.1 pad_maximum_fusion
  245.4 1.3 convert.3
  (1 shorter events, 0.0 us)
Async XLA Ops:
  0.6 10.7 %collective-permute-start = (bf16[32,128,256]{2,1,0:T(8,128)(2,1)}, bf16[32,128,256]{2,1,0:T(8,128)(2,1)}, u32[]{:S(2)}, u32[]{:S(2)}) collective-permute-start(bf16[32,128,256]{2,1,0:T(8,128)(2,1)} %bitcast.3.feat), channel_id=1, source_target_pairs={{0,1},{1,0},{2,3},{3,2},{4,5},{5,4},{6,7},{7,6},{8,9},{9,8},{10,11... | collective-permute-start | bytes 6291464 | tf_op jit(solution)/shard_map/ppermute | solution.py:382
  11.4 158.8 %copy-start.1 = (bf16[4096,256]{1,0:T(8,128)(2,1)S(1)}, bf16[4096,256]{1,0:T(8,128)(2,1)}, u32[]{:S(2)}) copy-start(bf16[4096,256]{1,0:T(8,128)(2,1)} %param.12) | copy-start | bytes 6291460
  170.2 20.5 %copy-start = (bf16[128,400,128]{2,1,0:T(8,128)(2,1)}, bf16[128,400,128]{2,1,0:T(8,128)(2,1)S(1)}, u32[]{:S(2)}) copy-start(bf16[128,400,128]{2,1,0:T(8,128)(2,1)S(1)} %all_to_all.19.arrived_ref) | copy-start | bytes 39321604
  190.7 2.7 %collective-permute-start.1 = (f32[1536,128]{1,0:T(8,128)}, f32[1536,128]{1,0:T(8,128)}, u32[]{:S(2)}, u32[]{:S(2)}) collective-permute-start(f32[1536,128]{1,0:T(8,128)} %get-tuple-element.50), channel_id=1, source_target_pairs={{0,1},{1,0},{2,3},{3,2},{4,5},{5,4},{6,7},{7,6},{8,9},{9,8},{10,11... | collective-permute-start | bytes 2359304 | tf_op jit(solution)/shard_map/ppermute | solution.py:431
  192.4 8.6 %copy-start.2 = (bf16[5,256,256]{2,1,0:T(8,128)(2,1)S(1)}, bf16[5,256,256]{2,1,0:T(8,128)(2,1)}, u32[]{:S(2)}) copy-start(bf16[5,256,256]{2,1,0:T(8,128)(2,1)} %weight_ref.1) | copy-start | bytes 1966084
  195.7 24.0 %all-to-all-start.2 = ((f32[64,24,128]{2,1,0:T(8,128)}), f32[64,24,128]{2,1,0:T(8,128)S(1)}, u32[]{:S(2)}, u32[]{:S(2)}) async-start(f32[64,24,128]{2,1,0:T(8,128)} %bitcast.14), calls=%async_computation.2 | async-start | bytes 1572864 | tf_op jit(solution)/shard_map/all_to_all | solution.py:453
  201.0 0.9 copy-start.3
  218.4 1.3 copy-start.4
  219.7 11.2 %collective-permute-start.2 = (bf16[32,128,256]{2,1,0:T(8,128)(2,1)}, bf16[32,128,256]{2,1,0:T(8,128)(2,1)S(1)}, u32[]{:S(2)}, u32[]{:S(2)}) collective-permute-start(bf16[32,128,256]{2,1,0:T(8,128)(2,1)} %copy-done.4), channel_id=1, source_target_pairs={{0,1},{1,0},{2,3},{3,2},{4,5},{5,4},{6,7},{7,6},{8,9},{9,8},{10,11... | collective-permute-start | bytes 6291464 | tf_op jit(solution)/shard_map/ppermute | solution.py:463
  220.7 21.8 %all-to-all-start.3 = ((bf16[64,24,128]{2,1,0:T(8,128)(2,1)}), bf16[64,24,128]{2,1,0:T(8,128)(2,1)S(1)}, u32[]{:S(2)}, u32[]{:S(2)}) async-start(bf16[64,24,128]{2,1,0:T(8,128)(2,1)} %shard_map.107), calls=%async_computation.3 | async-start | bytes 786432 | tf_op jit(solution)/shard_map/all_to_all | solution.py:462
  242.4 2.8 %collective-permute-start.3 = (bf16[1536,128]{1,0:T(8,128)(2,1)S(1)}, bf16[1536,128]{1,0:T(8,128)(2,1)S(1)}, u32[]{:S(2)}, u32[]{:S(2)}) collective-permute-start(bf16[1536,128]{1,0:T(8,128)(2,1)S(1)} %bitcast.17), channel_id=1, source_target_pairs={{0,1},{1,0},{2,3},{3,2},{4,5},{5,4},{6,7},{7,6},{8,9},{9,8},{10,11... | collective-permute-start | bytes 1179656 | tf_op jit(solution)/shard_map/ppermute | solution.py:465

commit v12 on v11

--- a/solution.py
+++ b/solution.py
@@ -159,45 +159,49 @@
     return -(-(senders + (GROUP - 1) * rel_count) // LANES) * LANES
 
 
-def make_plan(tag, shift, blocks, rel_count):
-    senders = tag.shape[0]
+def make_plans(tags, core, blocks, rel_count):
+    senders = tags.shape[0]
     places = plan_places(senders, rel_count)
+    wide = 1 << (rel_count - 1).bit_length()
     square = (senders, senders)
     row, lane = lax.broadcasted_iota(jnp.int32, square, 0), lax.broadcasted_iota(jnp.int32, square, 1)
-    below = (lane < row).astype(jnp.float32)
-    ahead = (row < lane).astype(jnp.float32)
-    sender = lax.broadcasted_iota(jnp.int32, (senders, 1), 0).astype(jnp.float32)
-    rel = jnp.floor(tag * (1.0 / blocks))
-    block_of = tag - rel * blocks + shift
-    used = jnp.where((lane.astype(jnp.float32) == rel) & (tag >= 0), 1.0, 0.0)
-    totals = jnp.sum(used, axis=0, keepdims=True)
-    before = jnp.dot(below, used, preferred_element_type=jnp.float32)
-    groups = jnp.floor((totals + (GROUP - 1)) * (1.0 / GROUP))
-    first = jnp.dot(jnp.broadcast_to(groups, (8, senders)), ahead, preferred_element_type=jnp.float32)[0:1]
-    place = jnp.sum(used * (before + first * GROUP), axis=1, keepdims=True)
-    place = jnp.where(tag >= 0, place, -1.0)
+    lane_set, lane_rel = lane // wide, (lane % wide).astype(jnp.float32)
+    below = (lane < row).astype(jnp.float32).astype(jnp.bfloat16)
+    ahead = ((row < lane) & (row // wide == lane_set)).astype(jnp.float32).astype(jnp.bfloat16)
+    sender = row.astype(jnp.float32)
     at = lax.broadcasted_iota(jnp.int32, (senders, places), 1)
-    here = jnp.where(place == at.astype(jnp.float32), 1.0, 0.0)
-    leads = jnp.where(place == (at // GROUP * GROUP).astype(jnp.float32), 1.0, 0.0)
-
-    def gather(hits, values):
-        return jnp.sum(hits * values, axis=0, keepdims=True)
-
-    message = jnp.where(gather(here, 1.0) > 0, gather(here, sender), gather(leads, sender))
-    source = gather(here, block_of - 2 * blocks) + 2 * blocks
-    total = jnp.broadcast_to(jnp.sum(groups, axis=1, keepdims=True), (1, places))
-    return [message, source, gather(leads, rel), total]
-
-
-def make_plans(tags, core, blocks, rel_count):
+    at, lead = at.astype(jnp.float32), (at // GROUP * GROUP).astype(jnp.float32)
+    down = (((0,), (0,)), ((), ()))
+
     def column(i):
         return tags[:, i * FIELD : i * FIELD + 1]
 
-    rows = make_plan(column(0), jnp.zeros_like(column(0)), blocks, rel_count)
-    for i in (1, 3):
-        rows += make_plan(column(i), jnp.where(column(i + 1) == core, 0.0, float(blocks)), blocks, rel_count)
+    tag = [column(0), column(1), column(3)]
+    shift = [0.0] + [jnp.where(column(i) == core, 0.0, float(blocks)) for i in (2, 4)]
+    rel = [jnp.floor(t * (1.0 / blocks)) for t in tag]
+    used = [jnp.where((lane_set == q) & (lane_rel == r) & (t >= 0), 1.0, 0.0) for q, (t, r) in enumerate(zip(tag, rel))]
+    every = used[0] + used[1] + used[2]
+    before = jnp.dot(below, every.astype(jnp.bfloat16), preferred_element_type=jnp.float32)
+    groups = jnp.floor((jnp.sum(every, axis=0, keepdims=True) + (GROUP - 1)) * (1.0 / GROUP))
+    first = jnp.dot(
+        jnp.broadcast_to(groups, (TAG_ROWS, senders)).astype(jnp.bfloat16), ahead, preferred_element_type=jnp.float32
+    )[0:1]
+    spot = before + first * GROUP
+    rows = []
+    for q in range(3):
+        place = jnp.where(tag[q] >= 0, jnp.sum(used[q] * spot, axis=1, keepdims=True), -1.0)
+        here = jnp.where(place == at, 1.0, 0.0).astype(jnp.bfloat16)
+        leads = jnp.where(place == lead, 1.0, 0.0).astype(jnp.bfloat16)
+        source = tag[q] - rel[q] * blocks + shift[q] - 2 * blocks
+        named = jnp.where(lane == 0, 1.0, jnp.where(lane == 1, sender, jnp.where(lane == 2, source, rel[q])))
+        named = named.astype(jnp.bfloat16)
+        own = lax.dot_general(named, here, down, preferred_element_type=jnp.float32)
+        led = lax.dot_general(named, leads, down, preferred_element_type=jnp.float32)
+        total = jnp.sum(jnp.where(lane_set[0:1] == q, groups, 0.0), axis=1, keepdims=True)
+        rows += [jnp.where(own[0:1] > 0, own[1:2], led[1:2]), own[2:3] + 2 * blocks, led[3:4]]
+        rows.append(jnp.broadcast_to(total, (1, places)))
     any_later = jnp.max(jnp.where(column(5) > 0, 1.0, 0.0), axis=0, keepdims=True)
-    rows += [jnp.broadcast_to(any_later, rows[0].shape)] * 4
+    rows += [jnp.broadcast_to(any_later, (1, places))] * 4
     return jnp.concatenate(rows, axis=0).astype(jnp.int32)
 
 
@@ -234,17 +238,24 @@
 
 
 def weight_kernel(
-    arrived_ref, feat, mate, grad, core_ref, own_ref, other_ref, plan_ref, turned, acc, part, plan, plan_sem
+    arrived_ref, feat_any, mate_any, grad_any, core_ref, own_ref, other_ref, plan_ref,
+    feat, mate, grad, turned, acc, part, plan, plan_sem, sems,
 ):
     kinds, width, _ = acc.shape
     blocks, block, _ = feat.shape
     half = width // 2
+    pairs = ((feat_any, feat), (mate_any, mate), (grad_any, grad))
+    copies = [pltpu.make_async_copy(src, dst, sems.at[i]) for i, (src, dst) in enumerate(pairs)]
+    for copy in copies:
+        copy.start()
     tags = jnp.max(arrived_ref[:, pl.ds(3 * block, TAG_ROWS)].astype(jnp.float32), axis=1)
     plan_ref[...] = make_plans(tags, core_ref[0].astype(jnp.float32), blocks, kinds - 1)
     plan_copy = pltpu.make_async_copy(plan_ref, plan, plan_sem)
     plan_copy.start()
     acc[...] = jnp.zeros_like(acc)
     part[...] = jnp.zeros_like(part)
+    for copy in copies:
+        copy.wait()
     turn_blocks(feat, mate, turned)
 
     def root(g, carry):
@@ -303,61 +314,79 @@
     walk_groups(plan[11, 0], use)
 
 
-def feat_kernel(
-    plan_ref, core_ref, arrived_ref, later_any, grad_ref, root_ref, weight_ref, own_any, mate_ref,
-    held, halves, later, acc, sems, later_sem,
-):
+def add_groups(plan_ref, row, acc, block, products):
+    def use(g):
+        part = products(g)
+        for k in range(GROUP):
+            acc[plan_ref[row + 1, g * GROUP + k]] += part[k * block : (k + 1) * block]
+
+    walk_groups(plan_ref[row + 3, 0], use)
+
+
+ACROSS = (((1,), (1,)), ((), ()))
+
+
+def halves_kernel(plan_ref, core_ref, arrived_ref, later_any, weight_ref, own_any, mate_ref, halves, acc, sem, later_sem):
     blocks, block, width = mate_ref.shape
     half = width // 2
-    whole_copy = pltpu.make_async_copy(arrived_ref.at[:, pl.ds(0, 2 * block)], held, sems.at[0])
-    half_copy = pltpu.make_async_copy(arrived_ref.at[:, pl.ds(2 * block, block)], halves, sems.at[1])
-    whole_copy.start()
-    half_copy.start()
-    acc[pl.ds(blocks, blocks + 1)] = jnp.zeros((blocks + 1, block, width), jnp.float32)
-    across = (((1,), (1,)), ((), ()))
-
-    def base(g, carry):
-        rows = grad_ref[pl.ds(g * GROUP, GROUP)].reshape(GROUP * block, width)
-        part = lax.dot_general(rows, root_ref[...], across, preferred_element_type=jnp.float32)
-        acc[pl.ds(g * GROUP, GROUP)] = part.reshape(GROUP, block, width)
-        return carry
-
-    lax.fori_loop(0, blocks // GROUP, base, 0)
-    whole_copy.wait()
-
-    def add(g, row, part):
-        for k in range(GROUP):
-            acc[plan_ref[row + 1, g * GROUP + k]] += part[k * block : (k + 1) * block]
-
-    def use(g):
-        rows = jnp.concatenate([whole(held, plan_ref[0, g * GROUP + k], block) for k in range(GROUP)], axis=0)
-        add(g, 0, lax.dot_general(rows, weight_ref[plan_ref[2, g * GROUP]], across, preferred_element_type=jnp.float32))
-
-    def from_half(ref, row):
-        lanes = pl.ds(pl.multiple_of(core_ref[0] * half, half), half)
-
-        def use_half(g):
-            rows = jnp.concatenate([ref[plan_ref[row, g * GROUP + k]] for k in range(GROUP)], axis=0)
+    copy = pltpu.make_async_copy(arrived_ref.at[:, pl.ds(2 * block, block)], halves, sem)
+    copy.start()
+    acc[...] = jnp.zeros_like(acc)
+    lanes = pl.ds(pl.multiple_of(core_ref[0] * half, half), half)
+
+    def products(row):
+        def of_group(g):
+            rows = jnp.concatenate([halves[plan_ref[row, g * GROUP + k]] for k in range(GROUP)], axis=0)
             weight = weight_ref[plan_ref[row + 2, g * GROUP], :, lanes]
-            add(g, row, lax.dot_general(rows, weight, across, preferred_element_type=jnp.float32))
-
-        return use_half
-
-    walk_groups(plan_ref[3, 0], use)
-    half_copy.wait()
-    walk_groups(plan_ref[7, 0], from_half(halves, 4))
+            return lax.dot_general(rows, weight, ACROSS, preferred_element_type=jnp.float32)
+
+        return of_group
+
+    copy.wait()
+    add_groups(plan_ref, 4, acc, block, products(4))
 
     @pl.when(plan_ref[11, 0] > 0)
     def _():
-        copy = pltpu.make_async_copy(later_any, later, later_sem)
-        copy.start()
-        copy.wait()
-        walk_groups(plan_ref[11, 0], from_half(later, 8))
+        more = pltpu.make_async_copy(later_any, halves, later_sem)
+        more.start()
+        more.wait()
+        add_groups(plan_ref, 8, acc, block, products(8))
 
     own_copy = pltpu.make_async_copy(acc.at[pl.ds(0, blocks)], own_any, later_sem)
     own_copy.start()
     mate_ref[...] = acc[pl.ds(blocks, blocks)].astype(jnp.bfloat16)
     own_copy.wait()
+
+
+def feat_kernel(
+    plan_ref, arrived_ref, own_any, mate_any, grad_ref, root_ref, weight_ref, out_ref, held, mate, acc, sems
+):
+    blocks, block, width = out_ref.shape
+    own_copy = pltpu.make_async_copy(own_any, acc.at[pl.ds(0, blocks)], sems.at[0])
+    copy = pltpu.make_async_copy(arrived_ref.at[:, pl.ds(0, 2 * block)], held, sems.at[1])
+    mate_copy = pltpu.make_async_copy(mate_any, mate, sems.at[2])
+    own_copy.start()
+    copy.start()
+    mate_copy.start()
+    acc[2 * blocks] = jnp.zeros(acc.shape[1:], jnp.float32)
+    own_copy.wait()
+
+    def base(g, carry):
+        rows = grad_ref[pl.ds(g * GROUP, GROUP)].reshape(GROUP * block, width)
+        part = lax.dot_general(rows, root_ref[...], ACROSS, preferred_element_type=jnp.float32)
+        acc[pl.ds(g * GROUP, GROUP)] += part.reshape(GROUP, block, width)
+        return carry
+
+    lax.fori_loop(0, blocks // GROUP, base, 0)
+    copy.wait()
+
+    def products(g):
+        rows = jnp.concatenate([whole(held, plan_ref[0, g * GROUP + k], block) for k in range(GROUP)], axis=0)
+        return lax.dot_general(rows, weight_ref[plan_ref[2, g * GROUP]], ACROSS, preferred_element_type=jnp.float32)
+
+    add_groups(plan_ref, 0, acc, block, products)
+    mate_copy.wait()
+    out_ref[...] = (acc[pl.ds(0, blocks)] + mate[...].astype(jnp.float32)).astype(jnp.bfloat16)
 
 
 def share_kernel(scale, spread_ref, share_ref):
@@ -396,23 +425,30 @@
     )
     half_rows = (1 + rel_count) * width
     half = jax.ShapeDtypeStruct((half_rows, width // 2), jnp.float32)
+    local = pltpu.VMEM(grad_blocks.shape, jnp.bfloat16)
     turned = pltpu.VMEM((2 * blocks + 1, width, block), jnp.bfloat16)
     plan_type = jax.ShapeDtypeStruct((16, plan_places(dev_count, rel_count)), jnp.int32)
     own, other, plan = pl.pallas_call(
         weight_kernel,
         out_shape=(half, half, plan_type),
-        in_specs=[VMEM, VMEM, VMEM, VMEM, SMEM],
+        in_specs=[VMEM, HBM, HBM, HBM, SMEM],
         out_specs=(VMEM, VMEM, VMEM),
         scratch_shapes=[
+            local,
+            local,
+            local,
             turned,
             pltpu.VMEM((1 + rel_count, width, width), jnp.float32),
             pltpu.VMEM((rel_count, width, width // 2), jnp.float32),
             pltpu.SMEM(plan_type.shape, jnp.int32),
             dma,
+            dma((3,)),
         ],
-        compiler_params=pltpu.CompilerParams(vmem_limit_bytes=20 * MIB),
+        compiler_params=pltpu.CompilerParams(vmem_limit_bytes=24 * MIB),
         cost_estimate=cost,
     )(arrived, feat_blocks, mate_blocks, grad_blocks, core)
+
+    own = own + lax.ppermute(other, "c", swap)
 
     def take_later(later, own):
         later = exchange(later)
@@ -428,30 +464,28 @@
 
     later, own = lax.cond(plan[12, 0] > 0, take_later, lambda later, own: (later, own), later, own)
 
-    own = own + lax.ppermute(other, "c", swap)
     own, plan = lax.optimization_barrier((own, plan))
-    own_feat, mate_feat = pl.pallas_call(
-        feat_kernel,
+    own_part, mate_part = pl.pallas_call(
+        halves_kernel,
         out_shape=(
             jax.ShapeDtypeStruct(grad_blocks.shape, jnp.float32),
             jax.ShapeDtypeStruct(grad_blocks.shape, jnp.bfloat16),
         ),
-        in_specs=[SMEM, SMEM, HBM, HBM, VMEM, VMEM, VMEM],
+        in_specs=[SMEM, SMEM, HBM, HBM, VMEM],
         out_specs=(HBM, VMEM),
         scratch_shapes=[
-            pltpu.VMEM((dev_count, 2 * block, LANES), jnp.bfloat16),
-            pltpu.VMEM((dev_count, block, LANES), jnp.bfloat16),
             pltpu.VMEM((dev_count, block, LANES), jnp.bfloat16),
             pltpu.VMEM((2 * blocks + 1, block, width), jnp.float32),
-            dma((2,)),
+            dma,
             dma,
         ],
         compiler_params=pltpu.CompilerParams(vmem_limit_bytes=49 * MIB),
         cost_estimate=cost,
-    )(plan, core, arrived, later, grad_blocks, root_weight, rel_weight)
+    )(plan, core, arrived, later, rel_weight)
     shape = (chips, half_rows // chips, width // 2)
     spread = lax.all_to_all(own.reshape(shape), CHIPS, 0, 0, tiled=True)
-    spread, own_feat, mate_feat = lax.optimization_barrier((spread, own_feat, mate_feat))
+    spread, own_part, mate_part, plan = lax.optimization_barrier((spread, own_part, mate_part, plan))
+    mate_part = lax.ppermute(mate_part, "c", swap)
     share = pl.pallas_call(
         functools.partial(share_kernel, scale),
         out_shape=jax.ShapeDtypeStruct(shape, jnp.bfloat16),
@@ -460,7 +494,20 @@
         compiler_params=pltpu.CompilerParams(vmem_limit_bytes=8 * MIB),
     )(spread)
     own = lax.all_to_all(share, CHIPS, 0, 0, tiled=True).reshape(half.shape)
-    grad_feat = (own_feat + lax.ppermute(mate_feat, "c", swap).astype(jnp.float32)).astype(jnp.bfloat16)
+    grad_feat = pl.pallas_call(
+        feat_kernel,
+        out_shape=jax.ShapeDtypeStruct(grad_blocks.shape, jnp.bfloat16),
+        in_specs=[SMEM, HBM, HBM, HBM, VMEM, VMEM, VMEM],
+        out_specs=VMEM,
+        scratch_shapes=[
+            pltpu.VMEM((dev_count, 2 * block, LANES), jnp.bfloat16),
+            local,
+            pltpu.VMEM((2 * blocks + 1, block, width), jnp.float32),
+            dma((3,)),
+        ],
+        compiler_params=pltpu.CompilerParams(vmem_limit_bytes=49 * MIB),
+        cost_estimate=cost,
+    )(plan, arrived, own_part, mate_part, grad_blocks, root_weight, rel_weight)
     own, grad_feat = lax.optimization_barrier((own, grad_feat))
     other = lax.ppermute(own, "c", swap)
     core = core[0]

time: 247 us -> 313 us (1.27)
  waiting for transfers between devices: 9.6 us -> 61.9 us
  starting transfers between devices: 19 us -> 33 us
  local copies, waits for them, and re-layouts: 2.81 us -> 9.33 us
  other arithmetic: 7.96 us -> 2.39 us
  Pallas kernels: 47.1 us -> 43.7 us
    all_to_all x0 -> x1, waiting for transfers between devices: none -> 51.5 us  [exchange(): return lax.all_to_all(array, AXES, split_axis=0, concat_axis=0, tiled=True)]
    all_to_all x0 -> x1, starting transfers between devices: none -> 9.03 us  [exchange(): return lax.all_to_all(array, AXES, split_axis=0, concat_axis=0, tiled=True)]
    pallas_call x1, Pallas kernels: 20.5 us -> 11.9 us  [shards(): pl.pallas_call(weight_kernel, out_shape=(half, half, plan_type), in_specs...]
    all_to_all x1, waiting for transfers between devices: 0.01 us -> 8.25 us  [shards(): spread = lax.all_to_all(own.reshape(shape), CHIPS, 0, 0, tiled=True)]
    all_to_all x1, waiting for transfers between devices: 7.26 us -> 0.01 us  [shards(): own = lax.all_to_all(share, CHIPS, 0, 0, tiled=True).reshape(half.shape)]
    pallas_call x1 -> x3, Pallas kernels: 16.5 us -> 22.4 us  [the longest x1 11.5 us: shards(): pl.pallas_call(feat_kernel, out_shape=jax.ShapeDtypeStruct(grad_blocks.sh...]
    cond x0 -> x2, local copies, waits for them, and re-layouts: none -> 5.85 us
    convert_element_type x1 -> x0, other arithmetic: 4.2 us -> none  [shards(): (own_feat + lax.ppermute(mate_feat, 'c', swap).astype(jnp.float32)).astyp...]
  transfers between devices with their start and end apart: 6 -> 7, of which waited for: 3 -> 4; matrix products, arithmetic and copies ran while one was open for 2% -> 1% of each run, Pallas kernels for 11% -> 8%
where the time goes in v12:
time: 313 us; the launch traced here: 310 us
  blocking collectives  159 us (51%)
  waiting for transfers between devices  61.9 us (20%)
  Pallas kernels  43.7 us (14%)
  starting transfers between devices  33 us (11%)
  local copies, waits for them, and re-layouts  9.33 us (3%)
    all_to_all x1, blocking collectives, exchange(): return lax.all_to_all(array, AXES, split_axis=0, concat_axis=0, tiled=True)  159 us
    all_to_all x1, waiting for transfers between devices, exchange(): return lax.all_to_all(array, AXES, split_axis=0, concat_axis=0, tiled=True)  51.5 us
    pallas_call x1, Pallas kernels, shards(): pl.pallas_call(weight_kernel, out_shape=(half, half, plan_type), in_specs...  11.9 us
    pallas_call x1, Pallas kernels, shards(): pl.pallas_call(feat_kernel, out_shape=jax.ShapeDtypeStruct(grad_blocks.sh...  11.5 us
    all_to_all x1, starting transfers between devices, shards(): own = lax.all_to_all(share, CHIPS, 0, 0, tiled=True).reshape(half.shape)  10.6 us
    pallas_call x1, Pallas kernels, make_messages(): pl.pallas_call(kernel, out_shape=(jax.ShapeDtypeStruct((dev_count, 3 * bl...  9.23 us
    all_to_all x1, starting transfers between devices, exchange(): return lax.all_to_all(array, AXES, split_axis=0, concat_axis=0, tiled=True)  9.03 us
    all_to_all x1, waiting for transfers between devices, shards(): spread = lax.all_to_all(own.reshape(shape), CHIPS, 0, 0, tiled=True)  8.25 us
  transfers between devices with their start and end apart: 7, of which 4 were waited for; matrix products, arithmetic and copies ran while one was open for 1% of the time, Pallas kernels for 8%

profile of v12, /device:TPU:1, one launch (start us, length us, event | category | flops | bytes accessed | tf_op | source)
XLA Modules:
  0.0 310.5 jit_solution(12321498705737013109)
XLA Ops:
  0.6 1.5 collective-permute-start
  2.1 9.2 %shard_map.104 = (bf16[128,400,128]{2,1,0:T(8,128)(2,1)}, bf16[128,128,128]{2,1,0:T(8,128)(2,1)}) custom-call(s32[128]{0:T(128)} %refs_0_.1, s32[128]{0:T(128)} %bitcast.18, s32[128]{0:T(128)} %refs_2_.1, s32[128]{0:T(128)} %refs_3_.1, bf16[128,128,128]{2,1,0:T(8,128)(2,1)} %refs_4_.1, bf16[32,128,256]{2,1,0:T(8,128)(2,1)} %bitcast.11), custom_call_target="tpu_custom_call" | custom-call | flops 1073741824 | bytes 12582912 | tf_op jit(solution)/shard_map/pallas_call | solution.py:125
  11.4 0.0 collective-permute-done.mate_any
  11.4 0.0 copy-start.1
  11.4 158.8 %all_to_all.19.arrived_ref = bf16[128,400,128]{2,1,0:T(8,128)(2,1)S(1)} all-to-all(bf16[128,400,128]{2,1,0:T(8,128)(2,1)} %get-tuple-element.44), channel_id=1, replica_groups=mesh['z'=4,'y'=4,'x'=4,'c'=2] {'z','y','x','c'}, dimensions={0} | all-to-all | bytes 26214400 | tf_op jit(solution)/shard_map/all_to_all | solution.py:418
  170.1 0.0 copy-done.1
  170.2 0.0 copy-start
  170.2 11.9 %shard_map.105 = (f32[1536,128]{1,0:T(8,128)S(1)}, f32[1536,128]{1,0:T(8,128)S(1)}, s32[16,256]{1,0:T(8,128)S(1)}) custom-call(bf16[128,400,128]{2,1,0:T(8,128)(2,1)S(1)} %all_to_all.19.arrived_ref, bf16[32,128,256]{2,1,0:T(8,128)(2,1)} %bitcast.3.feat_any, bf16[32,128,256]{2,1,0:T(8,128)(2,1)} %collective-permute-done.mate_any, ...), custom_call_target="tpu_custom_call" | custom-call | flops 2147483648 | bytes 12582912 | tf_op jit(solution)/shard_map/pallas_call | solution.py:431
  182.1 0.0 copy-done
  182.1 1.1 collective-permute-start.1
  183.2 0.5 slice.3
  184.3 0.7 collective-permute-done.1
  185.1 1.0 add.3
  186.1 0.0 copy-start.2
  186.1 72.3 %conditional.1 = ((bf16[128,128,128]{2,1,0:T(8,128)(2,1)}, f32[1536,128]{1,0:T(8,128)})) conditional(s32[]{:T(128)} %bitcast.4, (bf16[128,128,128]{2,1,0:T(8,128)(2,1)}, f32[1536,128]{1,0:T(8,128)}) %tuple.20, (bf16[128,128,128]{2,1,0:T(8,128)(2,1)}, s32[16,256]{1,0:T(8,128)S(1)}, bf16[32,128,256]{2,1,0:T(8,128)(2,1)}, ...), branch_computations={%region_0.0_spmd, %region_1.0_spmd} | conditional | bytes 22544440 | solution.py:465
  186.1 9.0 %all-to-all-start = ((bf16[128,128,128]{2,1,0:T(8,128)(2,1)}), bf16[128,128,128]{2,1,0:T(8,128)(2,1)}, u32[]{:S(2)}, u32[]{:S(2)}) async-start(bf16[128,128,128]{2,1,0:T(8,128)(2,1)} %get-tuple-element.14), calls=%async_computation | async-start | bytes 8388608 | tf_op jit(solution)/shard_map/cond/branch_1_fun/all_to_all | solution.py:418
  195.1 1.1 copy.16.before_ref
  196.2 51.5 %all-to-all-done.later = bf16[128,128,128]{2,1,0:T(8,128)(2,1)} async-done(((bf16[128,128,128]{2,1,0:T(8,128)(2,1)}), bf16[128,128,128]{2,1,0:T(8,128)(2,1)}, u32[]{:S(2)}, u32[]{:S(2)}) %all-to-all-start) | async-done | bytes 4194336 | tf_op jit(solution)/shard_map/cond/branch_1_fun/all_to_all | solution.py:418
  247.7 4.7 %copy.13 = bf16[128,128,128]{2,1,0:T(8,128)(2,1)} copy(bf16[128,128,128]{2,1,0:T(8,128)(2,1)} %all-to-all-done.later) | data formatting | bytes 8388608 | tf_op jit(solution)/shard_map/cond
  252.4 5.9 %branch_1_fun.1 = f32[1536,128]{1,0:T(8,128)} custom-call(s32[16,256]{1,0:T(8,128)S(1)} %get-tuple-element.15.plan, bf16[128,128,128]{2,1,0:T(8,128)(2,1)} %all-to-all-done.later, bf16[32,128,256]{2,1,0:T(8,128)(2,1)} %get-tuple-element.16.feat, bf16[32,128,256]{2,1,0:T(8,128)(2,1)} %get-tuple-element.17.mate, f32[1536,128]{1,0:T(8,128)S(1)} %copy.16.before_ref), custom_call_target="tpu_custom_call" | custom-call | tf_op jit(solution)/shard_map/cond/branch_1_fun/pallas_call | solution.py:455
  258.3 8.0 %all-to-all-start.2 = ((f32[64,24,128]{2,1,0:T(8,128)}), f32[64,24,128]{2,1,0:T(8,128)S(1)}, u32[]{:S(2)}, u32[]{:S(2)}) async-start(f32[64,24,128]{2,1,0:T(8,128)} %bitcast.5), calls=%async_computation.2 | async-start | bytes 1572864 | tf_op jit(solution)/shard_map/all_to_all | solution.py:486
  266.3 0.0 copy-done.2
  266.3 5.0 %shard_map.106 = (f32[32,128,256]{2,1,0:T(8,128)}, bf16[32,128,256]{2,1,0:T(8,128)(2,1)S(1)}) custom-call(s32[16,256]{1,0:T(8,128)S(1)} %get-tuple-element.58.plan_ref, s32[1]{0:T(128)} %bitcast.2.core_ref, bf16[128,400,128]{2,1,0:T(8,128)(2,1)} %copy-done, bf16[128,128,128]{2,1,0:T(8,128)(2,1)} %get-tuple-element.54.later_any, ...), custom_call_target="tpu_custom_call" | custom-call | flops 2147483648 | bytes 12582912 | tf_op jit(solution)/shard_map/pallas_call | solution.py:468
  271.3 0.0 copy-start.5
  271.3 1.3 copy-done.5
  272.7 8.3 %all-to-all-done.2.spread_ref = f32[64,24,128]{2,1,0:T(8,128)S(1)} async-done(((f32[64,24,128]{2,1,0:T(8,128)}), f32[64,24,128]{2,1,0:T(8,128)S(1)}, u32[]{:S(2)}, u32[]{:S(2)}) %all-to-all-start.2) | async-done | bytes 786464 | tf_op jit(solution)/shard_map/all_to_all | solution.py:486
  280.9 2.3 collective-permute-start.2
  283.2 0.1 shard_map.107
  283.3 0.0 copy-start.3
  283.3 0.7 copy-done.3
  284.1 10.6 %all-to-all-start.3 = ((bf16[64,24,128]{2,1,0:T(8,128)(2,1)}), bf16[64,24,128]{2,1,0:T(8,128)(2,1)S(1)}, u32[]{:S(2)}, u32[]{:S(2)}) async-start(bf16[64,24,128]{2,1,0:T(8,128)(2,1)} %copy-done.3), calls=%async_computation.3 | async-start | bytes 786432 | tf_op jit(solution)/shard_map/all_to_all | solution.py:496
  294.6 0.0 collective-permute-done.2.mate_any
  294.6 0.0 copy-start.4
  294.7 0.9 copy-done.4
  295.6 11.5 %shard_map.108 = bf16[32,128,256]{2,1,0:T(8,128)(2,1)} custom-call(s32[16,256]{1,0:T(8,128)S(1)} %get-tuple-element.58.plan_ref, bf16[128,400,128]{2,1,0:T(8,128)(2,1)} %copy-done, f32[32,128,256]{2,1,0:T(8,128)} %get-tuple-element.59.own_any, bf16[32,128,256]{2,1,0:T(8,128)(2,1)} %collective-permute-done.2.mate_any, bf16[32,128,256]{2,1,0:T(8,128)(2,1)S(1)} %bitcast.13, ...), custom_call_target="tpu_custom_call" | custom-call | flops 2147483648 | bytes 12582912 | tf_op jit(solution)/shard_map/pallas_call | solution.py:497
  307.1 0.0 all-to-all-done.3
  307.1 0.5 collective-permute-start.3
  307.7 1.3 collective-permute-done.3
  309.0 0.1 broadcast_select_fusion.1
  309.1 0.1 pad_maximum_fusion
  309.2 1.3 convert.3
Async XLA Ops:
  0.6 10.7 %collective-permute-start = (bf16[32,128,256]{2,1,0:T(8,128)(2,1)}, bf16[32,128,256]{2,1,0:T(8,128)(2,1)}, u32[]{:S(2)}, u32[]{:S(2)}) collective-permute-start(bf16[32,128,256]{2,1,0:T(8,128)(2,1)} %bitcast.3.feat_any), channel_id=1, source_target_pairs={{0,1},{1,0},{2,3},{3,2},{4,5},{5,4},{6,7},{7,6},{8,9},{9,8},{10,11... | collective-permute-start | bytes 6291464 | tf_op jit(solution)/shard_map/ppermute | solution.py:411
  11.4 158.8 %copy-start.1 = (bf16[4096,256]{1,0:T(8,128)(2,1)S(1)}, bf16[4096,256]{1,0:T(8,128)(2,1)}, u32[]{:S(2)}) copy-start(bf16[4096,256]{1,0:T(8,128)(2,1)} %param.12) | copy-start | bytes 6291460
  170.2 11.9 %copy-start = (bf16[128,400,128]{2,1,0:T(8,128)(2,1)}, bf16[128,400,128]{2,1,0:T(8,128)(2,1)S(1)}, u32[]{:S(2)}) copy-start(bf16[128,400,128]{2,1,0:T(8,128)(2,1)S(1)} %all_to_all.19.arrived_ref) | copy-start | bytes 39321604
  182.1 3.0 collective-permute-start.1
  186.1 80.3 %copy-start.2 = (bf16[5,256,256]{2,1,0:T(8,128)(2,1)S(1)}, bf16[5,256,256]{2,1,0:T(8,128)(2,1)}, u32[]{:S(2)}) copy-start(bf16[5,256,256]{2,1,0:T(8,128)(2,1)} %weight_ref.3) | copy-start | bytes 1966084
  186.1 61.7 %all-to-all-start = ((bf16[128,128,128]{2,1,0:T(8,128)(2,1)}), bf16[128,128,128]{2,1,0:T(8,128)(2,1)}, u32[]{:S(2)}, u32[]{:S(2)}) async-start(bf16[128,128,128]{2,1,0:T(8,128)(2,1)} %get-tuple-element.14), calls=%async_computation | async-start | bytes 8388608 | tf_op jit(solution)/shard_map/cond/branch_1_fun/all_to_all | solution.py:418
  258.3 22.6 %all-to-all-start.2 = ((f32[64,24,128]{2,1,0:T(8,128)}), f32[64,24,128]{2,1,0:T(8,128)S(1)}, u32[]{:S(2)}, u32[]{:S(2)}) async-start(f32[64,24,128]{2,1,0:T(8,128)} %bitcast.5), calls=%async_computation.2 | async-start | bytes 1572864 | tf_op jit(solution)/shard_map/all_to_all | solution.py:486
  271.3 1.3 copy-start.5
  280.9 13.7 %collective-permute-start.2 = (bf16[32,128,256]{2,1,0:T(8,128)(2,1)}, bf16[32,128,256]{2,1,0:T(8,128)(2,1)}, u32[]{:S(2)}, u32[]{:S(2)}) collective-permute-start(bf16[32,128,256]{2,1,0:T(8,128)(2,1)} %copy-done.5), channel_id=1, source_target_pairs={{0,1},{1,0},{2,3},{3,2},{4,5},{5,4},{6,7},{7,6},{8,9},{9,8},{10,11... | collective-permute-start | bytes 6291464 | tf_op jit(solution)/shard_map/ppermute | solution.py:488
  283.3 0.7 copy-start.3
  284.1 23.0 %all-to-all-start.3 = ((bf16[64,24,128]{2,1,0:T(8,128)(2,1)}), bf16[64,24,128]{2,1,0:T(8,128)(2,1)S(1)}, u32[]{:S(2)}, u32[]{:S(2)}) async-start(bf16[64,24,128]{2,1,0:T(8,128)(2,1)} %copy-done.3), calls=%async_computation.3 | async-start | bytes 786432 | tf_op jit(solution)/shard_map/all_to_all | solution.py:496
  294.6 0.9 copy-start.4
  307.1 1.9 collective-permute-start.3
